TPU v7x, 256 devices: a whole 4x4x8 slice. The times are simulated.
256 devices in a mesh: context: 16 (over x_lo, y, core), tensor: 16 (over z, x_hi).
Axes of the slice: x: 4 (x_hi: 2, x_lo: 2; x = x_hi * 2 + x_lo), y: 4, z: 8, core: 2. Of those that a mesh axis runs over, the one named last changes fastest.
Arguments:
- ids: int32 [16384], P('context'), may hold values from 0 to 4, as said below
- complement: int32 [5], replicated, may hold values from 0 to 4, as said below
- embedding: bfloat16 [5, 2048], replicated, may hold values from -6 to 6
- norm_gain: float32 [2048], replicated, may hold values from 0.5 to 1.5
- w_z: bfloat16 [2048, 4096], P(None, 'tensor'), may hold values from -0.125 to 0.125
- w_x: bfloat16 [2048, 4096], P(None, 'tensor'), may hold values from -0.125 to 0.125
- w_bc: bfloat16 [2048, 256], replicated, may hold values from -0.125 to 0.125
- w_dt: bfloat16 [2048, 64], P(None, 'tensor'), may hold values from -0.0625 to 0.0625
- dt_bias: float32 [64], P('tensor')
- a_log: float32 [64], P('tensor')
- conv_x: float32 [4, 4096], P(None, 'tensor'), may hold values from -3 to 3
- conv_bc: float32 [4, 256], replicated, may hold values from -3 to 3
- d_skip: float32 [64], P('tensor'), may hold values from 0.5 to 2
- gate_gain: float32 [4096], P('tensor'), may hold values from 0.5 to 1.5
- w_out: bfloat16 [4096, 2048], P('tensor'), may hold values from -0.09375 to 0.09375
Outputs:
- mixed: bfloat16 [16384, 2048], P('context', 'tensor')
Inputs may be any that keep to these rules, and one draw needn't show every extreme that they name: Token ids of the bases and 4 for an unknown base; 4 occurs somewhere in every draw. `complement`: an involution: it pairs the ids 0 to 3 two by two and maps 4 to itself.
All inputs are finite; a program needn't handle non-finite values.
Results may differ from a plain program's by a relative error of at most 0.025.
Values may be sent and summed in bfloat16 or wider, within the bound.
No kernel may reach another device: no remote copies, remote signals or barrier semaphores. Data moves between devices by JAX's collectives and lax.ppermute only.
A program may use at most 128 MiB of HBM per device.

v0:
```python
import jax
import jax.numpy as jnp
from jax import lax
from jax.sharding import PartitionSpec as P

BLOCK = 256


highest = lax.Precision.HIGHEST
epsilon = 1e-05


def with_halo(value, sides, width):
    for axis, dim in sides:
        count, length = (lax.axis_size(axis), value.shape[dim])
        up = [(i, (i + 1) % count) for i in range(count - 1)]
        down = [(j, i) for i, j in up]
        last = lax.slice_in_dim(value, length - width, length, axis=dim)
        initial = lax.slice_in_dim(value, 0, width, axis=dim)
        before = lax.ppermute(last, axis, up)
        after = lax.ppermute(initial, axis, down)
        value = jnp.concatenate([before, value, after], axis=dim)
    return value


def shifted(value, axis, by):
    count = lax.axis_size(axis)
    pairs = [(i, i + by) for i in range(count) if 0 <= i + by < count]
    return lax.ppermute(value, axis, pairs)


def local(
    ids,
    complement,
    embedding,
    norm_gain,
    w_z,
    w_x,
    w_bc,
    w_dt,
    dt_bias,
    a_log,
    conv_x,
    conv_bc,
    d_skip,
    gate_gain,
    w_out,
):
    length = ids.shape[0]
    inner_dev = w_z.shape[1]
    heads_dev = dt_bias.shape[0]
    head_dim = inner_dev // heads_dev
    state_dim = w_bc.shape[1] // 2
    rim_width = conv_x.shape[0] - 1
    blocks = length // BLOCK
    letters = jnp.arange(5, dtype=jnp.int32)
    matches = ids[:, None] == letters[None, :]
    reverse_ids = jnp.sum(jnp.where(matches, complement[None, :], 0), axis=1)[::-1]
    strand_ids = jnp.concatenate([ids, reverse_ids])
    one_hot = (strand_ids[:, None] == letters[None, :]).astype(jnp.bfloat16)
    embedded = jnp.dot(one_hot, embedding, preferred_element_type=jnp.float32)
    normed = (
        embedded
        * lax.rsqrt(jnp.mean(embedded * embedded, axis=-1, keepdims=True) + epsilon)
        * norm_gain
    ).astype(jnp.bfloat16)
    gate_in = (
        jnp.dot(normed, w_z, preferred_element_type=jnp.float32)
        .astype(jnp.bfloat16)
        .reshape(2, length, inner_dev)
    )
    xs_pre = jnp.dot(normed, w_x, preferred_element_type=jnp.float32).astype(jnp.bfloat16)
    bc_pre = jnp.dot(normed, w_bc, preferred_element_type=jnp.float32).astype(jnp.bfloat16)
    stride = jax.nn.softplus(
        jnp.dot(normed, w_dt, preferred_element_type=jnp.float32) + dt_bias
    ).reshape(2, blocks, BLOCK, heads_dev)
    projected = jnp.concatenate([xs_pre, bc_pre], axis=1).reshape(2, length, -1)
    edges = jnp.concatenate(
        [projected[1, length - rim_width :], projected[0, length - rim_width :]], axis=0
    )
    padded_edges = with_halo(edges, (("context", 0),), rim_width)
    forward_ext = jnp.concatenate([padded_edges[:rim_width], projected[0]], axis=0)
    reverse_ext = jnp.concatenate([padded_edges[3 * rim_width :], projected[1]], axis=0)
    extended = jnp.stack([forward_ext, reverse_ext]).astype(jnp.float32)
    kernel = jnp.concatenate([conv_x, conv_bc], axis=1)
    convolved = kernel[0] * extended[:, 0:length]
    for offset in range(1, rim_width + 1):
        convolved = convolved + kernel[offset] * extended[:, offset : offset + length]
    activated = jax.nn.silu(convolved)
    values = activated[..., :inner_dev].reshape(2, blocks, BLOCK, heads_dev, head_dim)
    b_in = activated[..., inner_dev : inner_dev + state_dim].reshape(2, blocks, BLOCK, state_dim)
    c_out = activated[..., inner_dev + state_dim :].reshape(2, blocks, BLOCK, state_dim)
    log_steps = stride * -jnp.exp(a_log)
    cumul = jnp.cumsum(log_steps, axis=2)
    lower = jnp.arange(BLOCK)[:, None] >= jnp.arange(BLOCK)[None, :]
    differ = cumul[:, :, :, None, :] - cumul[:, :, None, :, :]
    decays = jnp.exp(jnp.where(lower[None, None, :, :, None], differ, -jnp.inf))
    scores = jnp.einsum("gctn,gcsn->gcts", c_out, b_in, precision=highest)
    weights = decays * scores[..., None] * stride[:, :, None, :, :]
    inside = jnp.einsum("gctsh,gcshp->gcthp", weights, values, precision=highest)
    remain = jnp.exp(cumul[:, :, -1:, :] - cumul) * stride
    block_states = jnp.einsum(
        "gcshp,gcsn->gchpn", values * remain[..., None], b_in, precision=highest
    )
    block_decay = jnp.exp(cumul[:, :, -1, :])

    def advance(running, piece):
        factor, update = piece
        return (factor[:, :, None, None] * running + update, running)

    zero_states = jnp.zeros((2, heads_dev, head_dim, state_dim), jnp.float32)
    device_state, entering = lax.scan(
        advance, zero_states, (jnp.moveaxis(block_decay, 1, 0), jnp.moveaxis(block_states, 1, 0))
    )
    entering = jnp.moveaxis(entering, 0, 1)
    device_decay = jnp.exp(jnp.sum(log_steps, axis=(1, 2)))

    def relay(counter, carried):
        into_forward, into_reverse = carried
        into_forward = shifted(
            (device_decay[0][:, None, None] * into_forward + device_state[0]).astype(jnp.bfloat16),
            "context",
            1,
        ).astype(jnp.float32)
        into_reverse = shifted(
            (device_decay[1][:, None, None] * into_reverse + device_state[1]).astype(jnp.bfloat16),
            "context",
            -1,
        ).astype(jnp.float32)
        return (into_forward, into_reverse)

    arrive_forward, arrive_reverse = lax.fori_loop(
        0, lax.axis_size("context") - 1, relay, (zero_states[0], zero_states[1])
    )
    arriving = jnp.stack([arrive_forward, arrive_reverse])
    before = jnp.cumsum(cumul[:, :, -1, :], axis=1) - cumul[:, :, -1, :]
    entering = entering + jnp.exp(before)[..., None, None] * arriving[:, None]
    carried_out = (
        jnp.einsum("gctn,gchpn->gcthp", c_out, entering, precision=highest)
        * jnp.exp(cumul)[..., None]
    )
    scanned = inside + carried_out + d_skip[:, None] * values
    gated = scanned.reshape(2, length, inner_dev) * jax.nn.silu(gate_in.astype(jnp.float32))
    squares = lax.psum(jnp.sum(gated * gated, axis=-1), "tensor")
    inverse = lax.rsqrt(squares / (inner_dev * lax.axis_size("tensor")) + epsilon)
    normalized = (gated * inverse[..., None] * gate_gain).astype(jnp.bfloat16)
    strand_terms = jnp.dot(
        normalized.reshape(2 * length, inner_dev), w_out, preferred_element_type=jnp.float32
    ).reshape(2, length, -1)
    shares = lax.psum_scatter(
        strand_terms.astype(jnp.bfloat16), "tensor", scatter_dimension=2, tiled=True
    ).astype(jnp.float32)
    mixed = (shares[0] + shares[1][::-1]).astype(jnp.bfloat16)
    return mixed


def solution(mesh):
    placed = (
        P("context"),
        P(),
        P(),
        P(),
        P(None, "tensor"),
        P(None, "tensor"),
        P(),
        P(None, "tensor"),
        P("tensor"),
        P("tensor"),
        P(None, "tensor"),
        P(),
        P("tensor"),
        P("tensor"),
        P("tensor", None),
    )
    return jax.shard_map(
        local, mesh=mesh, in_specs=placed, out_specs=P("context", "tensor"), check_vma=False
    )
```

profile of v0, /device:TPU:2, one launch (start us, length us, event | category | flops | bytes accessed | tf_op | source)
XLA Modules:
  0.0 629.5 jit_solution(5327299440110310254)
XLA Ops:
  8.2 3.2 multiply_reduce_fusion
  27.4 5.9 collective-permute-start.3
  36.4 4.6 compare_select_fusion
  41.8 10.1 %reduce-window.6 = f32[2,4,4,2,128]{4,3,2,1,0:T(2,128)S(1)} reduce-window(f32[2,4,4,2,128]{4,3,2,1,0:T(2,128)S(1)} %reshape.104, f32[]{:T(128)} %constant.26.clone.1), window={size=1x1x1x1x128 pad=0_0x0_0x0_0x0_0x127_0}, to_apply=%region_2.3 | reduce-window | flops 1040384 | bytes 65540 | tf_op jit(solution)/shard_map/reduce-window
  54.0 6.1 fusion.17
  66.7 4.8 copy.167
  75.6 3.9 divide_multiply_fusion
  85.7 5.1 fusion.23
  90.8 7.1 %while.26 = (s32[]{:T(128)}, f32[2,4,64,128]{3,2,1,0:T(8,128)S(1)}, f32[4,2,4,64,128]{4,3,2,1,0:T(8,128)}, f32[4,2,4]{2,0,1:T(4,128)S(1)}, f32[4,2,4,64,128]{4,3,2,0,1:T(8,128)}, /*index=5*/s32[]{:T(128)}, s32[]{:T(128)}) while((s32[]{:T(128)}, f32[2,4,64,128]{3,2,1,0:T(8,128)S(1)}, f32[4,2,4,64,128]{4,3,2,1,0:T(8,128)}, ...), condition=%wide.region_5.6_spmd.clone, body=%wide.region_4.5_spmd.clone.sunk | while | flops 262147 | bytes 1311424 | solution.py:112
  99.4 195.4 %while.27 = (s32[]{:T(128)}, f32[4,64,128]{2,1,0:T(8,128)S(1)}, f32[4,64,128]{2,1,0:T(8,128)}, f32[2,4]{1,0:T(2,128)S(1)}, f32[2,4,64,128]{3,2,1,0:T(8,128)S(1)}, /*index=5*/s32[]{:T(128)}, s32[]{:T(128)}) while((s32[]{:T(128)}, f32[4,64,128]{2,1,0:T(8,128)S(1)}, f32[4,64,128]{2,1,0:T(8,128)}, f32[2,4]{1,0:T(2,128)S(1)}, ...), condition=%wide.region_9.10_spmd.clone, body=%wide.region_8.9_spmd.clone.sunk | while | flops 327683 | bytes 1573127 | solution.py:132
  102.1 5.8 collective-permute-start.1
  115.1 5.8 collective-permute-start.1
  128.2 5.8 collective-permute-start.1
  141.3 5.8 collective-permute-start.1
  154.4 5.8 collective-permute-start.1
  167.4 5.8 collective-permute-start.1
  180.5 5.8 collective-permute-start.1
  193.6 5.8 collective-permute-start.1
  206.7 5.8 collective-permute-start.1
  219.8 5.8 collective-permute-start.1
  232.8 5.8 collective-permute-start.1
  245.9 5.8 collective-permute-start.1
  259.0 5.8 collective-permute-start.1
  272.1 5.8 collective-permute-start.1
  285.2 5.8 collective-permute-start.1
  297.7 9.5 %fusion.2 = f32[2,4,4,64,256]{4,3,2,1,0:T(8,128)S(1)} fusion(f32[2,4,256,4]{2,3,1,0:T(4,128)S(1)} %bitcast.127, f32[2,4,256,256]{3,2,1,0:T(8,128)S(1)} %fusion.28, f32[2,4,256,4]{2,3,1,0:T(4,128)S(1)} %bitcast.129, pred[256,256]{1,0:T(8,128)(4,1)S(1)} %copy-done.14, f32[2,4,256,4,64]{2,1,4,3,0:T(4,128)S(1)} %copy-done.4), kind=kOutput, calls=%fused_computation.13 | convolution fusion | flops 1619001344 | bytes 6422528 | tf_op jit(solution)/shard_map/gctsh,gcshp->gcthp/dot_general | solution.py:100
  313.6 5.5 reshape.113
  319.1 44.5 %psum.7 = f32[2,1024]{1,0:T(2,128)S(1)} all-reduce(f32[2,1024]{1,0:T(2,128)S(1)} %bitcast.132), channel_id=1, replica_groups=mesh['context'=16,'tensor'=16] {'tensor'}, use_global_device_ids=true, to_apply=%region_11.12 | all-reduce | flops 2048 | bytes 16384 | tf_op jit(solution)/shard_map/psum | solution.py:144
  366.0 5.6 convolution_convert_fusion
  371.6 21.4 %copy.175 = bf16[2,1024,2048]{1,0,2:T(2,128)(2,1)} copy(bf16[2,1024,2048]{2,1,0:T(8,128)(2,1)} %convolution_convert_fusion) | data formatting | bytes 16777216
  393.0 10.1 %copy.189 = bf16[256,8,2,1024]{3,1,2,0:T(8,128)(2,1)} copy(bf16[256,8,2,1024]{3,2,1,0:T(2,128)(2,1)} %bitcast.115) | data formatting | bytes 16777216
  403.1 216.3 %reduce-scatter.4.cloned.1.call-done = bf16[128,2048]{1,0:T(8,128)(2,1)} async-done(((bf16[2048,2048]{1,0:T(8,128)(2,1)}), bf16[128,2048]{1,0:T(8,128)(2,1)}) %reduce-scatter.4.cloned.1.call-update) | async-done | bytes 524304
  (246 shorter events, 171.1 us)
Async XLA Ops:
  6.5 612.9 %reduce-scatter.4.cloned.1.call-start = ((), (), s32[]{:S(2)}) async-start(), calls=%async_computation.1 | async-start | bytes 8912896
  24.6 46.8 %collective-permute-start.2 = (bf16[3,512]{0,1:T(8,128)(2,1)}, bf16[3,512]{0,1:T(8,128)(2,1)}, u32[]{:S(2)}, u32[]{:S(2)}) collective-permute-start(bf16[3,512]{0,1:T(8,128)(2,1)} %bitcast.2), channel_id=1, source_target_pairs={{0,16},{16,32},{32,48},{48,64},{64,80},{80,96},{96,112},{112,128},... | collective-permute-start | bytes 9224 | tf_op jit(solution)/shard_map/ppermute | solution.py:20
  27.4 46.0 %collective-permute-start.3 = (bf16[3,512]{0,1:T(8,128)(2,1)}, bf16[3,512]{0,1:T(8,128)(2,1)}, u32[]{:S(2)}, u32[]{:S(2)}) collective-permute-start(bf16[3,512]{0,1:T(8,128)(2,1)} %bitcast.4), channel_id=1, source_target_pairs={{16,0},{32,16},{48,32},{64,48},{80,64},{96,80},{112,96},{128,112},... | collective-permute-start | bytes 9224 | tf_op jit(solution)/shard_map/ppermute | solution.py:21
  100.2 8.0 %collective-permute-start = (bf16[4,64,128]{2,1,0:T(8,128)(2,1)}, bf16[4,64,128]{2,1,0:T(8,128)(2,1)}, u32[]{:S(2)}, u32[]{:S(2)}) collective-permute-start(bf16[4,64,128]{2,1,0:T(8,128)(2,1)} %get-tuple-element.263), channel_id=1, source_target_pairs={{0,16},{16,32},{32,48},{48,64},{64,80},{80,96},{96,112},{112,128},... | collective-permute-start | bytes 196616 | tf_op jit(solution)/shard_map/while/body/eval_jaxpr/ppermute | solution.py:29
  113.2 8.1 %collective-permute-start = (bf16[4,64,128]{2,1,0:T(8,128)(2,1)}, bf16[4,64,128]{2,1,0:T(8,128)(2,1)}, u32[]{:S(2)}, u32[]{:S(2)}) collective-permute-start(bf16[4,64,128]{2,1,0:T(8,128)(2,1)} %get-tuple-element.263), channel_id=1, source_target_pairs={{0,16},{16,32},{32,48},{48,64},{64,80},{80,96},{96,112},{112,128},... | collective-permute-start | bytes 196616 | tf_op jit(solution)/shard_map/while/body/eval_jaxpr/ppermute | solution.py:29
  115.1 8.0 %collective-permute-start.1 = (bf16[4,64,128]{2,1,0:T(8,128)(2,1)}, bf16[4,64,128]{2,1,0:T(8,128)(2,1)}, u32[]{:S(2)}, u32[]{:S(2)}) collective-permute-start(bf16[4,64,128]{2,1,0:T(8,128)(2,1)} %get-tuple-element.264), channel_id=1, source_target_pairs={{16,0},{32,16},{48,32},{64,48},{80,64},{96,80},{112,96},{128,112},... | collective-permute-start | bytes 196616 | tf_op jit(solution)/shard_map/while/body/eval_jaxpr/ppermute | solution.py:29
  126.3 8.1 %collective-permute-start = (bf16[4,64,128]{2,1,0:T(8,128)(2,1)}, bf16[4,64,128]{2,1,0:T(8,128)(2,1)}, u32[]{:S(2)}, u32[]{:S(2)}) collective-permute-start(bf16[4,64,128]{2,1,0:T(8,128)(2,1)} %get-tuple-element.263), channel_id=1, source_target_pairs={{0,16},{16,32},{32,48},{48,64},{64,80},{80,96},{96,112},{112,128},... | collective-permute-start | bytes 196616 | tf_op jit(solution)/shard_map/while/body/eval_jaxpr/ppermute | solution.py:29
  128.2 8.0 %collective-permute-start.1 = (bf16[4,64,128]{2,1,0:T(8,128)(2,1)}, bf16[4,64,128]{2,1,0:T(8,128)(2,1)}, u32[]{:S(2)}, u32[]{:S(2)}) collective-permute-start(bf16[4,64,128]{2,1,0:T(8,128)(2,1)} %get-tuple-element.264), channel_id=1, source_target_pairs={{16,0},{32,16},{48,32},{64,48},{80,64},{96,80},{112,96},{128,112},... | collective-permute-start | bytes 196616 | tf_op jit(solution)/shard_map/while/body/eval_jaxpr/ppermute | solution.py:29
  139.4 8.1 %collective-permute-start = (bf16[4,64,128]{2,1,0:T(8,128)(2,1)}, bf16[4,64,128]{2,1,0:T(8,128)(2,1)}, u32[]{:S(2)}, u32[]{:S(2)}) collective-permute-start(bf16[4,64,128]{2,1,0:T(8,128)(2,1)} %get-tuple-element.263), channel_id=1, source_target_pairs={{0,16},{16,32},{32,48},{48,64},{64,80},{80,96},{96,112},{112,128},... | collective-permute-start | bytes 196616 | tf_op jit(solution)/shard_map/while/body/eval_jaxpr/ppermute | solution.py:29
  141.3 8.0 %collective-permute-start.1 = (bf16[4,64,128]{2,1,0:T(8,128)(2,1)}, bf16[4,64,128]{2,1,0:T(8,128)(2,1)}, u32[]{:S(2)}, u32[]{:S(2)}) collective-permute-start(bf16[4,64,128]{2,1,0:T(8,128)(2,1)} %get-tuple-element.264), channel_id=1, source_target_pairs={{16,0},{32,16},{48,32},{64,48},{80,64},{96,80},{112,96},{128,112},... | collective-permute-start | bytes 196616 | tf_op jit(solution)/shard_map/while/body/eval_jaxpr/ppermute | solution.py:29
  152.4 8.1 %collective-permute-start = (bf16[4,64,128]{2,1,0:T(8,128)(2,1)}, bf16[4,64,128]{2,1,0:T(8,128)(2,1)}, u32[]{:S(2)}, u32[]{:S(2)}) collective-permute-start(bf16[4,64,128]{2,1,0:T(8,128)(2,1)} %get-tuple-element.263), channel_id=1, source_target_pairs={{0,16},{16,32},{32,48},{48,64},{64,80},{80,96},{96,112},{112,128},... | collective-permute-start | bytes 196616 | tf_op jit(solution)/shard_map/while/body/eval_jaxpr/ppermute | solution.py:29
  154.4 8.0 %collective-permute-start.1 = (bf16[4,64,128]{2,1,0:T(8,128)(2,1)}, bf16[4,64,128]{2,1,0:T(8,128)(2,1)}, u32[]{:S(2)}, u32[]{:S(2)}) collective-permute-start(bf16[4,64,128]{2,1,0:T(8,128)(2,1)} %get-tuple-element.264), channel_id=1, source_target_pairs={{16,0},{32,16},{48,32},{64,48},{80,64},{96,80},{112,96},{128,112},... | collective-permute-start | bytes 196616 | tf_op jit(solution)/shard_map/while/body/eval_jaxpr/ppermute | solution.py:29
  165.5 8.1 %collective-permute-start = (bf16[4,64,128]{2,1,0:T(8,128)(2,1)}, bf16[4,64,128]{2,1,0:T(8,128)(2,1)}, u32[]{:S(2)}, u32[]{:S(2)}) collective-permute-start(bf16[4,64,128]{2,1,0:T(8,128)(2,1)} %get-tuple-element.263), channel_id=1, source_target_pairs={{0,16},{16,32},{32,48},{48,64},{64,80},{80,96},{96,112},{112,128},... | collective-permute-start | bytes 196616 | tf_op jit(solution)/shard_map/while/body/eval_jaxpr/ppermute | solution.py:29
  167.4 8.0 %collective-permute-start.1 = (bf16[4,64,128]{2,1,0:T(8,128)(2,1)}, bf16[4,64,128]{2,1,0:T(8,128)(2,1)}, u32[]{:S(2)}, u32[]{:S(2)}) collective-permute-start(bf16[4,64,128]{2,1,0:T(8,128)(2,1)} %get-tuple-element.264), channel_id=1, source_target_pairs={{16,0},{32,16},{48,32},{64,48},{80,64},{96,80},{112,96},{128,112},... | collective-permute-start | bytes 196616 | tf_op jit(solution)/shard_map/while/body/eval_jaxpr/ppermute | solution.py:29
  178.6 8.1 %collective-permute-start = (bf16[4,64,128]{2,1,0:T(8,128)(2,1)}, bf16[4,64,128]{2,1,0:T(8,128)(2,1)}, u32[]{:S(2)}, u32[]{:S(2)}) collective-permute-start(bf16[4,64,128]{2,1,0:T(8,128)(2,1)} %get-tuple-element.263), channel_id=1, source_target_pairs={{0,16},{16,32},{32,48},{48,64},{64,80},{80,96},{96,112},{112,128},... | collective-permute-start | bytes 196616 | tf_op jit(solution)/shard_map/while/body/eval_jaxpr/ppermute | solution.py:29
  180.5 8.0 %collective-permute-start.1 = (bf16[4,64,128]{2,1,0:T(8,128)(2,1)}, bf16[4,64,128]{2,1,0:T(8,128)(2,1)}, u32[]{:S(2)}, u32[]{:S(2)}) collective-permute-start(bf16[4,64,128]{2,1,0:T(8,128)(2,1)} %get-tuple-element.264), channel_id=1, source_target_pairs={{16,0},{32,16},{48,32},{64,48},{80,64},{96,80},{112,96},{128,112},... | collective-permute-start | bytes 196616 | tf_op jit(solution)/shard_map/while/body/eval_jaxpr/ppermute | solution.py:29
  191.7 8.1 %collective-permute-start = (bf16[4,64,128]{2,1,0:T(8,128)(2,1)}, bf16[4,64,128]{2,1,0:T(8,128)(2,1)}, u32[]{:S(2)}, u32[]{:S(2)}) collective-permute-start(bf16[4,64,128]{2,1,0:T(8,128)(2,1)} %get-tuple-element.263), channel_id=1, source_target_pairs={{0,16},{16,32},{32,48},{48,64},{64,80},{80,96},{96,112},{112,128},... | collective-permute-start | bytes 196616 | tf_op jit(solution)/shard_map/while/body/eval_jaxpr/ppermute | solution.py:29
  193.6 8.0 %collective-permute-start.1 = (bf16[4,64,128]{2,1,0:T(8,128)(2,1)}, bf16[4,64,128]{2,1,0:T(8,128)(2,1)}, u32[]{:S(2)}, u32[]{:S(2)}) collective-permute-start(bf16[4,64,128]{2,1,0:T(8,128)(2,1)} %get-tuple-element.264), channel_id=1, source_target_pairs={{16,0},{32,16},{48,32},{64,48},{80,64},{96,80},{112,96},{128,112},... | collective-permute-start | bytes 196616 | tf_op jit(solution)/shard_map/while/body/eval_jaxpr/ppermute | solution.py:29
  204.8 8.1 %collective-permute-start = (bf16[4,64,128]{2,1,0:T(8,128)(2,1)}, bf16[4,64,128]{2,1,0:T(8,128)(2,1)}, u32[]{:S(2)}, u32[]{:S(2)}) collective-permute-start(bf16[4,64,128]{2,1,0:T(8,128)(2,1)} %get-tuple-element.263), channel_id=1, source_target_pairs={{0,16},{16,32},{32,48},{48,64},{64,80},{80,96},{96,112},{112,128},... | collective-permute-start | bytes 196616 | tf_op jit(solution)/shard_map/while/body/eval_jaxpr/ppermute | solution.py:29
  206.7 8.0 %collective-permute-start.1 = (bf16[4,64,128]{2,1,0:T(8,128)(2,1)}, bf16[4,64,128]{2,1,0:T(8,128)(2,1)}, u32[]{:S(2)}, u32[]{:S(2)}) collective-permute-start(bf16[4,64,128]{2,1,0:T(8,128)(2,1)} %get-tuple-element.264), channel_id=1, source_target_pairs={{16,0},{32,16},{48,32},{64,48},{80,64},{96,80},{112,96},{128,112},... | collective-permute-start | bytes 196616 | tf_op jit(solution)/shard_map/while/body/eval_jaxpr/ppermute | solution.py:29
  217.8 8.1 %collective-permute-start = (bf16[4,64,128]{2,1,0:T(8,128)(2,1)}, bf16[4,64,128]{2,1,0:T(8,128)(2,1)}, u32[]{:S(2)}, u32[]{:S(2)}) collective-permute-start(bf16[4,64,128]{2,1,0:T(8,128)(2,1)} %get-tuple-element.263), channel_id=1, source_target_pairs={{0,16},{16,32},{32,48},{48,64},{64,80},{80,96},{96,112},{112,128},... | collective-permute-start | bytes 196616 | tf_op jit(solution)/shard_map/while/body/eval_jaxpr/ppermute | solution.py:29
  219.8 8.0 %collective-permute-start.1 = (bf16[4,64,128]{2,1,0:T(8,128)(2,1)}, bf16[4,64,128]{2,1,0:T(8,128)(2,1)}, u32[]{:S(2)}, u32[]{:S(2)}) collective-permute-start(bf16[4,64,128]{2,1,0:T(8,128)(2,1)} %get-tuple-element.264), channel_id=1, source_target_pairs={{16,0},{32,16},{48,32},{64,48},{80,64},{96,80},{112,96},{128,112},... | collective-permute-start | bytes 196616 | tf_op jit(solution)/shard_map/while/body/eval_jaxpr/ppermute | solution.py:29
  230.9 8.1 %collective-permute-start = (bf16[4,64,128]{2,1,0:T(8,128)(2,1)}, bf16[4,64,128]{2,1,0:T(8,128)(2,1)}, u32[]{:S(2)}, u32[]{:S(2)}) collective-permute-start(bf16[4,64,128]{2,1,0:T(8,128)(2,1)} %get-tuple-element.263), channel_id=1, source_target_pairs={{0,16},{16,32},{32,48},{48,64},{64,80},{80,96},{96,112},{112,128},... | collective-permute-start | bytes 196616 | tf_op jit(solution)/shard_map/while/body/eval_jaxpr/ppermute | solution.py:29
  232.8 8.0 %collective-permute-start.1 = (bf16[4,64,128]{2,1,0:T(8,128)(2,1)}, bf16[4,64,128]{2,1,0:T(8,128)(2,1)}, u32[]{:S(2)}, u32[]{:S(2)}) collective-permute-start(bf16[4,64,128]{2,1,0:T(8,128)(2,1)} %get-tuple-element.264), channel_id=1, source_target_pairs={{16,0},{32,16},{48,32},{64,48},{80,64},{96,80},{112,96},{128,112},... | collective-permute-start | bytes 196616 | tf_op jit(solution)/shard_map/while/body/eval_jaxpr/ppermute | solution.py:29
  244.0 8.1 %collective-permute-start = (bf16[4,64,128]{2,1,0:T(8,128)(2,1)}, bf16[4,64,128]{2,1,0:T(8,128)(2,1)}, u32[]{:S(2)}, u32[]{:S(2)}) collective-permute-start(bf16[4,64,128]{2,1,0:T(8,128)(2,1)} %get-tuple-element.263), channel_id=1, source_target_pairs={{0,16},{16,32},{32,48},{48,64},{64,80},{80,96},{96,112},{112,128},... | collective-permute-start | bytes 196616 | tf_op jit(solution)/shard_map/while/body/eval_jaxpr/ppermute | solution.py:29
  245.9 8.0 %collective-permute-start.1 = (bf16[4,64,128]{2,1,0:T(8,128)(2,1)}, bf16[4,64,128]{2,1,0:T(8,128)(2,1)}, u32[]{:S(2)}, u32[]{:S(2)}) collective-permute-start(bf16[4,64,128]{2,1,0:T(8,128)(2,1)} %get-tuple-element.264), channel_id=1, source_target_pairs={{16,0},{32,16},{48,32},{64,48},{80,64},{96,80},{112,96},{128,112},... | collective-permute-start | bytes 196616 | tf_op jit(solution)/shard_map/while/body/eval_jaxpr/ppermute | solution.py:29
  257.1 8.1 %collective-permute-start = (bf16[4,64,128]{2,1,0:T(8,128)(2,1)}, bf16[4,64,128]{2,1,0:T(8,128)(2,1)}, u32[]{:S(2)}, u32[]{:S(2)}) collective-permute-start(bf16[4,64,128]{2,1,0:T(8,128)(2,1)} %get-tuple-element.263), channel_id=1, source_target_pairs={{0,16},{16,32},{32,48},{48,64},{64,80},{80,96},{96,112},{112,128},... | collective-permute-start | bytes 196616 | tf_op jit(solution)/shard_map/while/body/eval_jaxpr/ppermute | solution.py:29
  259.0 8.0 %collective-permute-start.1 = (bf16[4,64,128]{2,1,0:T(8,128)(2,1)}, bf16[4,64,128]{2,1,0:T(8,128)(2,1)}, u32[]{:S(2)}, u32[]{:S(2)}) collective-permute-start(bf16[4,64,128]{2,1,0:T(8,128)(2,1)} %get-tuple-element.264), channel_id=1, source_target_pairs={{16,0},{32,16},{48,32},{64,48},{80,64},{96,80},{112,96},{128,112},... | collective-permute-start | bytes 196616 | tf_op jit(solution)/shard_map/while/body/eval_jaxpr/ppermute | solution.py:29
  270.2 8.1 %collective-permute-start = (bf16[4,64,128]{2,1,0:T(8,128)(2,1)}, bf16[4,64,128]{2,1,0:T(8,128)(2,1)}, u32[]{:S(2)}, u32[]{:S(2)}) collective-permute-start(bf16[4,64,128]{2,1,0:T(8,128)(2,1)} %get-tuple-element.263), channel_id=1, source_target_pairs={{0,16},{16,32},{32,48},{48,64},{64,80},{80,96},{96,112},{112,128},... | collective-permute-start | bytes 196616 | tf_op jit(solution)/shard_map/while/body/eval_jaxpr/ppermute | solution.py:29
  272.1 8.0 %collective-permute-start.1 = (bf16[4,64,128]{2,1,0:T(8,128)(2,1)}, bf16[4,64,128]{2,1,0:T(8,128)(2,1)}, u32[]{:S(2)}, u32[]{:S(2)}) collective-permute-start(bf16[4,64,128]{2,1,0:T(8,128)(2,1)} %get-tuple-element.264), channel_id=1, source_target_pairs={{16,0},{32,16},{48,32},{64,48},{80,64},{96,80},{112,96},{128,112},... | collective-permute-start | bytes 196616 | tf_op jit(solution)/shard_map/while/body/eval_jaxpr/ppermute | solution.py:29
  283.2 8.1 %collective-permute-start = (bf16[4,64,128]{2,1,0:T(8,128)(2,1)}, bf16[4,64,128]{2,1,0:T(8,128)(2,1)}, u32[]{:S(2)}, u32[]{:S(2)}) collective-permute-start(bf16[4,64,128]{2,1,0:T(8,128)(2,1)} %get-tuple-element.263), channel_id=1, source_target_pairs={{0,16},{16,32},{32,48},{48,64},{64,80},{80,96},{96,112},{112,128},... | collective-permute-start | bytes 196616 | tf_op jit(solution)/shard_map/while/body/eval_jaxpr/ppermute | solution.py:29
  285.2 8.0 %collective-permute-start.1 = (bf16[4,64,128]{2,1,0:T(8,128)(2,1)}, bf16[4,64,128]{2,1,0:T(8,128)(2,1)}, u32[]{:S(2)}, u32[]{:S(2)}) collective-permute-start(bf16[4,64,128]{2,1,0:T(8,128)(2,1)} %get-tuple-element.264), channel_id=1, source_target_pairs={{16,0},{32,16},{48,32},{64,48},{80,64},{96,80},{112,96},{128,112},... | collective-permute-start | bytes 196616 | tf_op jit(solution)/shard_map/while/body/eval_jaxpr/ppermute | solution.py:29
  (32 other events, 646.1 us)
Sparse Core Ops, SparseCore 0:
  403.3 216.0 reduce-scatter.3
where the time goes:
time: 642 us; the launch traced here: 630 us
  waiting for transfers between devices  236 us (37%)
  starting transfers between devices  123 us (19%)
  other arithmetic  97.2 us (15%)
  local copies, waits for them, and re-layouts  69.2 us (11%)
  blocking collectives  44.5 us (7%)
  matrix products  43.9 us (7%)
  between operations  14.2 us (2%)
    unnamed x2, waiting for transfers between devices  216 us
    ppermute x30, starting transfers between devices, shifted(): return lax.ppermute(value, axis, pairs)  116 us
    psum x1, blocking collectives, local(): squares = lax.psum(jnp.sum(gated * gated, axis=-1), 'tensor')  44.5 us
    unnamed x73, local copies, waits for them, and re-layouts  38.9 us
    convert_element_type x15, other arithmetic, relay(): (device_decay[1][:, None, None] * into_reverse + device_state[1]).astype(...  23.9 us
    convert_element_type x15, other arithmetic, relay(): into_reverse = shifted((device_decay[1][:, None, None] * into_reverse + d...  22.4 us
    ppermute x30, waiting for transfers between devices, shifted(): return lax.ppermute(value, axis, pairs)  20.2 us
  transfers between devices with their start and end apart: 33, of which 31 were waited for; matrix products, arithmetic and copies ran while one was open for 8% of the time, Pallas kernels for 0%

commit v1 on v0

v1 whole, which is shorter than its diff:
```python
import functools

import jax
import jax.numpy as jnp
from jax import lax
from jax.experimental import pallas as pl
from jax.experimental.pallas import tpu as pltpu
from jax.sharding import PartitionSpec as P

f32 = jnp.float32
bf16 = jnp.bfloat16
i32 = jnp.int32
highest = lax.Precision.HIGHEST
epsilon = 1e-05

LANES = 128
SEQ = 16384
ROWS = SEQ // LANES
BLOCK = 256
STATE = 128
HEAD = 64
TOKENS = 5
NONE = 5
WIDE = 1024
HEADS = WIDE // HEAD
GRAMS = 144

SAME_HEADS = [[0, 1, 2, 3], [4, 5, 6, 7], [8, 9, 10, 11], [12, 13, 14, 15]]
SAME_POSITIONS = [[0, 4, 8, 12], [1, 5, 9, 13], [2, 6, 10, 14], [3, 7, 11, 15]]

TN = (((0,), (0,)), ((), ()))
NT = (((1,), (1,)), ((), ()))


def iota(shape, dim):
    return lax.broadcasted_iota(i32, shape, dim)


def silu(v):
    return v / (1.0 + jnp.exp(-v))


def split(x, terms=3):
    parts = []
    for _ in range(terms):
        part = x.astype(bf16)
        parts.append(part)
        x = x - part.astype(f32)
    return parts


def table_kernel(
    emb, gain, wz, wx, wbc, wdt, bias, alog, dskip, convx, convbc, ggain, tab, cbc, rows
):
    rows[...] = jnp.zeros_like(rows)
    rows[0:TOKENS, :] = emb[...].astype(f32)
    e = rows[...]
    normed = (
        e * lax.rsqrt(jnp.mean(e * e, axis=-1, keepdims=True) + epsilon) * gain[...]
    ).astype(bf16)

    def project(w):
        return jnp.dot(normed, w[...], preferred_element_type=f32)

    z = project(wz).astype(bf16).astype(f32)
    xs = project(wx).astype(bf16).astype(f32)
    bc = project(wbc).astype(bf16).astype(f32)
    raw = project(wdt) + bias[...]
    dt = jnp.maximum(raw, 0.0) + jnp.log1p(jnp.exp(-jnp.abs(raw)))
    width = z.shape[1]

    def spread(v):
        lane = iota((v.shape[0], width), 1)
        out = jnp.broadcast_to(v[:, 0:1], lane.shape)
        for h in range(1, v.shape[1]):
            out = jnp.where(lane >= h * HEAD, v[:, h : h + 1], out)
        return out

    row = iota((8, width), 0)
    own = jnp.where(row == 6, spread(dskip[...]), spread(jnp.exp(alog[...])))
    own = jnp.where(row == 5, ggain[...], own)
    tab[0:8, :] = jnp.where(row < TOKENS, silu(z), own)
    tab[8:16, :] = xs
    tab[16:24, :] = jnp.zeros((8, width), f32)
    tab[16:20, :] = convx[...]
    tab[24:32, :] = jnp.where(row < TOKENS, spread(dt), 0.0)
    for k in range(4):
        cbc[8 * k : 8 * k + 8, :] = convbc[k : k + 1, :] * bc


def block_kernel(
    place, comp, ids_ref, t0, t1, t2, t3, cbc, vg, sq, toks, gram, side_tok, count
):
    r0 = place[0]
    ids = ids_ref[...]
    row = iota((ROWS, LANES), 0)
    lane = iota((ROWS, LANES), 1)
    at = row * LANES + lane
    flip = jnp.zeros_like(ids)
    for k in range(TOKENS):
        flip = jnp.where(ids == k, comp[k], flip)

    def before(x):
        y = pltpu.roll(x, 1, 1)
        y = jnp.where(lane == 0, pltpu.roll(y, 1, 0), y)
        return jnp.where(at == 0, NONE, y)

    def after(x):
        y = pltpu.roll(x, LANES - 1, 1)
        y = jnp.where(lane == LANES - 1, pltpu.roll(y, ROWS - 1, 0), y)
        return jnp.where(at == SEQ - 1, NONE, y)

    fs = [ids]
    rs = [flip]
    for k in range(3):
        fs.append(before(fs[-1]))
        rs.append(after(rs[-1]))
    for k in range(4):
        toks[k] = fs[k]
        toks[4 + k] = rs[k]
    g_f = 25 * fs[3] + 5 * fs[2] + fs[1]
    g_r = 25 * rs[3] + 5 * rs[2] + rs[1]
    for k in range(3):
        g_f = jnp.where(at == k, 125 + k, g_f)
        g_r = jnp.where(at == SEQ - 1 - k, 125 if k == 0 else 127 + k, g_r)
    ahead = row < r0
    tok = jnp.where(ahead, ids, flip)
    tok = jnp.where(ahead | (row > r0 + 1), tok, -1)
    gram[...] = jnp.where(ahead, g_f, g_r)
    side_tok[...] = tok

    hot = [jnp.where(tok == k, 1.0, 0.0) for k in range(TOKENS)]
    hots = jnp.concatenate(hot, axis=0).astype(bf16)
    strict = jnp.where(row < lane, 1.0, 0.0).astype(bf16)
    prior = jnp.dot(hots, strict, preferred_element_type=f32)
    total = jnp.dot(hots, jnp.ones((LANES, LANES), bf16), preferred_element_type=f32)
    between = ((row < lane) & (lane < r0)) | ((lane > r0 + 1) & (lane < row))
    between = jnp.where(between, 1.0, 0.0).astype(bf16)
    for k in range(TOKENS):
        part = slice(k * ROWS, (k + 1) * ROWS)
        far = jnp.dot(between, total[part].astype(bf16), preferred_element_type=f32)
        near = jnp.where(ahead, total[part] - prior[part] - hot[k], prior[part])
        count[k] = near + far

    tab = jnp.concatenate([t0[...], t1[...], t2[...], t3[...]], axis=1)
    dt_tab = tab[24:32]
    rate_tab = tab[7:8] * dt_tab
    pick = jnp.where(iota((HEADS, WIDE), 1) == HEAD * iota((HEADS, WIDE), 0), 1.0, 0.0)
    rate = lax.dot_general(pick, rate_tab, NT, precision=highest, preferred_element_type=f32)
    rate_t = lax.dot_general(rate_tab, pick, NT, precision=highest, preferred_element_type=f32)
    columns = [jnp.broadcast_to(-rate[:, k : k + 1], (HEADS, BLOCK)) for k in range(TOKENS)]

    def pair(ref, index):
        r = 2 * index
        return jnp.concatenate([ref[pl.ds(r, 1), :], ref[pl.ds(r + 1, 1), :]], axis=1)

    gram_row = iota((GRAMS, BLOCK), 0)

    def gather(step, total):
        windows = []
        weights = []
        for j in range(4):
            index = 4 * step + j
            token = pair(side_tok, index)
            window = pair(gram, index)
            exponent = columns[0] * pair(count.at[0], index)
            for k in range(1, TOKENS):
                exponent = exponent + columns[k] * pair(count.at[k], index)
            weight = jnp.exp(exponent)
            first = jnp.where(2 * index < r0, 1.0, 0.0)
            forward = weight * first
            reverse = weight * (1.0 - first)
            weights.append(
                jnp.concatenate(
                    [
                        jnp.where(token == k, w, 0.0)
                        for w in (forward, reverse)
                        for k in range(TOKENS)
                    ],
                    axis=0,
                ).astype(bf16)
            )
            windows.append(jnp.where(gram_row == window, 1.0, 0.0).astype(bf16))
        return total + lax.dot_general(
            jnp.concatenate(windows, axis=1),
            jnp.concatenate(weights, axis=1),
            NT,
            preferred_element_type=f32,
        )

    hist = jnp.zeros((GRAMS, 2 * TOKENS * HEADS), f32)
    for step in range(ROWS // 8):
        hist = gather(step, hist)
    hist = hist.astype(bf16)

    taps = jnp.concatenate([tab[16 + k : 17 + k] * tab[8:16] for k in range(4)], axis=0)
    bc_taps = cbc[...]
    g = iota((GRAMS, 24), 0)
    col = iota((GRAMS, 24), 1)
    d0 = sum(jnp.where(g >= 25 * m, 1, 0) for m in range(1, TOKENS))
    rest = g - 25 * d0
    d1 = sum(jnp.where(rest >= 5 * m, 1, 0) for m in range(1, TOKENS))
    d2 = rest - 5 * d1
    plain = g < 125
    d0 = jnp.where(plain, d0, NONE)
    d1 = jnp.where(plain, d1, NONE)
    d2 = jnp.where(plain, d2, NONE)
    d1 = jnp.where(g == 127, ids[0:1, 0:1], d1)
    d2 = jnp.where(g == 126, ids[0:1, 0:1], d2)
    d2 = jnp.where(g == 127, ids[0:1, 1:2], d2)
    d1 = jnp.where(g == 129, flip[ROWS - 1 :, LANES - 1 :], d1)
    d2 = jnp.where(g == 128, flip[ROWS - 1 :, LANES - 1 :], d2)
    d2 = jnp.where(g == 129, flip[ROWS - 1 :, LANES - 2 : LANES - 1], d2)
    digit = jnp.where(col < 8, d0, jnp.where(col < 16, d1, d2))
    older = jnp.where(digit == (col & 7), 1.0, 0.0)
    x_older = jnp.dot(older, taps[0:24], precision=highest, preferred_element_type=f32)
    b_older = jnp.dot(older, bc_taps[0:24, :STATE], precision=highest, preferred_element_type=f32)
    lift = iota((HEADS, WIDE), 1) - HEAD * iota((HEADS, WIDE), 0)
    lift = jnp.where((lift >= 0) & (lift < HEAD), 1.0, 0.0).astype(bf16)
    feeds = []
    moved = [[], []]
    for k in range(TOKENS):
        feeds.append(silu(b_older + bc_taps[24 + k : 25 + k, :STATE]).astype(bf16))
        act = silu(x_older + taps[24 + k : 25 + k]) * dt_tab[k : k + 1]
        for s in range(2):
            start = (s * TOKENS + k) * HEADS
            part = jnp.dot(hist[:, start : start + HEADS], lift, preferred_element_type=f32)
            moved[s].append((act * part).astype(bf16))
    feeds = jnp.concatenate(feeds, axis=0)
    entering = [
        lax.dot_general(
            feeds, jnp.concatenate(moved[s], axis=0), TN, preferred_element_type=f32
        ).astype(bf16)
        for s in range(2)
    ]

    def own(m):
        return jnp.concatenate([toks[m, pl.ds(r0, 1), :], toks[m, pl.ds(r0 + 1, 1), :]], axis=1)

    place_row = iota((32, BLOCK), 0)
    hot_own = []
    for s in range(2):
        digit = own(4 * s)
        for k in range(3):
            digit = jnp.where(place_row < 8 * (3 - k), own(4 * s + k + 1), digit)
        hot_own.append(jnp.where(digit == (place_row & 7), 1.0, 0.0))
    hot_all = jnp.concatenate(hot_own, axis=1)
    hot_taps = jnp.concatenate([hot_all] * 3, axis=0).astype(bf16)
    hot_now = jnp.concatenate([hot_all[24:32]] * 3, axis=0).astype(bf16)

    def look(hots, table):
        return lax.dot_general(
            hots, jnp.concatenate(split(table), axis=0), TN, preferred_element_type=f32
        )

    bc_act = silu(look(hot_taps, bc_taps))
    lane_b = iota((BLOCK, BLOCK), 1)
    row_b = iota((BLOCK, BLOCK), 0)
    lane_p = iota((BLOCK, LANES), 1)
    low = lane_p < HEAD
    gate_tab = jnp.where(iota((8, WIDE), 0) < TOKENS, tab[0:8], 0.0)
    for s in range(2):
        rows = slice(s * BLOCK, (s + 1) * BLOCK)
        taps_s = hot_taps[:, rows]
        now_s = hot_now[:, rows]
        feed = bc_act[rows, :STATE].astype(bf16)
        read = bc_act[rows, STATE:].astype(bf16)
        seen = (lane_b <= row_b) if s == 0 else (lane_b >= row_b)
        scores = lax.dot_general(read, feed, NT, preferred_element_type=f32)
        scores = jnp.where(seen, scores, 0.0)
        inclusive = (row_b <= lane_b) if s == 0 else (row_b >= lane_b)
        inclusive = jnp.where(inclusive, 1.0, 0.0).astype(bf16)
        counts = jnp.dot(hot_own[s][24:32].astype(bf16), inclusive, preferred_element_type=f32)
        cum_row = -jnp.dot(rate, counts, precision=highest, preferred_element_type=f32)
        cum_col = -lax.dot_general(
            counts, rate_t, TN, precision=highest, preferred_element_type=f32
        )
        decay = jnp.exp(cum_col)
        squares = jnp.zeros((BLOCK, LANES), f32)
        for p in range(HEADS // 2):
            chans = slice(p * LANES, (p + 1) * LANES)
            xs = silu(look(taps_s, taps[:, chans]))
            steps = look(now_s, dt_tab[:, chans])
            gate = look(now_s, gate_tab[:, chans])
            fed = (xs * steps).astype(bf16)
            parts = []
            for h in (2 * p, 2 * p + 1):
                differ = cum_col[:, h : h + 1] - cum_row[h : h + 1, :]
                parts.append((jnp.exp(jnp.minimum(differ, 0.0)) * scores).astype(bf16))
            zero = jnp.zeros_like(fed)
            inside = jnp.dot(
                jnp.concatenate(parts, axis=1),
                jnp.concatenate([jnp.where(low, fed, zero), jnp.where(low, zero, fed)], axis=0),
                preferred_element_type=f32,
            )
            carried = jnp.dot(read, entering[s][:, chans], preferred_element_type=f32)
            carried = carried * jnp.where(
                low, decay[:, 2 * p : 2 * p + 1], decay[:, 2 * p + 1 : 2 * p + 2]
            )
            v = (inside + carried + tab[6:7, chans] * xs) * gate
            squares = squares + v * v
            vg[rows, chans] = (v * tab[5:6, chans]).astype(bf16)
        summed = lax.dot_general(
            jnp.ones((8, LANES), f32), squares, NT, precision=highest, preferred_element_type=f32
        )
        sq[:, rows] = summed[0:1]


def out_kernel(parity, vg, sq, w_own, a1, a2, a3, b1, b2, b3, out, g_all):
    @pl.when(pl.program_id(0) == 0)
    def _():
        first = iota((8, 2 * BLOCK), 0) == 0
        inverse = jnp.where(first, lax.rsqrt(sq[...] / 4096.0 + epsilon), 0.0)
        inverse = lax.dot_general(
            inverse, jnp.ones((8, LANES), f32), TN, precision=highest, preferred_element_type=f32
        )
        for p in range(WIDE // LANES):
            chans = slice(p * LANES, (p + 1) * LANES)
            strands = [
                (vg[s * BLOCK : (s + 1) * BLOCK, chans].astype(f32) * inverse[s * BLOCK : (s + 1) * BLOCK])
                .astype(bf16)
                .astype(f32)
                for s in range(2)
            ]
            g_all[:, chans] = (strands[0] + strands[1]).astype(bf16)

    even = parity[0] == 0
    weights = [w_own[...]]
    for a, b in ((a1, b1), (a2, b2), (a3, b3)):
        mine = a[...]
        theirs = b[...]
        weights.append(jnp.where(even, mine, theirs))
        weights.append(jnp.where(even, theirs, mine))
    result = jnp.dot(
        g_all[...], jnp.concatenate(weights, axis=0), preferred_element_type=f32
    ).astype(bf16)
    for j in range(out.shape[0]):
        out[j] = result[:, j * LANES : (j + 1) * LANES]


def build_tables(
    embedding, norm_gain, w_z, w_x, w_bc, w_dt, dt_bias, a_log, d_skip, conv_x, conv_bc, gate_gain
):
    width = w_z.shape[1]
    return pl.pallas_call(
        table_kernel,
        out_shape=(
            jax.ShapeDtypeStruct((32, width), f32),
            jax.ShapeDtypeStruct((32, w_bc.shape[1]), f32),
        ),
        scratch_shapes=[pltpu.VMEM((8, embedding.shape[1]), f32)],
        compiler_params=pltpu.CompilerParams(vmem_limit_bytes=40 * 2**20),
        name="tables",
    )(
        embedding,
        norm_gain[None],
        w_z,
        w_x,
        w_bc,
        w_dt,
        dt_bias[None],
        a_log[None],
        d_skip[None],
        conv_x,
        conv_bc,
        gate_gain[None],
    )


def run_block(place, complement, ids, tabs, cbc):
    smem = pl.BlockSpec(memory_space=pltpu.SMEM)
    vmem = pl.BlockSpec(memory_space=pltpu.VMEM)
    return pl.pallas_call(
        block_kernel,
        in_specs=[smem, smem] + [vmem] * 6,
        out_specs=(vmem, vmem),
        out_shape=(
            jax.ShapeDtypeStruct((2 * BLOCK, WIDE), bf16),
            jax.ShapeDtypeStruct((1, 2 * BLOCK), f32),
        ),
        scratch_shapes=[
            pltpu.VMEM((8, ROWS, LANES), i32),
            pltpu.VMEM((ROWS, LANES), i32),
            pltpu.VMEM((ROWS, LANES), i32),
            pltpu.VMEM((TOKENS, ROWS, LANES), f32),
        ],
        compiler_params=pltpu.CompilerParams(vmem_limit_bytes=48 * 2**20),
        name="block",
    )(place, complement, ids, *tabs, cbc)


def run_out(parity, vg, sq, w_own, mine, theirs):
    features = w_own.shape[1]
    tile = 512
    half = w_own.shape[0] // 2
    whole = pl.BlockSpec((2 * BLOCK, WIDE), lambda n: (0, 0))
    half_spec = pl.BlockSpec((half, tile), lambda n: (0, n))
    return pl.pallas_call(
        out_kernel,
        grid=(features // tile,),
        in_specs=[
            pl.BlockSpec(memory_space=pltpu.SMEM),
            whole,
            pl.BlockSpec((1, 2 * BLOCK), lambda n: (0, 0)),
            pl.BlockSpec((2 * half, tile), lambda n: (0, n)),
        ]
        + [half_spec] * 6,
        out_specs=pl.BlockSpec((tile // LANES, BLOCK, LANES), lambda n: (n, 0, 0)),
        out_shape=jax.ShapeDtypeStruct((features // LANES, BLOCK, LANES), bf16),
        scratch_shapes=[pltpu.VMEM((BLOCK, WIDE), bf16)],
        compiler_params=pltpu.CompilerParams(vmem_limit_bytes=40 * 2**20),
        name="project",
    )(parity, vg, sq, w_own, *mine, *theirs)


def swap(x, axis, distance):
    count = lax.axis_size(axis)
    return lax.ppermute(x, axis, [(i, i ^ distance) for i in range(count)])


def local(
    ids,
    complement,
    embedding,
    norm_gain,
    w_z,
    w_x,
    w_bc,
    w_dt,
    dt_bias,
    a_log,
    conv_x,
    conv_bc,
    d_skip,
    gate_gain,
    w_out,
):
    context = lax.axis_index("context").astype(i32)
    tensor = lax.axis_index("tensor").astype(i32)
    parity = context % 2
    half = w_out.shape[0] // 2
    share = lax.dynamic_slice_in_dim(w_out, parity * half, half, 0)
    mine = [swap(share, "tensor", d) for d in (1, 2, 3)]
    theirs = [swap(x, "context", 1) for x in mine]

    tab, cbc = build_tables(
        embedding, norm_gain, w_z, w_x, w_bc, w_dt, dt_bias, a_log, d_skip, conv_x, conv_bc, gate_gain
    )
    tabs = [tab] + [swap(tab, "tensor", d) for d in (1, 2, 3)]

    count = lax.axis_size("context")
    spread = jnp.broadcast_to(ids.reshape(1, -1, LANES), (count, ids.shape[0] // LANES, LANES))
    everyone = lax.all_to_all(spread, "context", 0, 0, tiled=True).reshape(ROWS, LANES)

    place = (context * (ids.shape[0] // LANES) + (tensor % 4) * (BLOCK // LANES)).reshape(1)
    vg, sq = run_block(place, complement, everyone, tabs, cbc)
    sq = lax.psum(sq, "tensor", axis_index_groups=SAME_POSITIONS)
    terms = run_out(parity.reshape(1), vg, sq, w_out, mine, theirs)
    arrived = lax.all_to_all(terms, "tensor", 0, 0, tiled=True)
    summed = jnp.sum(arrived.astype(f32).reshape(4, 4, BLOCK, LANES), axis=0)
    return summed.reshape(4 * BLOCK, LANES).astype(bf16)


def solution(mesh):
    placed = (
        P("context"),
        P(),
        P(),
        P(),
        P(None, "tensor"),
        P(None, "tensor"),
        P(),
        P(None, "tensor"),
        P("tensor"),
        P("tensor"),
        P(None, "tensor"),
        P(),
        P("tensor"),
        P("tensor"),
        P("tensor", None),
    )
    return jax.shard_map(
        local, mesh=mesh, in_specs=placed, out_specs=P("context", "tensor"), check_vma=False
    )
```

time: 642 us -> 114 us (0.18); the launches traced: 630 us -> 113 us
  waiting for transfers between devices: 236 us -> 26.4 us
  starting transfers between devices: 123 us -> 16.3 us
  other arithmetic: 97.2 us -> 0.91 us
  local copies, waits for them, and re-layouts: 69.2 us -> 5.93 us
  matrix products: 43.9 us -> 0 us
  Pallas kernels: 0 us -> 17.7 us
  between operations: 14.2 us -> 0.11 us
    unnamed x2 -> x0, waiting for transfers between devices: 216 us -> none
    ppermute x32 -> x9, starting transfers between devices: 123 us -> 10.3 us  [swap(): return lax.ppermute(x, axis, [(i, i ^ distance) for i in range(count)])]
    convert_element_type x50 -> x0, other arithmetic: 64.7 us -> none  [the longest x15 23.9 us: relay(): (device_decay[1][:, None, None] * into_reverse + device_state[1]).astype(...]
    dot_general x10 -> x0, matrix products: 43.9 us -> none  [the longest x1 9.49 us: local(): jnp.einsum('gctsh,gcshp->gcthp', weights, values, precision=highest)]
    unnamed x73 -> x31, local copies, waits for them, and re-layouts: 38.9 us -> 4.12 us
    all_to_all x0 -> x1, blocking collectives: none -> 31.2 us  [local(): arrived = lax.all_to_all(terms, 'tensor', 0, 0, tiled=True)]
    psum x1, blocking collectives: 44.5 us -> 14.8 us  [local(): sq = lax.psum(sq, 'tensor', axis_index_groups=SAME_POSITIONS)]
    pallas_call x0 -> x3, Pallas kernels: none -> 17.7 us  [the longest x1 12.4 us: run_block(): pl.pallas_call(block_kernel, in_specs=[smem, smem] + [vmem] * 6, out_spec...]
  transfers between devices with their start and end apart: 33 -> 10, of which waited for: 31 -> 5; matrix products, arithmetic and copies ran while one was open for 8% -> 1% of each run, Pallas kernels for 0% -> 12%
where the time goes in v1:
time: 114 us; the launch traced here: 113 us
  blocking collectives  46 us (40%)
  waiting for transfers between devices  26.4 us (23%)
  Pallas kernels  17.7 us (16%)
  starting transfers between devices  16.3 us (14%)
  local copies, waits for them, and re-layouts  5.93 us (5%)
    all_to_all x1, blocking collectives, local(): arrived = lax.all_to_all(terms, 'tensor', 0, 0, tiled=True)  31.2 us
    ppermute x9, waiting for transfers between devices, swap(): return lax.ppermute(x, axis, [(i, i ^ distance) for i in range(count)])  26.4 us
    psum x1, blocking collectives, local(): sq = lax.psum(sq, 'tensor', axis_index_groups=SAME_POSITIONS)  14.8 us
    pallas_call x1, Pallas kernels, run_block(): pl.pallas_call(block_kernel, in_specs=[smem, smem] + [vmem] * 6, out_spec...  12.4 us
    ppermute x9, starting transfers between devices, swap(): return lax.ppermute(x, axis, [(i, i ^ distance) for i in range(count)])  10.3 us
    all_to_all x1, starting transfers between devices, local(): lax.all_to_all(spread, 'context', 0, 0, tiled=True).reshape(ROWS, LANES)  5.95 us
    pallas_call x1, Pallas kernels, run_out(): pl.pallas_call(out_kernel, grid=(features // tile,), in_specs=[pl.BlockSp...  4.46 us
    unnamed x31, local copies, waits for them, and re-layouts  4.12 us
  transfers between devices with their start and end apart: 10, of which 5 were waited for; matrix products, arithmetic and copies ran while one was open for 1% of the time, Pallas kernels for 12%

profile of v1, /device:TPU:2, one launch (start us, length us, event | category | flops | bytes accessed | tf_op | source)
XLA Modules:
  0.0 113.3 jit_solution(11019996459787542094)
XLA Ops:
  0.0 1.2 %constant_dynamic-slice_fusion = bf16[128,2048]{1,0:T(8,128)(2,1)S(1)} fusion(bf16[256,2048]{1,0:T(8,128)(2,1)} %w_own.1, s32[]{:T(128)S(6)} %select_n.16), kind=kLoop, calls=%fused_computation | loop fusion | bytes 1048580 | tf_op jit(solution)/shard_map/dynamic_slice | solution.py:442
  1.2 0.0 copy-start.4
  1.2 3.6 %collective-permute-start.5 = (bf16[128,2048]{1,0:T(8,128)(2,1)S(1)}, bf16[128,2048]{1,0:T(8,128)(2,1)S(1)}, u32[]{:S(2)}, u32[]{:S(2)}) collective-permute-start(bf16[128,2048]{1,0:T(8,128)(2,1)S(1)} %constant_dynamic-slice_fusion), channel_id=1, source_target_pairs={{0,3},{1,2},{2,1},{3,0},{4,7},{5,6},{6,5},{7,4},{8,11},{9,10},{10,... | collective-permute-start | bytes 1572872 | tf_op jit(solution)/shard_map/ppermute | solution.py:418
  4.8 0.1 collective-permute-start.4
  4.9 1.4 %collective-permute-start.3 = (bf16[128,2048]{1,0:T(8,128)(2,1)S(1)}, bf16[128,2048]{1,0:T(8,128)(2,1)}, u32[]{:S(2)}, u32[]{:S(2)}) collective-permute-start(bf16[128,2048]{1,0:T(8,128)(2,1)S(1)} %constant_dynamic-slice_fusion), channel_id=1, source_target_pairs={{0,1},{1,0},{2,3},{3,2},{4,5},{5,4},{6,7},{7,6},{8,9},{9,8},{10,11... | collective-permute-start | bytes 1572872 | tf_op jit(solution)/shard_map/ppermute | solution.py:418
  6.3 12.3 %collective-permute-done.5.a3 = bf16[128,2048]{1,0:T(8,128)(2,1)S(1)} collective-permute-done((bf16[128,2048]{1,0:T(8,128)(2,1)S(1)}, bf16[128,2048]{1,0:T(8,128)(2,1)S(1)}, u32[]{:S(2)}, u32[]{:S(2)}) %collective-permute-start.5) | collective-permute-done | bytes 524320 | tf_op jit(solution)/shard_map/ppermute | solution.py:418
  18.5 9.3 %collective-permute-done.4.a2 = bf16[128,2048]{1,0:T(8,128)(2,1)} collective-permute-done((bf16[128,2048]{1,0:T(8,128)(2,1)S(1)}, bf16[128,2048]{1,0:T(8,128)(2,1)}, u32[]{:S(2)}, u32[]{:S(2)}) %collective-permute-start.4) | collective-permute-done | bytes 524320 | tf_op jit(solution)/shard_map/ppermute | solution.py:418
  27.9 0.8 collective-permute-done.3.a1
  28.7 0.0 collective-permute-start.6
  28.7 0.0 copy-start.10
  28.7 0.3 copy.16.wdt
  29.1 0.0 copy-start.8
  29.1 0.3 copy-done.6
  29.4 0.0 copy-done.7
  29.4 0.0 copy-done.11
  29.4 0.3 copy-done.5
  29.8 1.2 %copy-done.2 = bf16[2048,256]{1,0:T(8,128)(2,1)S(1)} copy-done((bf16[2048,256]{1,0:T(8,128)(2,1)S(1)}, bf16[2048,256]{1,0:T(8,128)(2,1)}, u32[]{:S(2)}) %copy-start.2) | copy-done | bytes 1048600
  31.0 1.2 %copy-done.3 = bf16[2048,256]{1,0:T(8,128)(2,1)S(1)} copy-done((bf16[2048,256]{1,0:T(8,128)(2,1)S(1)}, bf16[2048,256]{1,0:T(8,128)(2,1)}, u32[]{:S(2)}) %copy-start.3) | copy-done | bytes 1048600
  32.2 0.8 tables.1
  33.0 3.5 %collective-permute-start.2 = (f32[32,256]{1,0:T(8,128)S(1)}, f32[32,256]{1,0:T(8,128)S(1)}, u32[]{:S(2)}, u32[]{:S(2)}) collective-permute-start(f32[32,256]{1,0:T(8,128)S(1)} %get-tuple-element.9.t0), channel_id=1, source_target_pairs={{0,3},{1,2},{2,1},{3,0},{4,7},{5,6},{6,5},{7,4},{8,11},{9,10},{10,... | collective-permute-start | bytes 98312 | tf_op jit(solution)/shard_map/ppermute | solution.py:418
  36.5 0.6 broadcast_in_dim.23
  37.1 5.9 %all-to-all-start = ((s32[16,8,128]{2,1,0:T(8,128)}), s32[16,8,128]{2,1,0:T(8,128)S(1)}, u32[]{:S(2)}, u32[]{:S(2)}) async-start(s32[16,8,128]{2,1,0:T(8,128)} %broadcast_in_dim.23), calls=%async_computation | async-start | bytes 131072 | tf_op jit(solution)/shard_map/all_to_all | solution.py:453
  43.1 0.1 collective-permute-start.1
  43.2 1.6 %collective-permute-start = (f32[32,256]{1,0:T(8,128)S(1)}, f32[32,256]{1,0:T(8,128)S(1)}, u32[]{:S(2)}, u32[]{:S(2)}) collective-permute-start(f32[32,256]{1,0:T(8,128)S(1)} %get-tuple-element.9.t0), channel_id=1, source_target_pairs={{0,1},{1,0},{2,3},{3,2},{4,5},{5,4},{6,7},{7,6},{8,9},{9,8},{10,11... | collective-permute-start | bytes 98312 | tf_op jit(solution)/shard_map/ppermute | solution.py:418
  44.8 2.2 %collective-permute-done.1.t2 = f32[32,256]{1,0:T(8,128)S(1)} collective-permute-done((f32[32,256]{1,0:T(8,128)S(1)}, f32[32,256]{1,0:T(8,128)S(1)}, u32[]{:S(2)}, u32[]{:S(2)}) %collective-permute-start.1) | collective-permute-done | bytes 32800 | tf_op jit(solution)/shard_map/ppermute | solution.py:418
  47.0 1.8 %collective-permute-done.t1 = f32[32,256]{1,0:T(8,128)S(1)} collective-permute-done((f32[32,256]{1,0:T(8,128)S(1)}, f32[32,256]{1,0:T(8,128)S(1)}, u32[]{:S(2)}, u32[]{:S(2)}) %collective-permute-start) | collective-permute-done | bytes 32800 | tf_op jit(solution)/shard_map/ppermute | solution.py:418
  48.8 0.7 copy-done.12
  49.5 12.4 %block.1 = (bf16[512,1024]{1,0:T(8,128)(2,1)S(1)}, f32[1,512]{1,0:T(1,128)S(1)}) custom-call(s32[1]{0:T(128)} %bitcast.1.place, s32[5]{0:T(128)S(1)} %copy-done.12, s32[128,128]{1,0:T(8,128)S(1)} %bitcast.11, f32[32,256]{1,0:T(8,128)S(1)} %get-tuple-element.9.t0, f32[32,256]{1,0:T(8,128)S(1)} %collective-permute-done.t1, ...), custom_call_target="tpu_custom_call" | custom-call | tf_op jit(solution)/shard_map/block/pallas_call | solution.py:373
  61.9 14.8 %psum.7.sq = f32[1,512]{1,0:T(1,128)S(1)} all-reduce(f32[1,512]{1,0:T(1,128)S(1)} %get-tuple-element.12), channel_id=1, replica_groups={{0,4,8,12},{1,5,9,13},{2,6,10,14},{3,7,11,15},{16,20,24,28},{17,21,25,2..., use_global_device_ids=true, to_apply=%region_0.1 | all-reduce | flops 512 | bytes 4096 | tf_op jit(solution)/shard_map/psum | solution.py:457
  76.7 4.5 %project.1 = bf16[16,256,128]{2,1,0:T(8,128)(2,1)S(1)} custom-call(s32[1]{0:T(128)} %bitcast.parity, bf16[512,1024]{1,0:T(8,128)(2,1)S(1)} %get-tuple-element.11.vg, f32[1,512]{1,0:T(1,128)S(1)} %psum.7.sq, bf16[256,2048]{1,0:T(8,128)(2,1)S(1)} %copy-done, bf16[128,2048]{1,0:T(8,128)(2,1)} %collective-permute-done.3.a1, ...), custom_call_target="tpu_custom_call" | custom-call | tf_op jit(solution)/shard_map/project/pallas_call | solution.py:398
  81.1 31.2 %all_to_all.10 = bf16[16,256,128]{2,1,0:T(8,128)(2,1)S(1)} all-to-all(bf16[16,256,128]{2,1,0:T(8,128)(2,1)S(1)} %project.1), channel_id=1, replica_groups=mesh['context'=16,'tensor'=16] {'tensor'}, dimensions={0} | all-to-all | bytes 2097152 | tf_op jit(solution)/shard_map/all_to_all | solution.py:459
  112.4 0.9 reduce
  (27 shorter events, 0.1 us)
Async XLA Ops:
  0.0 29.1 %copy-start.1 = (bf16[2048,256]{1,0:T(8,128)(2,1)S(1)}, bf16[2048,256]{1,0:T(8,128)(2,1)}, u32[]{:S(2)}) copy-start(bf16[2048,256]{1,0:T(8,128)(2,1)} %wz.1) | copy-start | bytes 3145732
  0.0 28.7 %copy-start.13 = (bf16[2048,4]{0,1:T(4,128)(2,1)S(1)}, bf16[2048,4]{0,1:T(4,128)(2,1)}, u32[]{:S(2)}) copy-start(bf16[2048,4]{0,1:T(4,128)(2,1)} %param.22) | copy-start | bytes 49156
  1.2 27.9 %copy-start.4 = (bf16[5,2048]{1,0:T(8,128)(2,1)S(1)}, bf16[5,2048]{1,0:T(8,128)(2,1)}, u32[]{:S(2)}) copy-start(bf16[5,2048]{1,0:T(8,128)(2,1)} %emb.1) | copy-start | bytes 61444
  1.2 17.3 %collective-permute-start.5 = (bf16[128,2048]{1,0:T(8,128)(2,1)S(1)}, bf16[128,2048]{1,0:T(8,128)(2,1)S(1)}, u32[]{:S(2)}, u32[]{:S(2)}) collective-permute-start(bf16[128,2048]{1,0:T(8,128)(2,1)S(1)} %constant_dynamic-slice_fusion), channel_id=1, source_target_pairs={{0,3},{1,2},{2,1},{3,0},{4,7},{5,6},{6,5},{7,4},{8,11},{9,10},{10,... | collective-permute-start | bytes 1572872 | tf_op jit(solution)/shard_map/ppermute | solution.py:418
  4.8 23.1 %collective-permute-start.4 = (bf16[128,2048]{1,0:T(8,128)(2,1)S(1)}, bf16[128,2048]{1,0:T(8,128)(2,1)}, u32[]{:S(2)}, u32[]{:S(2)}) collective-permute-start(bf16[128,2048]{1,0:T(8,128)(2,1)S(1)} %constant_dynamic-slice_fusion), channel_id=1, source_target_pairs={{0,2},{1,3},{2,0},{3,1},{4,6},{5,7},{6,4},{7,5},{8,10},{9,11},{10,... | collective-permute-start | bytes 1572872 | tf_op jit(solution)/shard_map/ppermute | solution.py:418
  4.9 23.8 %collective-permute-start.3 = (bf16[128,2048]{1,0:T(8,128)(2,1)S(1)}, bf16[128,2048]{1,0:T(8,128)(2,1)}, u32[]{:S(2)}, u32[]{:S(2)}) collective-permute-start(bf16[128,2048]{1,0:T(8,128)(2,1)S(1)} %constant_dynamic-slice_fusion), channel_id=1, source_target_pairs={{0,1},{1,0},{2,3},{3,2},{4,5},{5,4},{6,7},{7,6},{8,9},{9,8},{10,11... | collective-permute-start | bytes 1572872 | tf_op jit(solution)/shard_map/ppermute | solution.py:418
  18.5 58.1 %collective-permute-start.8 = (bf16[128,2048]{1,0:T(8,128)(2,1)S(1)}, bf16[128,2048]{1,0:T(8,128)(2,1)}, u32[]{:S(2)}, u32[]{:S(2)}) collective-permute-start(bf16[128,2048]{1,0:T(8,128)(2,1)S(1)} %collective-permute-done.5.a3), channel_id=1, source_target_pairs={{0,16},{16,0},{32,48},{48,32},{64,80},{80,64},{96,112},{112,96},{1... | collective-permute-start | bytes 1572872 | tf_op jit(solution)/shard_map/ppermute | solution.py:418
  27.9 48.8 %collective-permute-start.7 = (bf16[128,2048]{1,0:T(8,128)(2,1)}, bf16[128,2048]{1,0:T(8,128)(2,1)}, u32[]{:S(2)}, u32[]{:S(2)}) collective-permute-start(bf16[128,2048]{1,0:T(8,128)(2,1)} %collective-permute-done.4.a2), channel_id=1, source_target_pairs={{0,16},{16,0},{32,48},{48,32},{64,80},{80,64},{96,112},{112,96},{1... | collective-permute-start | bytes 1572872 | tf_op jit(solution)/shard_map/ppermute | solution.py:418
  28.7 48.0 %collective-permute-start.6 = (bf16[128,2048]{1,0:T(8,128)(2,1)}, bf16[128,2048]{1,0:T(8,128)(2,1)}, u32[]{:S(2)}, u32[]{:S(2)}) collective-permute-start(bf16[128,2048]{1,0:T(8,128)(2,1)} %collective-permute-done.3.a1), channel_id=1, source_target_pairs={{0,16},{16,0},{32,48},{48,32},{64,80},{80,64},{96,112},{112,96},{1... | collective-permute-start | bytes 1572872 | tf_op jit(solution)/shard_map/ppermute | solution.py:418
  28.7 0.7 copy-start.6
  28.7 0.7 copy-start.7
  28.7 0.7 copy-start.9
  28.7 0.7 copy-start.10
  28.7 0.7 copy-start.11
  29.1 0.7 copy-start.5
  29.1 0.7 copy-start.8
  29.8 1.2 %copy-start.2 = (bf16[2048,256]{1,0:T(8,128)(2,1)S(1)}, bf16[2048,256]{1,0:T(8,128)(2,1)}, u32[]{:S(2)}) copy-start(bf16[2048,256]{1,0:T(8,128)(2,1)} %wx.1) | copy-start | bytes 3145732
  31.0 1.2 %copy-start.3 = (bf16[2048,256]{1,0:T(8,128)(2,1)S(1)}, bf16[2048,256]{1,0:T(8,128)(2,1)}, u32[]{:S(2)}) copy-start(bf16[2048,256]{1,0:T(8,128)(2,1)} %wbc.1) | copy-start | bytes 3145732
  32.2 4.3 %copy-start.14 = (s32[1024]{0:T(1024)S(1)}, s32[1024]{0:T(1024)}, u32[]{:S(2)}) copy-start(s32[1024]{0:T(1024)} %param.15) | copy-start | bytes 12292
  32.2 44.4 %copy-start = (bf16[256,2048]{1,0:T(8,128)(2,1)S(1)}, bf16[256,2048]{1,0:T(8,128)(2,1)}, u32[]{:S(2)}) copy-start(bf16[256,2048]{1,0:T(8,128)(2,1)} %w_own.1) | copy-start | bytes 3145732
  33.0 10.2 %collective-permute-start.2 = (f32[32,256]{1,0:T(8,128)S(1)}, f32[32,256]{1,0:T(8,128)S(1)}, u32[]{:S(2)}, u32[]{:S(2)}) collective-permute-start(f32[32,256]{1,0:T(8,128)S(1)} %get-tuple-element.9.t0), channel_id=1, source_target_pairs={{0,3},{1,2},{2,1},{3,0},{4,7},{5,6},{6,5},{7,4},{8,11},{9,10},{10,... | collective-permute-start | bytes 98312 | tf_op jit(solution)/shard_map/ppermute | solution.py:418
  37.1 11.7 %all-to-all-start = ((s32[16,8,128]{2,1,0:T(8,128)}), s32[16,8,128]{2,1,0:T(8,128)S(1)}, u32[]{:S(2)}, u32[]{:S(2)}) async-start(s32[16,8,128]{2,1,0:T(8,128)} %broadcast_in_dim.23), calls=%async_computation | async-start | bytes 131072 | tf_op jit(solution)/shard_map/all_to_all | solution.py:453
  43.1 3.9 %collective-permute-start.1 = (f32[32,256]{1,0:T(8,128)S(1)}, f32[32,256]{1,0:T(8,128)S(1)}, u32[]{:S(2)}, u32[]{:S(2)}) collective-permute-start(f32[32,256]{1,0:T(8,128)S(1)} %get-tuple-element.9.t0), channel_id=1, source_target_pairs={{0,2},{1,3},{2,0},{3,1},{4,6},{5,7},{6,4},{7,5},{8,10},{9,11},{10,... | collective-permute-start | bytes 98312 | tf_op jit(solution)/shard_map/ppermute | solution.py:418
  43.2 5.6 %collective-permute-start = (f32[32,256]{1,0:T(8,128)S(1)}, f32[32,256]{1,0:T(8,128)S(1)}, u32[]{:S(2)}, u32[]{:S(2)}) collective-permute-start(f32[32,256]{1,0:T(8,128)S(1)} %get-tuple-element.9.t0), channel_id=1, source_target_pairs={{0,1},{1,0},{2,3},{3,2},{4,5},{5,4},{6,7},{7,6},{8,9},{9,8},{10,11... | collective-permute-start | bytes 98312 | tf_op jit(solution)/shard_map/ppermute | solution.py:418
  48.8 0.7 copy-start.12

commit v2 on v1

v2 whole, which is shorter than its diff:
```python
import functools

import jax
import jax.numpy as jnp
from jax import lax
from jax.experimental import pallas as pl
from jax.experimental.pallas import tpu as pltpu
from jax.sharding import PartitionSpec as P

f32 = jnp.float32
bf16 = jnp.bfloat16
i32 = jnp.int32
highest = lax.Precision.HIGHEST
epsilon = 1e-05

LANES = 128
SEQ = 16384
ROWS = SEQ // LANES
BLOCK = 256
STATE = 128
HEAD = 64
TOKENS = 5
NONE = 5
LOG2E = 1.4426950408889634
TINY = 2.0**-126
WIDE = 1024
HEADS = WIDE // HEAD
GRAMS = 144
TABLE_ARGS = 12
PIECES = 4

SAME_HEADS = [[0, 1, 2, 3], [4, 5, 6, 7], [8, 9, 10, 11], [12, 13, 14, 15]]
SAME_POSITIONS = [[0, 4, 8, 12], [1, 5, 9, 13], [2, 6, 10, 14], [3, 7, 11, 15]]

TN = (((0,), (0,)), ((), ()))
NT = (((1,), (1,)), ((), ()))


def iota(shape, dim):
    return lax.broadcasted_iota(i32, shape, dim)


def silu(v):
    half = 0.5 * v
    return half + half * jnp.tanh(half)


def split(x, terms=3):
    parts = []
    for _ in range(terms):
        part = x.astype(bf16)
        parts.append(part)
        x = x - part.astype(f32)
    return parts


def table_kernel(parity, w_out, *refs):
    given = refs[:TABLE_ARGS]
    tab, cbc, share, rows = refs[TABLE_ARGS : TABLE_ARGS + 4]
    held = refs[TABLE_ARGS + 4 : -2]
    arrived, shared = refs[-2:]
    half = share.shape[0]
    part = w_out.at[pl.ds(pl.multiple_of(parity[0] * half, half), half), :]
    copies = []
    for source, target in zip(given, held):
        count = PIECES if source.shape[0] > 1024 else 1
        size = source.shape[0] // count
        for n in range(count):
            span = pl.ds(n * size, size)
            one = (source, target) if count == 1 else (source.at[span, :], target.at[span, :])
            copies.append(pltpu.make_async_copy(*one, arrived.at[len(copies)]))
    for copy in copies:
        copy.start()
    kept = pltpu.make_async_copy(part, share, shared)
    kept.start()
    for copy in copies:
        copy.wait()
    emb, gain, wz, wx, wbc, wdt, bias, alog, dskip, convx, convbc, ggain = held
    rows[...] = jnp.zeros_like(rows)
    rows[0:TOKENS, :] = emb[...].astype(f32)
    e = rows[...]
    normed = (
        e * lax.rsqrt(jnp.mean(e * e, axis=-1, keepdims=True) + epsilon) * gain[...]
    ).astype(bf16)

    def project(w):
        return jnp.dot(normed, w[...], preferred_element_type=f32)

    z = project(wz).astype(bf16).astype(f32)
    xs = project(wx).astype(bf16).astype(f32)
    bc = project(wbc).astype(bf16).astype(f32)
    raw = lax.dot_general(normed, wdt[...], NT, preferred_element_type=f32) + bias[...]
    dt = jnp.maximum(raw, 0.0) + jnp.log1p(jnp.exp(-jnp.abs(raw)))
    width = z.shape[1]

    def spread(v):
        lane = iota((v.shape[0], width), 1)
        out = jnp.broadcast_to(v[:, 0:1], lane.shape)
        for h in range(1, v.shape[1]):
            out = jnp.where(lane >= h * HEAD, v[:, h : h + 1], out)
        return out

    row = iota((8, width), 0)
    own = jnp.where(row == 6, spread(dskip[...]), spread(jnp.exp(alog[...])))
    own = jnp.where(row == 5, ggain[...], own)
    tab[0:8, :] = jnp.where(row < TOKENS, silu(z), own)
    tab[8:16, :] = xs
    tab[16:24, :] = jnp.zeros((8, width), f32)
    tab[16:20, :] = convx[...]
    tab[24:32, :] = jnp.where(row < TOKENS, spread(dt), 0.0)
    for k in range(4):
        cbc[8 * k : 8 * k + 8, :] = convbc[k : k + 1, :] * bc
    kept.wait()


def prepare_kernel(
    place, comp, ids_ref, grams, side_tok, count, hot_taps, own_rows, older
):
    r0 = place[0]
    ids = ids_ref[...]
    row = iota((ROWS, LANES), 0)
    lane = iota((ROWS, LANES), 1)
    at = row * LANES + lane
    flip = jnp.zeros_like(ids)
    for k in range(TOKENS):
        flip = jnp.where(ids == k, comp[k], flip)

    def before(x):
        y = pltpu.roll(x, 1, 1)
        y = jnp.where(lane == 0, pltpu.roll(y, 1, 0), y)
        return jnp.where(at == 0, NONE, y)

    def after(x):
        y = pltpu.roll(x, LANES - 1, 1)
        y = jnp.where(lane == LANES - 1, pltpu.roll(y, ROWS - 1, 0), y)
        return jnp.where(at == SEQ - 1, NONE, y)

    fs = [ids]
    rs = [flip]
    for k in range(3):
        fs.append(before(fs[-1]))
        rs.append(after(rs[-1]))
    g_f = 25 * fs[3] + 5 * fs[2] + fs[1]
    g_r = 25 * rs[3] + 5 * rs[2] + rs[1]
    for k in range(3):
        g_f = jnp.where(at == k, 125 + k, g_f)
        g_r = jnp.where(at == SEQ - 1 - k, 125 if k == 0 else 127 + k, g_r)
    ahead = row < r0
    tok = jnp.where(ahead, ids, flip)
    tok = jnp.where(ahead | (row > r0 + 1), tok, -1)
    grams[...] = jnp.where(ahead, g_f, g_r).astype(f32)
    side_tok[...] = tok.astype(f32)

    hot = [jnp.where(tok == k, 1.0, 0.0) for k in range(TOKENS)]
    hots = jnp.concatenate(hot, axis=0).astype(bf16)
    strict = jnp.where(row < lane, 1.0, 0.0).astype(bf16)
    prior = jnp.dot(hots, strict, preferred_element_type=f32)
    total = jnp.dot(hots, jnp.ones((LANES, LANES), bf16), preferred_element_type=f32)
    between = ((row < lane) & (lane < r0)) | ((lane > r0 + 1) & (lane < row))
    between = jnp.where(between, 1.0, 0.0).astype(bf16)
    for k in range(TOKENS):
        part = slice(k * ROWS, (k + 1) * ROWS)
        far = jnp.dot(between, total[part].astype(bf16), preferred_element_type=f32)
        near = jnp.where(ahead, total[part] - prior[part] - hot[k], prior[part])
        count[k] = near + far

    g = iota((GRAMS, LANES), 0)
    col = iota((GRAMS, LANES), 1)
    d0 = sum(jnp.where(g >= 25 * m, 1, 0) for m in range(1, TOKENS))
    rest = g - 25 * d0
    d1 = sum(jnp.where(rest >= 5 * m, 1, 0) for m in range(1, TOKENS))
    d2 = rest - 5 * d1
    plain = g < 125
    d0 = jnp.where(plain, d0, NONE)
    d1 = jnp.where(plain, d1, NONE)
    d2 = jnp.where(plain, d2, NONE)
    d1 = jnp.where(g == 127, ids[0:1, 0:1], d1)
    d2 = jnp.where(g == 126, ids[0:1, 0:1], d2)
    d2 = jnp.where(g == 127, ids[0:1, 1:2], d2)
    d1 = jnp.where(g == 129, flip[ROWS - 1 :, LANES - 1 :], d1)
    d2 = jnp.where(g == 128, flip[ROWS - 1 :, LANES - 1 :], d2)
    d2 = jnp.where(g == 129, flip[ROWS - 1 :, LANES - 2 : LANES - 1], d2)
    tap = (col >> 3) % 3
    digit = jnp.where(tap == 0, d0, jnp.where(tap == 1, d1, d2))
    older[...] = jnp.where((digit == (col & 7)) & (col < 72), 1.0, 0.0).astype(bf16)

    place_row = iota((32, BLOCK), 0)
    lane_b = iota((BLOCK, BLOCK), 1)
    row_b = iota((BLOCK, BLOCK), 0)

    def own(x):
        first = jnp.sum(jnp.where(row == r0, x, 0), axis=0, keepdims=True)
        second = jnp.sum(jnp.where(row == r0 + 1, x, 0), axis=0, keepdims=True)
        return jnp.concatenate([first, second], axis=1)

    for s, values in enumerate((fs, rs)):
        digit = own(values[0])
        for k in range(3):
            digit = jnp.where(place_row < 8 * (3 - k), own(values[k + 1]), digit)
        hot_own = jnp.where(digit == (place_row & 7), 1.0, 0.0)
        now = hot_own[24:32]
        inclusive = (row_b <= lane_b) if s == 0 else (row_b >= lane_b)
        inclusive = jnp.where(inclusive, 1.0, 0.0).astype(bf16)
        counts = jnp.dot(now.astype(bf16), inclusive, preferred_element_type=f32)
        own_rows[16 * s : 16 * s + 8, :] = counts
        own_rows[16 * s + 8 : 16 * s + 16, :] = now
        hot_taps[s * BLOCK : (s + 1) * BLOCK, :] = jnp.concatenate(
            [hot_own] * 2 + [now] * 2 + [counts] * 3 + [jnp.zeros((24, BLOCK), f32)], axis=0
        ).T.astype(bf16)


def block_kernel(
    place, grams, side_tok, count, hot_taps, own_rows, older, t0, t1, t2, t3, cbc, vg, sq
):
    chunk = place[0] // 8
    r0 = place[0]
    tab = jnp.concatenate([t0[...], t1[...], t2[...], t3[...]], axis=1)
    dt_tab = tab[24:32]
    rate_tab = tab[7:8] * dt_tab * LOG2E
    log_tab = jnp.log2(jnp.maximum(dt_tab, TINY))
    pick = jnp.where(iota((HEADS, WIDE), 1) == HEAD * iota((HEADS, WIDE), 0), 1.0, 0.0).astype(bf16)

    def stack(*parts):
        return jnp.concatenate([part.astype(f32) for part in parts], axis=0).astype(bf16)

    spare = jnp.zeros((8, WIDE), f32)
    both_tab = stack(*split(rate_tab), *split(log_tab), spare, spare)
    both = lax.dot_general(pick, both_tab, NT, preferred_element_type=f32)
    rate = both[:, 0:8] + both[:, 8:16] + both[:, 16:24]
    log_dt = both[:, 24:32] + both[:, 32:40] + both[:, 40:48]
    both_t = lax.dot_general(both_tab, pick, NT, preferred_element_type=f32)
    rate_t = both_t[0:8] + both_t[8:16] + both_t[16:24]
    columns = [jnp.broadcast_to(-rate[:, k : k + 1], (HEADS, BLOCK)) for k in range(TOKENS)]

    def pair(ref, r):
        return jnp.concatenate([ref[pl.ds(r, 1), :], ref[pl.ds(r + 1, 1), :]], axis=1)

    nothing = jnp.zeros((HEADS, BLOCK), bf16)

    def weigh(r):
        token = jnp.broadcast_to(pair(side_tok, r), (HEADS, BLOCK)).astype(bf16)
        exponent = columns[0] * pair(count.at[0], r)
        for k in range(1, TOKENS):
            exponent = exponent + columns[k] * pair(count.at[k], r)
        weight = jnp.exp2(exponent)
        return token, weight

    def by_token(token, weight):
        return [jnp.where(token == k, weight, nothing) for k in range(TOKENS)]

    gram_row = iota((GRAMS, BLOCK), 0).astype(bf16)
    one = jnp.ones((GRAMS, BLOCK), bf16)
    none = jnp.zeros((GRAMS, BLOCK), bf16)

    def window(r):
        kind = jnp.broadcast_to(pair(grams, r), (GRAMS, BLOCK)).astype(bf16)
        return jnp.where(gram_row == kind, one, none)

    def tally(seen, weights):
        return lax.dot_general(
            jnp.concatenate(seen, axis=1),
            jnp.concatenate(weights, axis=1),
            NT,
            preferred_element_type=f32,
        )

    sides = [jnp.zeros((GRAMS, TOKENS * HEADS), f32) for _ in range(2)]
    for step in range(ROWS // 8):
        weights = []
        for j in range(4):
            token, weight = weigh(8 * step + 2 * j)
            weights.append(jnp.concatenate(by_token(token, weight.astype(bf16)), axis=0))
        part = tally([window(8 * step + 2 * j) for j in range(4)], weights)
        sides[0] = sides[0] + part * jnp.where(step < chunk, 1.0, 0.0)
        sides[1] = sides[1] + part * jnp.where(step > chunk, 1.0, 0.0)
    weights = []
    for j in range(4):
        r = pl.multiple_of(8 * chunk, 8) + 2 * j
        token, weight = weigh(r)
        first = jnp.where(r < r0, 1.0, 0.0)
        forward = by_token(token, (weight * first).astype(bf16))
        reverse = by_token(token, (weight * (1.0 - first)).astype(bf16))
        weights.append(jnp.concatenate(forward + reverse, axis=0))
    part = tally([window(pl.multiple_of(8 * chunk, 8) + 2 * j) for j in range(4)], weights)
    hist = (part + jnp.concatenate(sides, axis=1)).astype(bf16)

    taps = jnp.concatenate([tab[16 + k : 17 + k] * tab[8:16] for k in range(4)], axis=0)
    bc_taps = cbc[...]
    kinds = older[...]
    rest = jnp.zeros((56, WIDE), f32)
    x_older = jnp.dot(kinds, stack(*split(taps[0:24]), rest), preferred_element_type=f32)
    b_older = jnp.dot(
        kinds, stack(*split(bc_taps[0:24, :STATE]), rest[:, :STATE]), preferred_element_type=f32
    )
    lift = iota((HEADS, WIDE), 1) - HEAD * iota((HEADS, WIDE), 0)
    lift = jnp.where((lift >= 0) & (lift < HEAD), 1.0, 0.0).astype(bf16)
    feeds = []
    moved = [[], []]
    for k in range(TOKENS):
        feeds.append(silu(b_older + bc_taps[24 + k : 25 + k, :STATE]).astype(bf16))
        act = (silu(x_older + taps[24 + k : 25 + k]) * dt_tab[k : k + 1]).astype(bf16)
        for s in range(2):
            start = (s * TOKENS + k) * HEADS
            part = jnp.dot(hist[:, start : start + HEADS], lift, preferred_element_type=f32)
            moved[s].append(act * part.astype(bf16))
    feeds = jnp.concatenate(feeds, axis=0)
    entering = [
        lax.dot_general(
            feeds, jnp.concatenate(moved[s], axis=0), TN, preferred_element_type=f32
        ).astype(bf16)
        for s in range(2)
    ]

    def look(hots, table):
        return jnp.dot(hots, table, preferred_element_type=f32)

    def blank(count, width):
        return jnp.zeros((count, width), f32)

    gate_tab = jnp.where(iota((8, WIDE), 0) < TOKENS, tab[0:8], 0.0)
    taps2 = stack(*split(taps, 2), blank(64, WIDE))
    bc2 = stack(*split(bc_taps, 2), blank(64, 2 * STATE))
    gate2 = stack(blank(64, WIDE), *split(gate_tab, 2), blank(48, WIDE))
    rate3 = stack(blank(80, HEADS), *split(rate_t), blank(24, HEADS))
    cap = jnp.broadcast_to(jnp.max(log_dt[:, :TOKENS], axis=1, keepdims=True), (HEADS, BLOCK))
    row_tab = jnp.concatenate([rate, log_dt], axis=1)
    lane_h = iota((LANES, LANES), 1)
    row_h = iota((LANES, LANES), 0)
    low = iota((BLOCK, LANES), 1) < HEAD
    zero = jnp.zeros((BLOCK, LANES), bf16)
    for s in range(2):
        rows = slice(s * BLOCK, (s + 1) * BLOCK)
        hot = hot_taps[rows, :]
        bc_act = silu(look(hot, bc2))
        feed = bc_act[:, :STATE].astype(bf16)
        read = bc_act[:, STATE:].astype(bf16)
        scores = lax.dot_general(read, feed, NT, preferred_element_type=f32)
        cum_row = -jnp.dot(
            row_tab, own_rows[16 * s : 16 * s + 16, :], precision=highest, preferred_element_type=f32
        )
        cum_col = -look(hot, rate3)
        decay = jnp.exp2(cum_col)
        near = (lane_h <= row_h) if s == 0 else (lane_h >= row_h)
        halves = ((0, 0, 1), (1, 0, 2)) if s == 0 else ((0, 0, 2), (1, 1, 1))
        masked = []
        for half, key, keys in halves:
            t = slice(half * LANES, (half + 1) * LANES)
            pieces = []
            for j in range(key, key + keys):
                piece = scores[t, j * LANES : (j + 1) * LANES]
                pieces.append(jnp.where(near, piece, 0.0) if j == half else piece)
            masked.append(jnp.concatenate(pieces, axis=1).astype(bf16))
        squares = [jnp.zeros((LANES, LANES), f32) for _ in range(2)]
        for p in range(HEADS // 2):
            chans = slice(p * LANES, (p + 1) * LANES)
            if p % 2 == 0:
                wide = slice(p * LANES, (p + 2) * LANES)
                xs_wide = silu(look(hot, taps2[:, wide]))
                gate_wide = look(hot, gate2[:, wide])
                far_wide = look(read, entering[s][:, wide])
            part = slice((p % 2) * LANES, (p % 2 + 1) * LANES)
            xs = xs_wide[:, part]
            gate = gate_wide[:, part]
            far = far_wide[:, part] * jnp.where(
                low, decay[:, 2 * p : 2 * p + 1], decay[:, 2 * p + 1 : 2 * p + 2]
            )
            fed = xs.astype(bf16)
            lows = jnp.where(low, fed, zero)
            highs = jnp.where(low, zero, fed)
            for (half, key, keys), score in zip(halves, masked):
                t = slice(half * LANES, (half + 1) * LANES)
                source = slice(key * LANES, (key + keys) * LANES)
                parts = []
                for h in (2 * p, 2 * p + 1):
                    differ = cum_col[t, h : h + 1] - cum_row[h : h + 1, source]
                    differ = jnp.minimum(differ, cap[h : h + 1, source])
                    parts.append(jnp.exp2(differ).astype(bf16) * score)
                y = jnp.dot(
                    jnp.concatenate(parts, axis=1),
                    jnp.concatenate([lows[source], highs[source]], axis=0),
                    preferred_element_type=f32,
                )
                v = (y + far[t] + tab[6:7, chans] * xs[t]) * gate[t]
                squares[half] = squares[half] + v * v
                out_rows = slice(s * BLOCK + half * LANES, s * BLOCK + (half + 1) * LANES)
                vg[out_rows, chans] = (v * tab[5:6, chans]).astype(bf16)
        summed = lax.dot_general(
            jnp.ones((8, LANES), f32),
            jnp.concatenate(squares, axis=0),
            NT,
            precision=highest,
            preferred_element_type=f32,
        )
        sq[:, rows] = summed[0:1]


def out_kernel(parity, vg, sq, w_own, a1, a2, a3, b1, b2, b3, out, g_all):
    first = iota((8, 2 * BLOCK), 0) == 0
    inverse = jnp.where(first, lax.rsqrt(sq[...] / 4096.0 + epsilon), 0.0)
    inverse = lax.dot_general(
        inverse, jnp.ones((8, LANES), f32), TN, precision=highest, preferred_element_type=f32
    )
    half = LANES
    for p in range(WIDE // half):
        chans = slice(p * half, (p + 1) * half)
        strands = [
            (vg[s * BLOCK : (s + 1) * BLOCK, chans].astype(f32) * inverse[s * BLOCK : (s + 1) * BLOCK])
            .astype(bf16)
            .astype(f32)
            for s in range(2)
        ]
        g = (strands[0] + strands[1]).astype(bf16)
        if p < 2:
            g_all[:, chans] = g
        else:
            at = (p - p % 2 + (parity[0] ^ (p % 2))) * half
            g_all[:, pl.ds(pl.multiple_of(at, half), half)] = g
    g = g_all[...]
    tile = 2 * LANES
    for n in range(out.shape[0] // 2):
        cols = slice(n * tile, (n + 1) * tile)
        weights = [w_own[:, cols]]
        for a, b in ((a1, b1), (a2, b2), (a3, b3)):
            weights.append(a[:, cols])
            weights.append(b[:, cols])
        result = jnp.dot(
            g, jnp.concatenate(weights, axis=0), preferred_element_type=f32
        ).astype(bf16)
        out[2 * n] = result[:, :LANES]
        out[2 * n + 1] = result[:, LANES:]


def build_tables(
    parity, w_out, embedding, norm_gain, w_z, w_x, w_bc, w_dt, dt_bias, a_log, d_skip, conv_x, conv_bc, gate_gain
):
    width = w_z.shape[1]
    given = (
        embedding,
        norm_gain[None],
        w_z,
        w_x,
        w_bc,
        w_dt.T,
        dt_bias[None],
        a_log[None],
        d_skip[None],
        conv_x,
        conv_bc,
        gate_gain[None],
    )
    return pl.pallas_call(
        table_kernel,
        in_specs=[pl.BlockSpec(memory_space=pltpu.SMEM)]
        + [pl.BlockSpec(memory_space=pltpu.HBM)] * (TABLE_ARGS + 1),
        out_specs=(
            pl.BlockSpec(memory_space=pltpu.VMEM),
            pl.BlockSpec(memory_space=pltpu.VMEM),
            pl.BlockSpec(memory_space=pltpu.VMEM),
        ),
        out_shape=(
            jax.ShapeDtypeStruct((32, width), f32),
            jax.ShapeDtypeStruct((32, w_bc.shape[1]), f32),
            jax.ShapeDtypeStruct((w_out.shape[0] // 2, w_out.shape[1]), w_out.dtype),
        ),
        scratch_shapes=[pltpu.VMEM((8, embedding.shape[1]), f32)]
        + [pltpu.VMEM(x.shape, x.dtype) for x in given]
        + [pltpu.SemaphoreType.DMA((TABLE_ARGS + 3 * (PIECES - 1),)), pltpu.SemaphoreType.DMA(())],
        compiler_params=pltpu.CompilerParams(vmem_limit_bytes=60 * 2**20),
        name="tables",
    )(parity, w_out, *given)


def prepare(place, complement, ids):
    smem = pl.BlockSpec(memory_space=pltpu.SMEM)
    vmem = pl.BlockSpec(memory_space=pltpu.VMEM)
    shape = jax.ShapeDtypeStruct
    return pl.pallas_call(
        prepare_kernel,
        in_specs=[smem, smem, vmem],
        out_specs=(vmem,) * 6,
        out_shape=(
            shape((ROWS, LANES), f32),
            shape((ROWS, LANES), f32),
            shape((TOKENS, ROWS, LANES), f32),
            shape((2 * BLOCK, LANES), bf16),
            shape((32, BLOCK), f32),
            shape((GRAMS, LANES), bf16),
        ),
        compiler_params=pltpu.CompilerParams(vmem_limit_bytes=32 * 2**20),
        name="prepare",
    )(place, complement, ids)


def run_block(place, prepared, tabs, cbc):
    smem = pl.BlockSpec(memory_space=pltpu.SMEM)
    vmem = pl.BlockSpec(memory_space=pltpu.VMEM)
    return pl.pallas_call(
        block_kernel,
        in_specs=[smem] + [vmem] * 11,
        out_specs=(vmem, vmem),
        out_shape=(
            jax.ShapeDtypeStruct((2 * BLOCK, WIDE), bf16),
            jax.ShapeDtypeStruct((1, 2 * BLOCK), f32),
        ),
        compiler_params=pltpu.CompilerParams(vmem_limit_bytes=48 * 2**20),
        cost_estimate=pl.CostEstimate(
            flops=40 * 10**9, bytes_accessed=100 * 2**20, transcendentals=10**7
        ),
        name="block",
    )(place, *prepared, *tabs, cbc)


def run_out(parity, vg, sq, w_own, mine, theirs):
    features = w_own.shape[1]
    smem = pl.BlockSpec(memory_space=pltpu.SMEM)
    vmem = pl.BlockSpec(memory_space=pltpu.VMEM)
    return pl.pallas_call(
        out_kernel,
        in_specs=[smem] + [vmem] * 9,
        out_specs=vmem,
        out_shape=jax.ShapeDtypeStruct((features // LANES, BLOCK, LANES), bf16),
        scratch_shapes=[pltpu.VMEM((BLOCK, WIDE), bf16)],
        compiler_params=pltpu.CompilerParams(vmem_limit_bytes=40 * 2**20),
        name="project",
    )(parity, vg, sq, w_own, *mine, *theirs)


def swap(x, axis, distance):
    count = lax.axis_size(axis)
    return lax.ppermute(x, axis, [(i, i ^ distance) for i in range(count)])


def local(
    ids,
    complement,
    embedding,
    norm_gain,
    w_z,
    w_x,
    w_bc,
    w_dt,
    dt_bias,
    a_log,
    conv_x,
    conv_bc,
    d_skip,
    gate_gain,
    w_out,
):
    context = lax.axis_index("context").astype(i32)
    tensor = lax.axis_index("tensor").astype(i32)
    parity = context % 2
    count = lax.axis_size("context")
    spread = jnp.broadcast_to(ids.reshape(1, -1, LANES), (count, ids.shape[0] // LANES, LANES))
    everyone = lax.all_to_all(spread, "context", 0, 0, tiled=True).reshape(ROWS, LANES)
    place = (context * (ids.shape[0] // LANES) + (tensor % 4) * (BLOCK // LANES)).reshape(1)
    tab, cbc, share = build_tables(
        parity.reshape(1), w_out, embedding, norm_gain, w_z, w_x, w_bc, w_dt, dt_bias, a_log, d_skip, conv_x, conv_bc, gate_gain
    )
    tab, everyone, share = lax.optimization_barrier((tab, everyone, share))
    tabs = [tab] + [swap(tab, "tensor", d) for d in (1, 2, 3)]
    everyone, tabs[1] = lax.optimization_barrier((everyone, tabs[1]))
    prepared = prepare(place, complement, everyone)
    mine = [swap(share, "tensor", d) for d in (1, 2, 3)]

    vg, sq = run_block(place, prepared, tabs, cbc)
    sq = lax.psum(sq, "tensor", axis_index_groups=SAME_POSITIONS)
    sq, *mine = lax.optimization_barrier((sq, *mine))
    theirs = [swap(x, "context", 1) for x in mine]
    terms = run_out(parity.reshape(1), vg, sq, w_out, mine, theirs)
    arrived = lax.all_to_all(terms, "tensor", 0, 0, tiled=True)
    summed = jnp.sum(arrived.astype(f32).reshape(4, 4, BLOCK, LANES), axis=0)
    return summed.reshape(4 * BLOCK, LANES).astype(bf16)


def solution(mesh):
    placed = (
        P("context"),
        P(),
        P(),
        P(),
        P(None, "tensor"),
        P(None, "tensor"),
        P(),
        P(None, "tensor"),
        P("tensor"),
        P("tensor"),
        P(None, "tensor"),
        P(),
        P("tensor"),
        P("tensor"),
        P("tensor", None),
    )
    return jax.shard_map(
        local, mesh=mesh, in_specs=placed, out_specs=P("context", "tensor"), check_vma=False
    )
```

time: 114 us -> 96.1 us (0.84)
  waiting for transfers between devices: 26.4 us -> 4.04 us
  blocking collectives: 46 us -> 56.5 us
  local copies, waits for them, and re-layouts: 5.93 us -> 1.34 us
  Pallas kernels: 17.7 us -> 16.1 us
    ppermute x9, waiting for transfers between devices: 26.4 us -> 2.81 us  [swap(): return lax.ppermute(x, axis, [(i, i ^ distance) for i in range(count)])]
    psum x1, blocking collectives: 14.8 us -> 20.5 us  [local(): sq = lax.psum(sq, 'tensor', axis_index_groups=SAME_POSITIONS)]
    all_to_all x1, blocking collectives: 31.2 us -> 36 us  [local(): arrived = lax.all_to_all(terms, 'tensor', 0, 0, tiled=True)]
    unnamed x31 -> x8, local copies, waits for them, and re-layouts: 4.12 us -> 0.02 us
    pallas_call x3 -> x4, Pallas kernels: 17.7 us -> 16.1 us  [the longest x1 7.86 us: run_block(): pl.pallas_call(block_kernel, in_specs=[smem] + [vmem] * 11, out_specs=(vm...]
    all_to_all x1, waiting for transfers between devices: 0.01 us -> 1.23 us  [local(): lax.all_to_all(spread, 'context', 0, 0, tiled=True).reshape(ROWS, LANES)]
    dynamic_slice x1 -> x0, local copies, waits for them, and re-layouts: 1.18 us -> none  [local(): share = lax.dynamic_slice_in_dim(w_out, parity * half, half, 0)]
  transfers between devices with their start and end apart: 10 -> 10, of which waited for: 5 -> 4; matrix products, arithmetic and copies ran while one was open for 1% -> 0% of each run, Pallas kernels for 12% -> 13%
where the time goes in v2:
time: 96.1 us; the launch traced here: 95.8 us
  blocking collectives  56.5 us (59%)
  starting transfers between devices  16.8 us (17%)
  Pallas kernels  16.1 us (17%)
  waiting for transfers between devices  4.04 us (4%)
  local copies, waits for them, and re-layouts  1.34 us (1%)
    all_to_all x1, blocking collectives, local(): arrived = lax.all_to_all(terms, 'tensor', 0, 0, tiled=True)  36 us
    psum x1, blocking collectives, local(): sq = lax.psum(sq, 'tensor', axis_index_groups=SAME_POSITIONS)  20.5 us
    ppermute x9, starting transfers between devices, swap(): return lax.ppermute(x, axis, [(i, i ^ distance) for i in range(count)])  10.9 us
    pallas_call x1, Pallas kernels, run_block(): pl.pallas_call(block_kernel, in_specs=[smem] + [vmem] * 11, out_specs=(vm...  7.86 us
    all_to_all x1, starting transfers between devices, local(): lax.all_to_all(spread, 'context', 0, 0, tiled=True).reshape(ROWS, LANES)  5.95 us
    pallas_call x1, Pallas kernels, build_tables(): pl.pallas_call(table_kernel, in_specs=[pl.BlockSpec(memory_space=pltpu.SM...  3.6 us
    pallas_call x1, Pallas kernels, run_out(): pl.pallas_call(out_kernel, in_specs=[smem] + [vmem] * 9, out_specs=vmem,...  3.41 us
    ppermute x9, waiting for transfers between devices, swap(): return lax.ppermute(x, axis, [(i, i ^ distance) for i in range(count)])  2.81 us
  transfers between devices with their start and end apart: 10, of which 4 were waited for; matrix products, arithmetic and copies ran while one was open for 0% of the time, Pallas kernels for 13%

profile of v2, /device:TPU:2, one launch (start us, length us, event | category | flops | bytes accessed | tf_op | source)
XLA Modules:
  0.0 95.8 jit_solution(17139688414890961481)
XLA Ops:
  0.0 1.3 %broadcast_in_dim.28 = s32[16,8,128]{2,1,0:T(8,128)} broadcast(s32[8,128]{1,0:T(8,128)} %bitcast.16), dimensions={1,2} | broadcast | bytes 69632 | tf_op jit(solution)/shard_map/broadcast_in_dim | solution.py:554
  1.3 5.9 %all-to-all-start = ((s32[16,8,128]{2,1,0:T(8,128)}), s32[16,8,128]{2,1,0:T(8,128)S(1)}, u32[]{:S(2)}, u32[]{:S(2)}) async-start(s32[16,8,128]{2,1,0:T(8,128)} %broadcast_in_dim.28), calls=%async_computation | async-start | bytes 131072 | tf_op jit(solution)/shard_map/all_to_all | solution.py:555
  7.3 3.6 %tables.1 = (f32[32,256]{1,0:T(8,128)}, f32[32,256]{1,0:T(8,128)}, bf16[128,2048]{1,0:T(8,128)(2,1)}) custom-call(s32[1]{0:T(128)} %bitcast.parity, bf16[256,2048]{1,0:T(8,128)(2,1)} %w_own.1, bf16[5,2048]{1,0:T(8,128)(2,1)} %refs_0_.1, f32[1,2048]{1,0:T(1,128)} %bitcast.15, bf16[2048,256]{1,0:T(8,128)(2,1)} %refs_2_.1, bf16[2048,256]{1,0:T(8,128)(2,1)} %refs_3_.1, ...), custom_call_target="tpu_custom_call" | custom-call | tf_op jit(solution)/shard_map/tables/pallas_call | solution.py:451
  10.9 1.2 %all-to-all-done = s32[16,8,128]{2,1,0:T(8,128)S(1)} async-done(((s32[16,8,128]{2,1,0:T(8,128)}), s32[16,8,128]{2,1,0:T(8,128)S(1)}, u32[]{:S(2)}, u32[]{:S(2)}) %all-to-all-start) | async-done | bytes 65568 | tf_op jit(solution)/shard_map/all_to_all | solution.py:555
  12.1 2.1 %collective-permute-start = (f32[32,256]{1,0:T(8,128)}, f32[32,256]{1,0:T(8,128)S(1)}, u32[]{:S(2)}, u32[]{:S(2)}) collective-permute-start(f32[32,256]{1,0:T(8,128)} %get-tuple-element.28.t0), channel_id=1, source_target_pairs={{0,1},{1,0},{2,3},{3,2},{4,5},{5,4},{6,7},{7,6},{8,9},{9,8},{10,11... | collective-permute-start | bytes 98312 | tf_op jit(solution)/shard_map/ppermute | solution.py:530
  14.2 2.8 %collective-permute-start.2 = (f32[32,256]{1,0:T(8,128)}, f32[32,256]{1,0:T(8,128)S(1)}, u32[]{:S(2)}, u32[]{:S(2)}) collective-permute-start(f32[32,256]{1,0:T(8,128)} %get-tuple-element.28.t0), channel_id=1, source_target_pairs={{0,3},{1,2},{2,1},{3,0},{4,7},{5,6},{6,5},{7,4},{8,11},{9,10},{10,... | collective-permute-start | bytes 98312 | tf_op jit(solution)/shard_map/ppermute | solution.py:530
  17.0 0.1 collective-permute-start.1
  17.1 3.5 %collective-permute-start.5 = (bf16[128,2048]{1,0:T(8,128)(2,1)}, bf16[128,2048]{1,0:T(8,128)(2,1)S(1)}, u32[]{:S(2)}, u32[]{:S(2)}) collective-permute-start(bf16[128,2048]{1,0:T(8,128)(2,1)} %get-tuple-element.40), channel_id=1, source_target_pairs={{0,3},{1,2},{2,1},{3,0},{4,7},{5,6},{6,5},{7,4},{8,11},{9,10},{10,... | collective-permute-start | bytes 1572872 | tf_op jit(solution)/shard_map/ppermute | solution.py:530
  20.6 0.1 collective-permute-start.4
  20.7 0.0 collective-permute-done.t1
  20.7 1.4 %collective-permute-start.3 = (bf16[128,2048]{1,0:T(8,128)(2,1)}, bf16[128,2048]{1,0:T(8,128)(2,1)}, u32[]{:S(2)}, u32[]{:S(2)}) collective-permute-start(bf16[128,2048]{1,0:T(8,128)(2,1)} %get-tuple-element.40), channel_id=1, source_target_pairs={{0,1},{1,0},{2,3},{3,2},{4,5},{5,4},{6,7},{7,6},{8,9},{9,8},{10,11... | collective-permute-start | bytes 1572872 | tf_op jit(solution)/shard_map/ppermute | solution.py:530
  22.1 0.0 copy-done.1
  22.1 1.2 %prepare.1 = (f32[128,128]{1,0:T(8,128)S(1)}, f32[128,128]{1,0:T(8,128)S(1)}, f32[5,128,128]{2,1,0:T(8,128)S(1)}, bf16[512,128]{1,0:T(8,128)(2,1)S(1)}, f32[32,2...) custom-call(s32[1]{0:T(128)} %bitcast.1.place, s32[5]{0:T(128)S(1)} %copy-done.1, s32[128,128]{1,0:T(8,128)S(1)} %bitcast.12), custom_call_target="tpu_custom_call" | custom-call | tf_op jit(solution)/shard_map/prepare/pallas_call | solution.py:477
  23.3 0.0 collective-permute-done.2.t3
  23.3 0.0 collective-permute-done.1.t2
  23.4 0.0 copy-done.2
  23.4 0.0 copy-done.3
  23.4 0.0 copy-start
  23.4 7.9 %block.1 = (bf16[512,1024]{1,0:T(8,128)(2,1)S(1)}, f32[1,512]{1,0:T(1,128)S(1)}) custom-call(s32[1]{0:T(128)} %bitcast.1.place, f32[128,128]{1,0:T(8,128)S(1)} %get-tuple-element.30.grams, f32[128,128]{1,0:T(8,128)S(1)} %get-tuple-element.31.side_tok, f32[5,128,128]{2,1,0:T(8,128)S(1)} %get-tuple-element.32.count, ...), custom_call_target="tpu_custom_call" | custom-call | flops 40000000000 | bytes 104857600 | tf_op jit(solution)/shard_map/block/pallas_call | solution.py:497
  31.2 20.5 %psum.7.sq = f32[1,512]{1,0:T(1,128)S(1)} all-reduce(f32[1,512]{1,0:T(1,128)S(1)} %get-tuple-element.39), channel_id=1, replica_groups={{0,4,8,12},{1,5,9,13},{2,6,10,14},{3,7,11,15},{16,20,24,28},{17,21,25,2..., use_global_device_ids=true, to_apply=%region_0.1 | all-reduce | flops 512 | bytes 4096 | tf_op jit(solution)/shard_map/psum | solution.py:567
  51.8 0.0 collective-permute-done.5.a3
  51.8 0.0 collective-permute-done.4.a2
  51.8 0.0 collective-permute-done.3.a1
  51.8 0.3 collective-permute-start.6
  52.1 0.5 collective-permute-start.7
  52.6 0.1 collective-permute-start.8
  52.7 1.5 %collective-permute-done.6.b1 = bf16[128,2048]{1,0:T(8,128)(2,1)S(1)} collective-permute-done((bf16[128,2048]{1,0:T(8,128)(2,1)}, bf16[128,2048]{1,0:T(8,128)(2,1)S(1)}, u32[]{:S(2)}, u32[]{:S(2)}) %collective-permute-start.6) | collective-permute-done | bytes 524320 | tf_op jit(solution)/shard_map/ppermute | solution.py:530
  54.2 0.5 collective-permute-done.7.b2
  54.7 0.7 collective-permute-done.8.b3
  55.5 3.4 %project.1 = bf16[16,256,128]{2,1,0:T(8,128)(2,1)S(1)} custom-call(s32[1]{0:T(128)} %bitcast.parity, bf16[512,1024]{1,0:T(8,128)(2,1)S(1)} %get-tuple-element.38.vg, f32[1,512]{1,0:T(1,128)S(1)} %psum.7.sq, bf16[256,2048]{1,0:T(8,128)(2,1)S(1)} %copy-done, bf16[128,2048]{1,0:T(8,128)(2,1)} %collective-permute-done.3.a1, ...), custom_call_target="tpu_custom_call" | custom-call | tf_op jit(solution)/shard_map/project/pallas_call | solution.py:517
  58.9 36.0 %all_to_all.10 = bf16[16,256,128]{2,1,0:T(8,128)(2,1)S(1)} all-to-all(bf16[16,256,128]{2,1,0:T(8,128)(2,1)S(1)} %project.1), channel_id=1, replica_groups=mesh['context'=16,'tensor'=16] {'tensor'}, dimensions={0} | all-to-all | bytes 2097152 | tf_op jit(solution)/shard_map/all_to_all | solution.py:571
  94.9 0.9 reduce
  (4 shorter events, 0.0 us)
Async XLA Ops:
  1.3 10.8 %all-to-all-start = ((s32[16,8,128]{2,1,0:T(8,128)}), s32[16,8,128]{2,1,0:T(8,128)S(1)}, u32[]{:S(2)}, u32[]{:S(2)}) async-start(s32[16,8,128]{2,1,0:T(8,128)} %broadcast_in_dim.28), calls=%async_computation | async-start | bytes 131072 | tf_op jit(solution)/shard_map/all_to_all | solution.py:555
  12.1 8.6 %collective-permute-start = (f32[32,256]{1,0:T(8,128)}, f32[32,256]{1,0:T(8,128)S(1)}, u32[]{:S(2)}, u32[]{:S(2)}) collective-permute-start(f32[32,256]{1,0:T(8,128)} %get-tuple-element.28.t0), channel_id=1, source_target_pairs={{0,1},{1,0},{2,3},{3,2},{4,5},{5,4},{6,7},{7,6},{8,9},{9,8},{10,11... | collective-permute-start | bytes 98312 | tf_op jit(solution)/shard_map/ppermute | solution.py:530
  14.2 9.1 %collective-permute-start.2 = (f32[32,256]{1,0:T(8,128)}, f32[32,256]{1,0:T(8,128)S(1)}, u32[]{:S(2)}, u32[]{:S(2)}) collective-permute-start(f32[32,256]{1,0:T(8,128)} %get-tuple-element.28.t0), channel_id=1, source_target_pairs={{0,3},{1,2},{2,1},{3,0},{4,7},{5,6},{6,5},{7,4},{8,11},{9,10},{10,... | collective-permute-start | bytes 98312 | tf_op jit(solution)/shard_map/ppermute | solution.py:530
  17.0 6.4 %collective-permute-start.1 = (f32[32,256]{1,0:T(8,128)}, f32[32,256]{1,0:T(8,128)S(1)}, u32[]{:S(2)}, u32[]{:S(2)}) collective-permute-start(f32[32,256]{1,0:T(8,128)} %get-tuple-element.28.t0), channel_id=1, source_target_pairs={{0,2},{1,3},{2,0},{3,1},{4,6},{5,7},{6,4},{7,5},{8,10},{9,11},{10,... | collective-permute-start | bytes 98312 | tf_op jit(solution)/shard_map/ppermute | solution.py:530
  17.1 5.0 %copy-start.1 = (s32[5]{0:T(128)S(1)}, s32[5]{0:T(128)}, u32[]{:S(2)}) copy-start(s32[5]{0:T(128)} %comp.1) | copy-start | bytes 64
  17.1 34.7 %collective-permute-start.5 = (bf16[128,2048]{1,0:T(8,128)(2,1)}, bf16[128,2048]{1,0:T(8,128)(2,1)S(1)}, u32[]{:S(2)}, u32[]{:S(2)}) collective-permute-start(bf16[128,2048]{1,0:T(8,128)(2,1)} %get-tuple-element.40), channel_id=1, source_target_pairs={{0,3},{1,2},{2,1},{3,0},{4,7},{5,6},{6,5},{7,4},{8,11},{9,10},{10,... | collective-permute-start | bytes 1572872 | tf_op jit(solution)/shard_map/ppermute | solution.py:530
  20.6 31.2 %collective-permute-start.4 = (bf16[128,2048]{1,0:T(8,128)(2,1)}, bf16[128,2048]{1,0:T(8,128)(2,1)S(1)}, u32[]{:S(2)}, u32[]{:S(2)}) collective-permute-start(bf16[128,2048]{1,0:T(8,128)(2,1)} %get-tuple-element.40), channel_id=1, source_target_pairs={{0,2},{1,3},{2,0},{3,1},{4,6},{5,7},{6,4},{7,5},{8,10},{9,11},{10,... | collective-permute-start | bytes 1572872 | tf_op jit(solution)/shard_map/ppermute | solution.py:530
  20.7 31.1 %collective-permute-start.3 = (bf16[128,2048]{1,0:T(8,128)(2,1)}, bf16[128,2048]{1,0:T(8,128)(2,1)}, u32[]{:S(2)}, u32[]{:S(2)}) collective-permute-start(bf16[128,2048]{1,0:T(8,128)(2,1)} %get-tuple-element.40), channel_id=1, source_target_pairs={{0,1},{1,0},{2,3},{3,2},{4,5},{5,4},{6,7},{7,6},{8,9},{9,8},{10,11... | collective-permute-start | bytes 1572872 | tf_op jit(solution)/shard_map/ppermute | solution.py:530
  22.1 1.3 %copy-start.2 = (f32[32,256]{1,0:T(8,128)S(1)}, f32[32,256]{1,0:T(8,128)}, u32[]{:S(2)}) copy-start(f32[32,256]{1,0:T(8,128)} %get-tuple-element.28.t0) | copy-start | bytes 98308
  22.1 1.3 %copy-start.3 = (f32[32,256]{1,0:T(8,128)S(1)}, f32[32,256]{1,0:T(8,128)}, u32[]{:S(2)}) copy-start(f32[32,256]{1,0:T(8,128)} %get-tuple-element.37.cbc) | copy-start | bytes 98308
  23.4 32.1 %copy-start = (bf16[256,2048]{1,0:T(8,128)(2,1)S(1)}, bf16[256,2048]{1,0:T(8,128)(2,1)}, u32[]{:S(2)}) copy-start(bf16[256,2048]{1,0:T(8,128)(2,1)} %w_own.1) | copy-start | bytes 3145732
  51.8 2.4 %collective-permute-start.6 = (bf16[128,2048]{1,0:T(8,128)(2,1)}, bf16[128,2048]{1,0:T(8,128)(2,1)S(1)}, u32[]{:S(2)}, u32[]{:S(2)}) collective-permute-start(bf16[128,2048]{1,0:T(8,128)(2,1)} %collective-permute-done.3.a1), channel_id=1, source_target_pairs={{0,16},{16,0},{32,48},{48,32},{64,80},{80,64},{96,112},{112,96},{1... | collective-permute-start | bytes 1572872 | tf_op jit(solution)/shard_map/ppermute | solution.py:530
  52.1 2.6 %collective-permute-start.7 = (bf16[128,2048]{1,0:T(8,128)(2,1)S(1)}, bf16[128,2048]{1,0:T(8,128)(2,1)S(1)}, u32[]{:S(2)}, u32[]{:S(2)}) collective-permute-start(bf16[128,2048]{1,0:T(8,128)(2,1)S(1)} %collective-permute-done.4.a2), channel_id=1, source_target_pairs={{0,16},{16,0},{32,48},{48,32},{64,80},{80,64},{96,112},{112,96},{1... | collective-permute-start | bytes 1572872 | tf_op jit(solution)/shard_map/ppermute | solution.py:530
  52.6 2.9 %collective-permute-start.8 = (bf16[128,2048]{1,0:T(8,128)(2,1)S(1)}, bf16[128,2048]{1,0:T(8,128)(2,1)S(1)}, u32[]{:S(2)}, u32[]{:S(2)}) collective-permute-start(bf16[128,2048]{1,0:T(8,128)(2,1)S(1)} %collective-permute-done.5.a3), channel_id=1, source_target_pairs={{0,16},{16,0},{32,48},{48,32},{64,80},{80,64},{96,112},{112,96},{1... | collective-permute-start | bytes 1572872 | tf_op jit(solution)/shard_map/ppermute | solution.py:530

commit v3 on v2

--- a/solution.py
+++ b/solution.py
@@ -29,8 +29,12 @@
 TABLE_ARGS = 12
 PIECES = 4
 
-SAME_HEADS = [[0, 1, 2, 3], [4, 5, 6, 7], [8, 9, 10, 11], [12, 13, 14, 15]]
-SAME_POSITIONS = [[0, 4, 8, 12], [1, 5, 9, 13], [2, 6, 10, 14], [3, 7, 11, 15]]
+QUARTERS = [[t for t in range(16) if (t // 2 + 2 * (t % 2) + 3) % 4 == q] for q in range(4)]
+PEERS = (
+    [(t, (t + 2) % 16) for t in range(16)],
+    [(t, (t - 2) % 16) for t in range(16)],
+    [(t, t ^ 1) for t in range(16)],
+)
 
 TN = (((0,), (0,)), ((), ()))
 NT = (((1,), (1,)), ((), ()))
@@ -525,9 +529,13 @@
     )(parity, vg, sq, w_own, *mine, *theirs)
 
 
-def swap(x, axis, distance):
-    count = lax.axis_size(axis)
-    return lax.ppermute(x, axis, [(i, i ^ distance) for i in range(count)])
+def from_peers(x):
+    return [lax.ppermute(x, "tensor", pairs) for pairs in PEERS]
+
+
+def other_core(x):
+    count = lax.axis_size("context")
+    return lax.ppermute(x, "context", [(i, i ^ 1) for i in range(count)])
 
 
 def local(
@@ -553,24 +561,25 @@
     count = lax.axis_size("context")
     spread = jnp.broadcast_to(ids.reshape(1, -1, LANES), (count, ids.shape[0] // LANES, LANES))
     everyone = lax.all_to_all(spread, "context", 0, 0, tiled=True).reshape(ROWS, LANES)
-    place = (context * (ids.shape[0] // LANES) + (tensor % 4) * (BLOCK // LANES)).reshape(1)
+    quarter = (tensor // 2 + 2 * (tensor % 2) + 3) % 4
+    place = (context * (ids.shape[0] // LANES) + quarter * (BLOCK // LANES)).reshape(1)
     tab, cbc, share = build_tables(
         parity.reshape(1), w_out, embedding, norm_gain, w_z, w_x, w_bc, w_dt, dt_bias, a_log, d_skip, conv_x, conv_bc, gate_gain
     )
     tab, everyone, share = lax.optimization_barrier((tab, everyone, share))
-    tabs = [tab] + [swap(tab, "tensor", d) for d in (1, 2, 3)]
+    tabs = [tab] + from_peers(tab)
     everyone, tabs[1] = lax.optimization_barrier((everyone, tabs[1]))
     prepared = prepare(place, complement, everyone)
-    mine = [swap(share, "tensor", d) for d in (1, 2, 3)]
+    mine = from_peers(share)
 
     vg, sq = run_block(place, prepared, tabs, cbc)
-    sq = lax.psum(sq, "tensor", axis_index_groups=SAME_POSITIONS)
-    sq, *mine = lax.optimization_barrier((sq, *mine))
-    theirs = [swap(x, "context", 1) for x in mine]
+    vg, sq, *mine = lax.optimization_barrier((vg, sq, *mine))
+    theirs = [other_core(x) for x in mine]
+    sq = lax.psum(sq, "tensor", axis_index_groups=QUARTERS)
     terms = run_out(parity.reshape(1), vg, sq, w_out, mine, theirs)
     arrived = lax.all_to_all(terms, "tensor", 0, 0, tiled=True)
-    summed = jnp.sum(arrived.astype(f32).reshape(4, 4, BLOCK, LANES), axis=0)
-    return summed.reshape(4 * BLOCK, LANES).astype(bf16)
+    summed = [sum(arrived[t].astype(f32) for t in members) for members in QUARTERS]
+    return jnp.concatenate(summed, axis=0).astype(bf16)
 
 
 def solution(mesh):

time: 96.1 us -> 89.8 us (0.934)
  blocking collectives: 56.5 us -> 46.7 us
  waiting for transfers between devices: 4.04 us -> 6.09 us
  starting transfers between devices: 16.8 us -> 17.9 us
    psum x1, blocking collectives: 20.5 us -> 13.3 us  [local(): sq = lax.psum(sq, 'tensor', axis_index_groups=QUARTERS)]
    all_to_all x1, blocking collectives: 36 us -> 33.4 us  [local(): arrived = lax.all_to_all(terms, 'tensor', 0, 0, tiled=True)]
    ppermute x9, waiting for transfers between devices: 2.81 us -> 4.86 us  [the longest x6 4.85 us: from_peers(): return [lax.ppermute(x, 'tensor', pairs) for pairs in PEERS]]
    ppermute x9, starting transfers between devices: 10.9 us -> 11.9 us  [the longest x6 11.4 us: from_peers(): return [lax.ppermute(x, 'tensor', pairs) for pairs in PEERS]]
  transfers between devices with their start and end apart: 10 -> 10, of which waited for: 4 -> 3; matrix products, arithmetic and copies ran while one was open for 0% -> 0% of each run, Pallas kernels for 13% -> 14%
where the time goes in v3:
time: 89.8 us; the launch traced here: 89.6 us
  blocking collectives  46.7 us (52%)
  starting transfers between devices  17.9 us (20%)
  Pallas kernels  16.6 us (18%)
  waiting for transfers between devices  6.09 us (7%)
  local copies, waits for them, and re-layouts  1.34 us (1%)
    all_to_all x1, blocking collectives, local(): arrived = lax.all_to_all(terms, 'tensor', 0, 0, tiled=True)  33.4 us
    psum x1, blocking collectives, local(): sq = lax.psum(sq, 'tensor', axis_index_groups=QUARTERS)  13.3 us
    ppermute x6, starting transfers between devices, from_peers(): return [lax.ppermute(x, 'tensor', pairs) for pairs in PEERS]  11.4 us
    pallas_call x1, Pallas kernels, run_block(): pl.pallas_call(block_kernel, in_specs=[smem] + [vmem] * 11, out_specs=(vm...  7.87 us
    all_to_all x1, starting transfers between devices, local(): lax.all_to_all(spread, 'context', 0, 0, tiled=True).reshape(ROWS, LANES)  5.95 us
    ppermute x6, waiting for transfers between devices, from_peers(): return [lax.ppermute(x, 'tensor', pairs) for pairs in PEERS]  4.85 us
    pallas_call x1, Pallas kernels, run_out(): pl.pallas_call(out_kernel, in_specs=[smem] + [vmem] * 9, out_specs=vmem,...  3.88 us
    pallas_call x1, Pallas kernels, build_tables(): pl.pallas_call(table_kernel, in_specs=[pl.BlockSpec(memory_space=pltpu.SM...  3.6 us
  transfers between devices with their start and end apart: 10, of which 3 were waited for; matrix products, arithmetic and copies ran while one was open for 0% of the time, Pallas kernels for 14%

profile of v3, /device:TPU:2, one launch (start us, length us, event | category | flops | bytes accessed | tf_op | source)
XLA Modules:
  0.0 89.6 jit_solution(8915578386278067489)
XLA Ops:
  0.0 1.3 %broadcast_in_dim.28 = s32[16,8,128]{2,1,0:T(8,128)} broadcast(s32[8,128]{1,0:T(8,128)} %bitcast.21), dimensions={1,2} | broadcast | bytes 69632 | tf_op jit(solution)/shard_map/broadcast_in_dim | solution.py:562
  1.3 5.9 %all-to-all-start = ((s32[16,8,128]{2,1,0:T(8,128)}), s32[16,8,128]{2,1,0:T(8,128)S(1)}, u32[]{:S(2)}, u32[]{:S(2)}) async-start(s32[16,8,128]{2,1,0:T(8,128)} %broadcast_in_dim.28), calls=%async_computation | async-start | bytes 131072 | tf_op jit(solution)/shard_map/all_to_all | solution.py:563
  7.3 3.6 %tables.1 = (f32[32,256]{1,0:T(8,128)}, f32[32,256]{1,0:T(8,128)}, bf16[128,2048]{1,0:T(8,128)(2,1)}) custom-call(s32[1]{0:T(128)} %bitcast.parity, bf16[256,2048]{1,0:T(8,128)(2,1)} %w_own.1, bf16[5,2048]{1,0:T(8,128)(2,1)} %refs_0_.1, f32[1,2048]{1,0:T(1,128)} %bitcast.20, bf16[2048,256]{1,0:T(8,128)(2,1)} %refs_2_.1, bf16[2048,256]{1,0:T(8,128)(2,1)} %refs_3_.1, ...), custom_call_target="tpu_custom_call" | custom-call | tf_op jit(solution)/shard_map/tables/pallas_call | solution.py:455
  10.9 1.2 %all-to-all-done = s32[16,8,128]{2,1,0:T(8,128)S(1)} async-done(((s32[16,8,128]{2,1,0:T(8,128)}), s32[16,8,128]{2,1,0:T(8,128)S(1)}, u32[]{:S(2)}, u32[]{:S(2)}) %all-to-all-start) | async-done | bytes 65568 | tf_op jit(solution)/shard_map/all_to_all | solution.py:563
  12.1 1.9 %collective-permute-start = (f32[32,256]{1,0:T(8,128)}, f32[32,256]{1,0:T(8,128)S(1)}, u32[]{:S(2)}, u32[]{:S(2)}) collective-permute-start(f32[32,256]{1,0:T(8,128)} %get-tuple-element.29.t0), channel_id=1, source_target_pairs={{0,2},{1,3},{2,4},{3,5},{4,6},{5,7},{6,8},{7,9},{8,10},{9,11},{10,... | collective-permute-start | bytes 98312 | tf_op jit(solution)/shard_map/ppermute | solution.py:533
  14.0 2.1 %collective-permute-start.2 = (f32[32,256]{1,0:T(8,128)}, f32[32,256]{1,0:T(8,128)S(1)}, u32[]{:S(2)}, u32[]{:S(2)}) collective-permute-start(f32[32,256]{1,0:T(8,128)} %get-tuple-element.29.t0), channel_id=1, source_target_pairs={{0,1},{1,0},{2,3},{3,2},{4,5},{5,4},{6,7},{7,6},{8,9},{9,8},{10,11... | collective-permute-start | bytes 98312 | tf_op jit(solution)/shard_map/ppermute | solution.py:533
  16.1 3.9 %collective-permute-start.1 = (f32[32,256]{1,0:T(8,128)}, f32[32,256]{1,0:T(8,128)S(1)}, u32[]{:S(2)}, u32[]{:S(2)}) collective-permute-start(f32[32,256]{1,0:T(8,128)} %get-tuple-element.29.t0), channel_id=1, source_target_pairs={{0,14},{1,15},{2,0},{3,1},{4,2},{5,3},{6,4},{7,5},{8,6},{9,7},{10,... | collective-permute-start | bytes 98312 | tf_op jit(solution)/shard_map/ppermute | solution.py:533
  20.1 1.4 %collective-permute-start.5 = (bf16[128,2048]{1,0:T(8,128)(2,1)}, bf16[128,2048]{1,0:T(8,128)(2,1)S(1)}, u32[]{:S(2)}, u32[]{:S(2)}) collective-permute-start(bf16[128,2048]{1,0:T(8,128)(2,1)} %get-tuple-element.41), channel_id=1, source_target_pairs={{0,1},{1,0},{2,3},{3,2},{4,5},{5,4},{6,7},{7,6},{8,9},{9,8},{10,11... | collective-permute-start | bytes 1572872 | tf_op jit(solution)/shard_map/ppermute | solution.py:533
  21.5 2.0 %collective-permute-start.4 = (bf16[128,2048]{1,0:T(8,128)(2,1)}, bf16[128,2048]{1,0:T(8,128)(2,1)S(1)}, u32[]{:S(2)}, u32[]{:S(2)}) collective-permute-start(bf16[128,2048]{1,0:T(8,128)(2,1)} %get-tuple-element.41), channel_id=1, source_target_pairs={{0,14},{1,15},{2,0},{3,1},{4,2},{5,3},{6,4},{7,5},{8,6},{9,7},{10,... | collective-permute-start | bytes 1572872 | tf_op jit(solution)/shard_map/ppermute | solution.py:533
  23.5 0.0 collective-permute-done.t1
  23.5 0.0 collective-permute-start.3
  23.5 0.0 copy-start.2
  23.5 0.0 copy-start.3
  23.6 1.2 %prepare.1 = (f32[128,128]{1,0:T(8,128)S(1)}, f32[128,128]{1,0:T(8,128)S(1)}, f32[5,128,128]{2,1,0:T(8,128)S(1)}, bf16[512,128]{1,0:T(8,128)(2,1)S(1)}, f32[32,2...) custom-call(s32[1]{0:T(128)} %bitcast.1.place, s32[5]{0:T(128)S(1)} %copy-done.1, s32[128,128]{1,0:T(8,128)S(1)} %bitcast.18), custom_call_target="tpu_custom_call" | custom-call | tf_op jit(solution)/shard_map/prepare/pallas_call | solution.py:481
  24.8 0.0 collective-permute-done.2.t3
  24.8 0.0 collective-permute-done.1.t2
  24.8 0.0 copy-start
  24.8 7.9 %block.1 = (bf16[512,1024]{1,0:T(8,128)(2,1)S(1)}, f32[1,512]{1,0:T(1,128)S(1)}) custom-call(s32[1]{0:T(128)} %bitcast.1.place, f32[128,128]{1,0:T(8,128)S(1)} %get-tuple-element.31.grams, f32[128,128]{1,0:T(8,128)S(1)} %get-tuple-element.32.side_tok, f32[5,128,128]{2,1,0:T(8,128)S(1)} %get-tuple-element.33.count, ...), custom_call_target="tpu_custom_call" | custom-call | flops 40000000000 | bytes 104857600 | tf_op jit(solution)/shard_map/block/pallas_call | solution.py:501
  32.7 2.4 %collective-permute-done.5.a3 = bf16[128,2048]{1,0:T(8,128)(2,1)S(1)} collective-permute-done((bf16[128,2048]{1,0:T(8,128)(2,1)}, bf16[128,2048]{1,0:T(8,128)(2,1)S(1)}, u32[]{:S(2)}, u32[]{:S(2)}) %collective-permute-start.5) | collective-permute-done | bytes 524320 | tf_op jit(solution)/shard_map/ppermute | solution.py:533
  35.1 0.0 collective-permute-done.4.a2
  35.2 2.4 %collective-permute-done.3.a1 = bf16[128,2048]{1,0:T(8,128)(2,1)} collective-permute-done((bf16[128,2048]{1,0:T(8,128)(2,1)}, bf16[128,2048]{1,0:T(8,128)(2,1)}, u32[]{:S(2)}, u32[]{:S(2)}) %collective-permute-start.3) | collective-permute-done | bytes 524320 | tf_op jit(solution)/shard_map/ppermute | solution.py:533
  37.6 0.0 collective-permute-start.6
  37.6 0.5 collective-permute-start.7
  38.1 0.0 collective-permute-start.8
  38.1 13.3 %psum.7.sq = f32[1,512]{1,0:T(1,128)S(1)} all-reduce(f32[1,512]{1,0:T(1,128)S(1)} %get-tuple-element.43), channel_id=1, replica_groups={{2,7,10,15},{1,4,9,12},{3,6,11,14},{0,5,8,13},{18,23,26,31},{17,20,25,2..., use_global_device_ids=true, to_apply=%region_0.1 | all-reduce | flops 512 | bytes 4096 | tf_op jit(solution)/shard_map/psum | solution.py:578
  51.4 0.0 collective-permute-done.6.b1
  51.4 0.0 collective-permute-done.7.b2
  51.4 0.0 collective-permute-done.8.b3
  51.4 3.9 %project.1 = bf16[16,256,128]{2,1,0:T(8,128)(2,1)S(1)} custom-call(s32[1]{0:T(128)} %bitcast.parity, bf16[512,1024]{1,0:T(8,128)(2,1)S(1)} %get-tuple-element.42.vg, f32[1,512]{1,0:T(1,128)S(1)} %psum.7.sq, bf16[256,2048]{1,0:T(8,128)(2,1)S(1)} %copy-done, bf16[128,2048]{1,0:T(8,128)(2,1)} %collective-permute-done.3.a1, ...), custom_call_target="tpu_custom_call" | custom-call | tf_op jit(solution)/shard_map/project/pallas_call | solution.py:521
  55.3 33.4 %all_to_all.10 = bf16[16,256,128]{2,1,0:T(8,128)(2,1)S(1)} all-to-all(bf16[16,256,128]{2,1,0:T(8,128)(2,1)S(1)} %project.1), channel_id=1, replica_groups=mesh['context'=16,'tensor'=16] {'tensor'}, dimensions={0} | all-to-all | bytes 2097152 | tf_op jit(solution)/shard_map/all_to_all | solution.py:580
  88.7 0.1 fusion
  88.8 0.7 pad_maximum_fusion
  (5 shorter events, 0.0 us)
Async XLA Ops:
  1.3 10.8 %all-to-all-start = ((s32[16,8,128]{2,1,0:T(8,128)}), s32[16,8,128]{2,1,0:T(8,128)S(1)}, u32[]{:S(2)}, u32[]{:S(2)}) async-start(s32[16,8,128]{2,1,0:T(8,128)} %broadcast_in_dim.28), calls=%async_computation | async-start | bytes 131072 | tf_op jit(solution)/shard_map/all_to_all | solution.py:563
  12.1 11.4 %collective-permute-start = (f32[32,256]{1,0:T(8,128)}, f32[32,256]{1,0:T(8,128)S(1)}, u32[]{:S(2)}, u32[]{:S(2)}) collective-permute-start(f32[32,256]{1,0:T(8,128)} %get-tuple-element.29.t0), channel_id=1, source_target_pairs={{0,2},{1,3},{2,4},{3,5},{4,6},{5,7},{6,8},{7,9},{8,10},{9,11},{10,... | collective-permute-start | bytes 98312 | tf_op jit(solution)/shard_map/ppermute | solution.py:533
  14.0 10.8 %collective-permute-start.2 = (f32[32,256]{1,0:T(8,128)}, f32[32,256]{1,0:T(8,128)S(1)}, u32[]{:S(2)}, u32[]{:S(2)}) collective-permute-start(f32[32,256]{1,0:T(8,128)} %get-tuple-element.29.t0), channel_id=1, source_target_pairs={{0,1},{1,0},{2,3},{3,2},{4,5},{5,4},{6,7},{7,6},{8,9},{9,8},{10,11... | collective-permute-start | bytes 98312 | tf_op jit(solution)/shard_map/ppermute | solution.py:533
  16.1 8.6 %collective-permute-start.1 = (f32[32,256]{1,0:T(8,128)}, f32[32,256]{1,0:T(8,128)S(1)}, u32[]{:S(2)}, u32[]{:S(2)}) collective-permute-start(f32[32,256]{1,0:T(8,128)} %get-tuple-element.29.t0), channel_id=1, source_target_pairs={{0,14},{1,15},{2,0},{3,1},{4,2},{5,3},{6,4},{7,5},{8,6},{9,7},{10,... | collective-permute-start | bytes 98312 | tf_op jit(solution)/shard_map/ppermute | solution.py:533
  20.1 3.4 %copy-start.1 = (s32[5]{0:T(128)S(1)}, s32[5]{0:T(128)}, u32[]{:S(2)}) copy-start(s32[5]{0:T(128)} %comp.1) | copy-start | bytes 64
  20.1 15.1 %collective-permute-start.5 = (bf16[128,2048]{1,0:T(8,128)(2,1)}, bf16[128,2048]{1,0:T(8,128)(2,1)S(1)}, u32[]{:S(2)}, u32[]{:S(2)}) collective-permute-start(bf16[128,2048]{1,0:T(8,128)(2,1)} %get-tuple-element.41), channel_id=1, source_target_pairs={{0,1},{1,0},{2,3},{3,2},{4,5},{5,4},{6,7},{7,6},{8,9},{9,8},{10,11... | collective-permute-start | bytes 1572872 | tf_op jit(solution)/shard_map/ppermute | solution.py:533
  21.5 13.7 %collective-permute-start.4 = (bf16[128,2048]{1,0:T(8,128)(2,1)}, bf16[128,2048]{1,0:T(8,128)(2,1)S(1)}, u32[]{:S(2)}, u32[]{:S(2)}) collective-permute-start(bf16[128,2048]{1,0:T(8,128)(2,1)} %get-tuple-element.41), channel_id=1, source_target_pairs={{0,14},{1,15},{2,0},{3,1},{4,2},{5,3},{6,4},{7,5},{8,6},{9,7},{10,... | collective-permute-start | bytes 1572872 | tf_op jit(solution)/shard_map/ppermute | solution.py:533
  23.5 14.0 %collective-permute-start.3 = (bf16[128,2048]{1,0:T(8,128)(2,1)}, bf16[128,2048]{1,0:T(8,128)(2,1)}, u32[]{:S(2)}, u32[]{:S(2)}) collective-permute-start(bf16[128,2048]{1,0:T(8,128)(2,1)} %get-tuple-element.41), channel_id=1, source_target_pairs={{0,2},{1,3},{2,4},{3,5},{4,6},{5,7},{6,8},{7,9},{8,10},{9,11},{10,... | collective-permute-start | bytes 1572872 | tf_op jit(solution)/shard_map/ppermute | solution.py:533
  23.5 1.3 %copy-start.2 = (f32[32,256]{1,0:T(8,128)S(1)}, f32[32,256]{1,0:T(8,128)}, u32[]{:S(2)}) copy-start(f32[32,256]{1,0:T(8,128)} %get-tuple-element.29.t0) | copy-start | bytes 98308
  23.5 1.3 %copy-start.3 = (f32[32,256]{1,0:T(8,128)S(1)}, f32[32,256]{1,0:T(8,128)}, u32[]{:S(2)}) copy-start(f32[32,256]{1,0:T(8,128)} %get-tuple-element.38.cbc) | copy-start | bytes 98308
  24.8 26.6 %copy-start = (bf16[256,2048]{1,0:T(8,128)(2,1)S(1)}, bf16[256,2048]{1,0:T(8,128)(2,1)}, u32[]{:S(2)}) copy-start(bf16[256,2048]{1,0:T(8,128)(2,1)} %w_own.1) | copy-start | bytes 3145732
  37.6 13.8 %collective-permute-start.6 = (bf16[128,2048]{1,0:T(8,128)(2,1)}, bf16[128,2048]{1,0:T(8,128)(2,1)}, u32[]{:S(2)}, u32[]{:S(2)}) collective-permute-start(bf16[128,2048]{1,0:T(8,128)(2,1)} %collective-permute-done.3.a1), channel_id=1, source_target_pairs={{0,16},{16,0},{32,48},{48,32},{64,80},{80,64},{96,112},{112,96},{1... | collective-permute-start | bytes 1572872 | tf_op jit(solution)/shard_map/ppermute | solution.py:538
  37.6 13.8 %collective-permute-start.7 = (bf16[128,2048]{1,0:T(8,128)(2,1)S(1)}, bf16[128,2048]{1,0:T(8,128)(2,1)}, u32[]{:S(2)}, u32[]{:S(2)}) collective-permute-start(bf16[128,2048]{1,0:T(8,128)(2,1)S(1)} %collective-permute-done.4.a2), channel_id=1, source_target_pairs={{0,16},{16,0},{32,48},{48,32},{64,80},{80,64},{96,112},{112,96},{1... | collective-permute-start | bytes 1572872 | tf_op jit(solution)/shard_map/ppermute | solution.py:538
  38.1 13.3 %collective-permute-start.8 = (bf16[128,2048]{1,0:T(8,128)(2,1)S(1)}, bf16[128,2048]{1,0:T(8,128)(2,1)}, u32[]{:S(2)}, u32[]{:S(2)}) collective-permute-start(bf16[128,2048]{1,0:T(8,128)(2,1)S(1)} %collective-permute-done.5.a3), channel_id=1, source_target_pairs={{0,16},{16,0},{32,48},{48,32},{64,80},{80,64},{96,112},{112,96},{1... | collective-permute-start | bytes 1572872 | tf_op jit(solution)/shard_map/ppermute | solution.py:538

commit v4 on v3

--- a/solution.py
+++ b/solution.py
@@ -58,27 +58,34 @@
     return parts
 
 
-def table_kernel(parity, w_out, *refs):
+def table_kernel(parity, ids, w_out, *refs):
     given = refs[:TABLE_ARGS]
-    tab, cbc, share, rows = refs[TABLE_ARGS : TABLE_ARGS + 4]
+    tab, share, spread, rows = refs[TABLE_ARGS : TABLE_ARGS + 4]
     held = refs[TABLE_ARGS + 4 : -2]
     arrived, shared = refs[-2:]
     half = share.shape[0]
     part = w_out.at[pl.ds(pl.multiple_of(parity[0] * half, half), half), :]
-    copies = []
+    groups = []
+    used = 0
     for source, target in zip(given, held):
         count = PIECES if source.shape[0] > 1024 else 1
         size = source.shape[0] // count
+        group = []
         for n in range(count):
             span = pl.ds(n * size, size)
             one = (source, target) if count == 1 else (source.at[span, :], target.at[span, :])
-            copies.append(pltpu.make_async_copy(*one, arrived.at[len(copies)]))
-    for copy in copies:
-        copy.start()
+            group.append(pltpu.make_async_copy(*one, arrived.at[used]))
+            used += 1
+        groups.append(group)
+    for group in sorted(groups, key=len):
+        for copy in group:
+            copy.start()
     kept = pltpu.make_async_copy(part, share, shared)
     kept.start()
-    for copy in copies:
-        copy.wait()
+    spread[...] = jnp.broadcast_to(ids[...][None], spread.shape)
+    for group in groups:
+        if len(group) == 1:
+            group[0].wait()
     emb, gain, wz, wx, wbc, wdt, bias, alog, dskip, convx, convbc, ggain = held
     rows[...] = jnp.zeros_like(rows)
     rows[0:TOKENS, :] = emb[...].astype(f32)
@@ -87,12 +94,14 @@
         e * lax.rsqrt(jnp.mean(e * e, axis=-1, keepdims=True) + epsilon) * gain[...]
     ).astype(bf16)
 
-    def project(w):
+    def project(w, group):
+        for copy in group:
+            copy.wait()
         return jnp.dot(normed, w[...], preferred_element_type=f32)
 
-    z = project(wz).astype(bf16).astype(f32)
-    xs = project(wx).astype(bf16).astype(f32)
-    bc = project(wbc).astype(bf16).astype(f32)
+    z = project(wz, groups[2]).astype(bf16).astype(f32)
+    xs = project(wx, groups[3]).astype(bf16).astype(f32)
+    bc = project(wbc, groups[4]).astype(bf16).astype(f32)
     raw = lax.dot_general(normed, wdt[...], NT, preferred_element_type=f32) + bias[...]
     dt = jnp.maximum(raw, 0.0) + jnp.log1p(jnp.exp(-jnp.abs(raw)))
     width = z.shape[1]
@@ -113,7 +122,7 @@
     tab[16:20, :] = convx[...]
     tab[24:32, :] = jnp.where(row < TOKENS, spread(dt), 0.0)
     for k in range(4):
-        cbc[8 * k : 8 * k + 8, :] = convbc[k : k + 1, :] * bc
+        tab[32 + 8 * k : 40 + 8 * k, :] = convbc[k : k + 1, :] * bc
     kept.wait()
 
 
@@ -214,11 +223,11 @@
 
 
 def block_kernel(
-    place, grams, side_tok, count, hot_taps, own_rows, older, t0, t1, t2, t3, cbc, vg, sq
+    place, grams, side_tok, count, hot_taps, own_rows, older, t0, t1, t2, t3, vg, sq
 ):
     chunk = place[0] // 8
     r0 = place[0]
-    tab = jnp.concatenate([t0[...], t1[...], t2[...], t3[...]], axis=1)
+    tab = jnp.concatenate([t[0:32, :] for t in (t0, t1, t2, t3)], axis=1)
     dt_tab = tab[24:32]
     rate_tab = tab[7:8] * dt_tab * LOG2E
     log_tab = jnp.log2(jnp.maximum(dt_tab, TINY))
@@ -289,7 +298,7 @@
     hist = (part + jnp.concatenate(sides, axis=1)).astype(bf16)
 
     taps = jnp.concatenate([tab[16 + k : 17 + k] * tab[8:16] for k in range(4)], axis=0)
-    bc_taps = cbc[...]
+    bc_taps = t0[32:64, :]
     kinds = older[...]
     rest = jnp.zeros((56, WIDE), f32)
     x_older = jnp.dot(kinds, stack(*split(taps[0:24]), rest), preferred_element_type=f32)
@@ -398,44 +407,48 @@
         sq[:, rows] = summed[0:1]
 
 
-def out_kernel(parity, vg, sq, w_own, a1, a2, a3, b1, b2, b3, out, g_all):
+def first_kernel(parity, vg, w_own, a1, a2, a3, forward, reverse, rest, known):
+    half = LANES
+    for s in range(2):
+        rows = slice(s * BLOCK, (s + 1) * BLOCK)
+        known[rows, 0 : 2 * half] = vg[rows, 0 : 2 * half]
+        for d in range(3):
+            even = vg[rows, (2 * d + 2) * half : (2 * d + 3) * half]
+            odd = vg[rows, (2 * d + 3) * half : (2 * d + 4) * half]
+            swapped = parity[0] == 1
+            known[rows, (d + 2) * half : (d + 3) * half] = jnp.where(swapped, odd, even)
+            rest[rows, d * half : (d + 1) * half] = jnp.where(swapped, even, odd)
+    tile = 2 * LANES
+    for n in range(forward.shape[1] // tile):
+        cols = slice(n * tile, (n + 1) * tile)
+        weights = jnp.concatenate([w[:, cols] for w in (w_own, a1, a2, a3)], axis=0)
+        both = jnp.dot(known[...], weights, preferred_element_type=f32)
+        forward[:, cols] = both[:BLOCK]
+        reverse[:, cols] = both[BLOCK:]
+
+
+def second_kernel(q0, q1, q2, q3, forward, reverse, rest, b1, b2, b3, out):
     first = iota((8, 2 * BLOCK), 0) == 0
-    inverse = jnp.where(first, lax.rsqrt(sq[...] / 4096.0 + epsilon), 0.0)
+    total = (q0[...] + q1[...]) + (q2[...] + q3[...])
+    inverse = jnp.where(first, lax.rsqrt(total / 4096.0 + epsilon), 0.0)
     inverse = lax.dot_general(
         inverse, jnp.ones((8, LANES), f32), TN, precision=highest, preferred_element_type=f32
     )
-    half = LANES
-    for p in range(WIDE // half):
-        chans = slice(p * half, (p + 1) * half)
-        strands = [
-            (vg[s * BLOCK : (s + 1) * BLOCK, chans].astype(f32) * inverse[s * BLOCK : (s + 1) * BLOCK])
-            .astype(bf16)
-            .astype(f32)
-            for s in range(2)
-        ]
-        g = (strands[0] + strands[1]).astype(bf16)
-        if p < 2:
-            g_all[:, chans] = g
-        else:
-            at = (p - p % 2 + (parity[0] ^ (p % 2))) * half
-            g_all[:, pl.ds(pl.multiple_of(at, half), half)] = g
-    g = g_all[...]
+    inverse = jnp.concatenate([inverse, inverse], axis=1)
+    g = rest[...]
     tile = 2 * LANES
     for n in range(out.shape[0] // 2):
         cols = slice(n * tile, (n + 1) * tile)
-        weights = [w_own[:, cols]]
-        for a, b in ((a1, b1), (a2, b2), (a3, b3)):
-            weights.append(a[:, cols])
-            weights.append(b[:, cols])
-        result = jnp.dot(
-            g, jnp.concatenate(weights, axis=0), preferred_element_type=f32
-        ).astype(bf16)
+        weights = jnp.concatenate([w[:, cols] for w in (b1, b2, b3)], axis=0)
+        both = jnp.dot(g, weights, preferred_element_type=f32)
+        result = (both[:BLOCK] + forward[:, cols]) * inverse[:BLOCK]
+        result = (result + (both[BLOCK:] + reverse[:, cols]) * inverse[BLOCK:]).astype(bf16)
         out[2 * n] = result[:, :LANES]
         out[2 * n + 1] = result[:, LANES:]
 
 
 def build_tables(
-    parity, w_out, embedding, norm_gain, w_z, w_x, w_bc, w_dt, dt_bias, a_log, d_skip, conv_x, conv_bc, gate_gain
+    parity, ids, count, w_out, embedding, norm_gain, w_z, w_x, w_bc, w_dt, dt_bias, a_log, d_skip, conv_x, conv_bc, gate_gain
 ):
     width = w_z.shape[1]
     given = (
@@ -454,7 +467,7 @@
     )
     return pl.pallas_call(
         table_kernel,
-        in_specs=[pl.BlockSpec(memory_space=pltpu.SMEM)]
+        in_specs=[pl.BlockSpec(memory_space=pltpu.SMEM), pl.BlockSpec(memory_space=pltpu.VMEM)]
         + [pl.BlockSpec(memory_space=pltpu.HBM)] * (TABLE_ARGS + 1),
         out_specs=(
             pl.BlockSpec(memory_space=pltpu.VMEM),
@@ -462,16 +475,16 @@
             pl.BlockSpec(memory_space=pltpu.VMEM),
         ),
         out_shape=(
-            jax.ShapeDtypeStruct((32, width), f32),
-            jax.ShapeDtypeStruct((32, w_bc.shape[1]), f32),
+            jax.ShapeDtypeStruct((64, width), f32),
             jax.ShapeDtypeStruct((w_out.shape[0] // 2, w_out.shape[1]), w_out.dtype),
+            jax.ShapeDtypeStruct((count, *ids.shape), i32),
         ),
         scratch_shapes=[pltpu.VMEM((8, embedding.shape[1]), f32)]
         + [pltpu.VMEM(x.shape, x.dtype) for x in given]
         + [pltpu.SemaphoreType.DMA((TABLE_ARGS + 3 * (PIECES - 1),)), pltpu.SemaphoreType.DMA(())],
         compiler_params=pltpu.CompilerParams(vmem_limit_bytes=60 * 2**20),
         name="tables",
-    )(parity, w_out, *given)
+    )(parity, ids, w_out, *given)
 
 
 def prepare(place, complement, ids):
@@ -495,12 +508,12 @@
     )(place, complement, ids)
 
 
-def run_block(place, prepared, tabs, cbc):
+def run_block(place, prepared, tabs):
     smem = pl.BlockSpec(memory_space=pltpu.SMEM)
     vmem = pl.BlockSpec(memory_space=pltpu.VMEM)
     return pl.pallas_call(
         block_kernel,
-        in_specs=[smem] + [vmem] * 11,
+        in_specs=[smem] + [vmem] * 10,
         out_specs=(vmem, vmem),
         out_shape=(
             jax.ShapeDtypeStruct((2 * BLOCK, WIDE), bf16),
@@ -511,26 +524,54 @@
             flops=40 * 10**9, bytes_accessed=100 * 2**20, transcendentals=10**7
         ),
         name="block",
-    )(place, *prepared, *tabs, cbc)
-
-
-def run_out(parity, vg, sq, w_own, mine, theirs):
+    )(place, *prepared, *tabs)
+
+
+def run_first(parity, vg, w_own, mine):
     features = w_own.shape[1]
+    part = mine[0].shape[0]
     smem = pl.BlockSpec(memory_space=pltpu.SMEM)
     vmem = pl.BlockSpec(memory_space=pltpu.VMEM)
     return pl.pallas_call(
-        out_kernel,
-        in_specs=[smem] + [vmem] * 9,
+        first_kernel,
+        in_specs=[smem] + [vmem] * 5,
+        out_specs=(vmem,) * 3,
+        out_shape=(
+            jax.ShapeDtypeStruct((BLOCK, features), f32),
+            jax.ShapeDtypeStruct((BLOCK, features), f32),
+            jax.ShapeDtypeStruct((2 * BLOCK, 3 * part), bf16),
+        ),
+        scratch_shapes=[pltpu.VMEM((2 * BLOCK, 5 * part), bf16)],
+        compiler_params=pltpu.CompilerParams(vmem_limit_bytes=32 * 2**20),
+        cost_estimate=pl.CostEstimate(
+            flops=60 * 10**9, bytes_accessed=100 * 2**20, transcendentals=0
+        ),
+        name="project_first",
+    )(parity, vg, w_own, *mine)
+
+
+def run_second(squares, forward, reverse, rest, theirs):
+    features = forward.shape[1]
+    vmem = pl.BlockSpec(memory_space=pltpu.VMEM)
+    return pl.pallas_call(
+        second_kernel,
+        in_specs=[vmem] * 10,
         out_specs=vmem,
         out_shape=jax.ShapeDtypeStruct((features // LANES, BLOCK, LANES), bf16),
-        scratch_shapes=[pltpu.VMEM((BLOCK, WIDE), bf16)],
-        compiler_params=pltpu.CompilerParams(vmem_limit_bytes=40 * 2**20),
-        name="project",
-    )(parity, vg, sq, w_own, *mine, *theirs)
-
-
-def from_peers(x):
-    return [lax.ppermute(x, "tensor", pairs) for pairs in PEERS]
+        compiler_params=pltpu.CompilerParams(vmem_limit_bytes=32 * 2**20),
+        name="project_second",
+    )(*squares, forward, reverse, rest, *theirs)
+
+
+MATES = (
+    [(t, (t + 8) % 16) for t in range(16)],
+    [(t, ((t + 4) % 16) ^ 1) for t in range(16)],
+    [(t, ((t - 4) % 16) ^ 1) for t in range(16)],
+)
+
+
+def exchange(x, group):
+    return [lax.ppermute(x, "tensor", pairs) for pairs in group]
 
 
 def other_core(x):
@@ -558,25 +599,24 @@
     context = lax.axis_index("context").astype(i32)
     tensor = lax.axis_index("tensor").astype(i32)
     parity = context % 2
-    count = lax.axis_size("context")
-    spread = jnp.broadcast_to(ids.reshape(1, -1, LANES), (count, ids.shape[0] // LANES, LANES))
-    everyone = lax.all_to_all(spread, "context", 0, 0, tiled=True).reshape(ROWS, LANES)
     quarter = (tensor // 2 + 2 * (tensor % 2) + 3) % 4
     place = (context * (ids.shape[0] // LANES) + quarter * (BLOCK // LANES)).reshape(1)
-    tab, cbc, share = build_tables(
-        parity.reshape(1), w_out, embedding, norm_gain, w_z, w_x, w_bc, w_dt, dt_bias, a_log, d_skip, conv_x, conv_bc, gate_gain
+    tab, share, spread = build_tables(
+        parity.reshape(1), ids.reshape(-1, LANES), lax.axis_size("context"), w_out,
+        embedding, norm_gain, w_z, w_x, w_bc, w_dt, dt_bias, a_log, d_skip, conv_x, conv_bc, gate_gain
     )
-    tab, everyone, share = lax.optimization_barrier((tab, everyone, share))
-    tabs = [tab] + from_peers(tab)
+    everyone = lax.all_to_all(spread, "context", 0, 0, tiled=True).reshape(ROWS, LANES)
+    tabs = [tab] + exchange(tab, PEERS)
     everyone, tabs[1] = lax.optimization_barrier((everyone, tabs[1]))
     prepared = prepare(place, complement, everyone)
-    mine = from_peers(share)
-
-    vg, sq = run_block(place, prepared, tabs, cbc)
-    vg, sq, *mine = lax.optimization_barrier((vg, sq, *mine))
+    mine = exchange(share, PEERS)
+
+    vg, sq = run_block(place, prepared, tabs)
+    squares = [sq] + exchange(sq, MATES)
+    vg, *mine = lax.optimization_barrier((vg, *mine))
     theirs = [other_core(x) for x in mine]
-    sq = lax.psum(sq, "tensor", axis_index_groups=QUARTERS)
-    terms = run_out(parity.reshape(1), vg, sq, w_out, mine, theirs)
+    forward, reverse, rest = run_first(parity.reshape(1), vg, w_out, mine)
+    terms = run_second(squares, forward, reverse, rest, theirs)
     arrived = lax.all_to_all(terms, "tensor", 0, 0, tiled=True)
     summed = [sum(arrived[t].astype(f32) for t in members) for members in QUARTERS]
     return jnp.concatenate(summed, axis=0).astype(bf16)

time: 89.8 us -> 84.6 us (0.942)
  starting transfers between devices: 17.9 us -> 30.4 us
  blocking collectives: 46.7 us -> 34.4 us
  waiting for transfers between devices: 6.09 us -> 1.17 us
    psum x1 -> x0, blocking collectives: 13.3 us -> none  [local(): sq = lax.psum(sq, 'tensor', axis_index_groups=QUARTERS)]
    ppermute x6 -> x9, starting transfers between devices: 11.4 us -> 23.8 us  [exchange(): return [lax.ppermute(x, 'tensor', pairs) for pairs in group]]
    ppermute x6 -> x9, waiting for transfers between devices: 4.85 us -> 0.02 us  [exchange(): return [lax.ppermute(x, 'tensor', pairs) for pairs in group]]
    broadcast_in_dim x1 -> x0, local copies, waits for them, and re-layouts: 1.32 us -> none  [local(): jnp.broadcast_to(ids.reshape(1, -1, LANES), (count, ids.shape[0] // LANES...]
    all_to_all x1, waiting for transfers between devices: 1.23 us -> 0.19 us  [local(): lax.all_to_all(spread, 'context', 0, 0, tiled=True).reshape(ROWS, LANES)]
    all_to_all x1, blocking collectives: 33.4 us -> 34.4 us  [local(): arrived = lax.all_to_all(terms, 'tensor', 0, 0, tiled=True)]
    ppermute x3, waiting for transfers between devices: 0.01 us -> 0.96 us  [other_core(): return lax.ppermute(x, 'context', [(i, i ^ 1) for i in range(count)])]
    pallas_call x2 -> x3, Pallas kernels: 11.8 us -> 11.2 us  [the longest x1 7.79 us: run_block(): pl.pallas_call(block_kernel, in_specs=[smem] + [vmem] * 10, out_specs=(vm...]
  transfers between devices with their start and end apart: 10 -> 13, of which waited for: 3 -> 3; matrix products, arithmetic and copies ran while one was open for 0% -> 0% of each run, Pallas kernels for 14% -> 13%
where the time goes in v4:
time: 84.6 us; the launch traced here: 84.3 us
  blocking collectives  34.4 us (41%)
  starting transfers between devices  30.4 us (36%)
  Pallas kernels  16.6 us (20%)
  waiting for transfers between devices  1.17 us (1%)
  other arithmetic  0.86 us (1%)
    all_to_all x1, blocking collectives, local(): arrived = lax.all_to_all(terms, 'tensor', 0, 0, tiled=True)  34.4 us
    ppermute x9, starting transfers between devices, exchange(): return [lax.ppermute(x, 'tensor', pairs) for pairs in group]  23.8 us
    pallas_call x1, Pallas kernels, run_block(): pl.pallas_call(block_kernel, in_specs=[smem] + [vmem] * 10, out_specs=(vm...  7.79 us
    all_to_all x1, starting transfers between devices, local(): lax.all_to_all(spread, 'context', 0, 0, tiled=True).reshape(ROWS, LANES)  5.95 us
    pallas_call x1, Pallas kernels, build_tables(): pl.pallas_call(table_kernel, in_specs=[pl.BlockSpec(memory_space=pltpu.SM...  4.13 us
    pallas_call x1, Pallas kernels, run_first(): pl.pallas_call(first_kernel, in_specs=[smem] + [vmem] * 5, out_specs=(vme...  1.8 us
  transfers between devices with their start and end apart: 13, of which 3 were waited for; matrix products, arithmetic and copies ran while one was open for 0% of the time, Pallas kernels for 13%

profile of v4, /device:TPU:2, one launch (start us, length us, event | category | flops | bytes accessed | tf_op | source)
XLA Modules:
  0.0 84.3 jit_solution(11181780934936321588)
XLA Ops:
  0.0 4.1 %tables.1 = (f32[64,256]{1,0:T(8,128)}, bf16[128,2048]{1,0:T(8,128)(2,1)}, s32[16,8,128]{2,1,0:T(8,128)}) custom-call(s32[1]{0:T(128)} %bitcast.1.parity, s32[8,128]{1,0:T(8,128)} %bitcast.21, bf16[256,2048]{1,0:T(8,128)(2,1)} %w_own.1, bf16[5,2048]{1,0:T(8,128)(2,1)} %refs_0_.1, f32[1,2048]{1,0:T(1,128)} %bitcast.20, bf16[2048,256]{1,0:T(8,128)(2,1)} %refs_2_.1, ...), custom_call_target="tpu_custom_call" | custom-call | tf_op jit(solution)/shard_map/tables/pallas_call | solution.py:468
  4.1 2.0 %collective-permute-start = (f32[64,256]{1,0:T(8,128)}, f32[64,256]{1,0:T(8,128)S(1)}, u32[]{:S(2)}, u32[]{:S(2)}) collective-permute-start(f32[64,256]{1,0:T(8,128)} %get-tuple-element.26.t0), channel_id=1, source_target_pairs={{0,2},{1,3},{2,4},{3,5},{4,6},{5,7},{6,8},{7,9},{8,10},{9,11},{10,... | collective-permute-start | bytes 196616 | tf_op jit(solution)/shard_map/ppermute | solution.py:574
  6.1 4.0 %collective-permute-start.1 = (f32[64,256]{1,0:T(8,128)}, f32[64,256]{1,0:T(8,128)S(1)}, u32[]{:S(2)}, u32[]{:S(2)}) collective-permute-start(f32[64,256]{1,0:T(8,128)} %get-tuple-element.26.t0), channel_id=1, source_target_pairs={{0,14},{1,15},{2,0},{3,1},{4,2},{5,3},{6,4},{7,5},{8,6},{9,7},{10,... | collective-permute-start | bytes 196616 | tf_op jit(solution)/shard_map/ppermute | solution.py:574
  10.2 2.1 %collective-permute-start.2 = (f32[64,256]{1,0:T(8,128)}, f32[64,256]{1,0:T(8,128)S(1)}, u32[]{:S(2)}, u32[]{:S(2)}) collective-permute-start(f32[64,256]{1,0:T(8,128)} %get-tuple-element.26.t0), channel_id=1, source_target_pairs={{0,1},{1,0},{2,3},{3,2},{4,5},{5,4},{6,7},{7,6},{8,9},{9,8},{10,11... | collective-permute-start | bytes 196616 | tf_op jit(solution)/shard_map/ppermute | solution.py:574
  12.3 5.9 %all-to-all-start = ((s32[16,8,128]{2,1,0:T(8,128)}), s32[16,8,128]{2,1,0:T(8,128)S(1)}, u32[]{:S(2)}, u32[]{:S(2)}) async-start(s32[16,8,128]{2,1,0:T(8,128)} %get-tuple-element.25), calls=%async_computation | async-start | bytes 131072 | tf_op jit(solution)/shard_map/all_to_all | solution.py:608
  18.2 0.0 collective-permute-start.6
  18.2 3.2 %collective-permute-start.7 = (bf16[128,2048]{1,0:T(8,128)(2,1)}, bf16[128,2048]{1,0:T(8,128)(2,1)S(1)}, u32[]{:S(2)}, u32[]{:S(2)}) collective-permute-start(bf16[128,2048]{1,0:T(8,128)(2,1)} %get-tuple-element.37), channel_id=1, source_target_pairs={{0,14},{1,15},{2,0},{3,1},{4,2},{5,3},{6,4},{7,5},{8,6},{9,7},{10,... | collective-permute-start | bytes 1572872 | tf_op jit(solution)/shard_map/ppermute | solution.py:574
  21.5 0.0 collective-permute-done.t1
  21.5 1.4 %collective-permute-start.8 = (bf16[128,2048]{1,0:T(8,128)(2,1)}, bf16[128,2048]{1,0:T(8,128)(2,1)S(1)}, u32[]{:S(2)}, u32[]{:S(2)}) collective-permute-start(bf16[128,2048]{1,0:T(8,128)(2,1)} %get-tuple-element.37), channel_id=1, source_target_pairs={{0,1},{1,0},{2,3},{3,2},{4,5},{5,4},{6,7},{7,6},{8,9},{9,8},{10,11... | collective-permute-start | bytes 1572872 | tf_op jit(solution)/shard_map/ppermute | solution.py:574
  22.9 0.2 all-to-all-done
  23.1 1.2 %prepare.1 = (f32[128,128]{1,0:T(8,128)S(1)}, f32[128,128]{1,0:T(8,128)S(1)}, f32[5,128,128]{2,1,0:T(8,128)S(1)}, bf16[512,128]{1,0:T(8,128)(2,1)S(1)}, f32[32,2...) custom-call(s32[1]{0:T(128)} %bitcast.place, s32[5]{0:T(128)S(1)} %copy-done.1, s32[128,128]{1,0:T(8,128)S(1)} %bitcast.18), custom_call_target="tpu_custom_call" | custom-call | tf_op jit(solution)/shard_map/prepare/pallas_call | solution.py:494
  24.3 0.0 collective-permute-done.1.t2
  24.3 0.0 copy-start.2
  24.3 0.8 copy-done.2
  25.2 7.8 %block.1 = (bf16[512,1024]{1,0:T(8,128)(2,1)S(1)}, f32[1,512]{1,0:T(1,128)S(1)}) custom-call(s32[1]{0:T(128)} %bitcast.place, f32[128,128]{1,0:T(8,128)S(1)} %get-tuple-element.28.grams, f32[128,128]{1,0:T(8,128)S(1)} %get-tuple-element.29.side_tok, f32[5,128,128]{2,1,0:T(8,128)S(1)} %get-tuple-element.30.count, ...), custom_call_target="tpu_custom_call" | custom-call | flops 40000000000 | bytes 104857600 | tf_op jit(solution)/shard_map/block/pallas_call | solution.py:514
  33.0 4.5 %collective-permute-start.3 = (f32[1,512]{1,0:T(1,128)S(1)}, f32[1,512]{1,0:T(1,128)S(1)}, u32[]{:S(2)}, u32[]{:S(2)}) collective-permute-start(f32[1,512]{1,0:T(1,128)S(1)} %get-tuple-element.35.q0), channel_id=1, source_target_pairs={{0,8},{1,9},{2,10},{3,11},{4,12},{5,13},{6,14},{7,15},{8,0},{9,1},... | collective-permute-start | bytes 6152 | tf_op jit(solution)/shard_map/ppermute | solution.py:574
  37.5 1.1 %collective-permute-start.4 = (f32[1,512]{1,0:T(1,128)S(1)}, f32[1,512]{1,0:T(1,128)S(1)}, u32[]{:S(2)}, u32[]{:S(2)}) collective-permute-start(f32[1,512]{1,0:T(1,128)S(1)} %get-tuple-element.35.q0), channel_id=1, source_target_pairs={{0,5},{1,4},{2,7},{3,6},{4,9},{5,8},{6,11},{7,10},{8,13},{9,12},{1... | collective-permute-start | bytes 6152 | tf_op jit(solution)/shard_map/ppermute | solution.py:574
  38.6 0.0 collective-permute-done.6.a1
  38.6 5.4 %collective-permute-start.5 = (f32[1,512]{1,0:T(1,128)S(1)}, f32[1,512]{1,0:T(1,128)S(1)}, u32[]{:S(2)}, u32[]{:S(2)}) collective-permute-start(f32[1,512]{1,0:T(1,128)S(1)} %get-tuple-element.35.q0), channel_id=1, source_target_pairs={{0,13},{1,12},{2,15},{3,14},{4,1},{5,0},{6,3},{7,2},{8,5},{9,4},{1... | collective-permute-start | bytes 6152 | tf_op jit(solution)/shard_map/ppermute | solution.py:574
  44.0 0.0 collective-permute-done.7.a2
  44.0 0.5 collective-permute-start.11
  44.6 0.0 collective-permute-done.3.q1
  44.6 0.1 collective-permute-start.9
  44.7 1.8 %project_first.1 = (f32[256,2048]{1,0:T(8,128)S(1)}, f32[256,2048]{1,0:T(8,128)S(1)}, bf16[512,384]{1,0:T(8,128)(2,1)S(1)}) custom-call(s32[1]{0:T(128)} %bitcast.1.parity, bf16[512,1024]{1,0:T(8,128)(2,1)S(1)} %get-tuple-element.38.vg, bf16[256,2048]{1,0:T(8,128)(2,1)S(1)} %copy-done, bf16[128,2048]{1,0:T(8,128)(2,1)S(1)} %collective-permute-done.6.a1, ...), custom_call_target="tpu_custom_call" | custom-call | flops 60000002048 | bytes 104857600 | tf_op jit(solution)/shard_map/project_first/pallas_call | solution.py:535
  46.5 0.0 collective-permute-done.4.q2
  46.5 0.0 collective-permute-done.10.b2
  46.5 0.2 collective-permute-done.11.b3
  46.7 0.7 collective-permute-done.9.b1
  47.5 1.6 %project_second.1 = bf16[16,256,128]{2,1,0:T(8,128)(2,1)S(1)} custom-call(f32[1,512]{1,0:T(1,128)S(1)} %get-tuple-element.35.q0, f32[1,512]{1,0:T(1,128)S(1)} %collective-permute-done.3.q1, f32[1,512]{1,0:T(1,128)S(1)} %collective-permute-done.4.q2, f32[1,512]{1,0:T(1,128)S(1)} %collective-permute-done.5.q3, f32[256,2048]{1,0:T(8,128)S(1)} %get-tuple-element.42.forward, ...), custom_call_target="tpu_custom_call" | custom-call | tf_op jit(solution)/shard_map/project_second/pallas_call | solution.py:556
  49.1 34.4 %all_to_all.10 = bf16[16,256,128]{2,1,0:T(8,128)(2,1)S(1)} all-to-all(bf16[16,256,128]{2,1,0:T(8,128)(2,1)S(1)} %project_second.1), channel_id=1, replica_groups=mesh['context'=16,'tensor'=16] {'tensor'}, dimensions={0} | all-to-all | bytes 2097152 | tf_op jit(solution)/shard_map/all_to_all | solution.py:620
  83.5 0.1 fusion
  83.6 0.7 pad_maximum_fusion
  (8 shorter events, 0.0 us)
Async XLA Ops:
  0.0 23.1 %copy-start.1 = (s32[5]{0:T(128)S(1)}, s32[5]{0:T(128)}, u32[]{:S(2)}) copy-start(s32[5]{0:T(128)} %comp.1) | copy-start | bytes 64
  4.1 17.3 %collective-permute-start = (f32[64,256]{1,0:T(8,128)}, f32[64,256]{1,0:T(8,128)S(1)}, u32[]{:S(2)}, u32[]{:S(2)}) collective-permute-start(f32[64,256]{1,0:T(8,128)} %get-tuple-element.26.t0), channel_id=1, source_target_pairs={{0,2},{1,3},{2,4},{3,5},{4,6},{5,7},{6,8},{7,9},{8,10},{9,11},{10,... | collective-permute-start | bytes 196616 | tf_op jit(solution)/shard_map/ppermute | solution.py:574
  6.1 18.2 %collective-permute-start.1 = (f32[64,256]{1,0:T(8,128)}, f32[64,256]{1,0:T(8,128)S(1)}, u32[]{:S(2)}, u32[]{:S(2)}) collective-permute-start(f32[64,256]{1,0:T(8,128)} %get-tuple-element.26.t0), channel_id=1, source_target_pairs={{0,14},{1,15},{2,0},{3,1},{4,2},{5,3},{6,4},{7,5},{8,6},{9,7},{10,... | collective-permute-start | bytes 196616 | tf_op jit(solution)/shard_map/ppermute | solution.py:574
  10.2 14.2 %collective-permute-start.2 = (f32[64,256]{1,0:T(8,128)}, f32[64,256]{1,0:T(8,128)S(1)}, u32[]{:S(2)}, u32[]{:S(2)}) collective-permute-start(f32[64,256]{1,0:T(8,128)} %get-tuple-element.26.t0), channel_id=1, source_target_pairs={{0,1},{1,0},{2,3},{3,2},{4,5},{5,4},{6,7},{7,6},{8,9},{9,8},{10,11... | collective-permute-start | bytes 196616 | tf_op jit(solution)/shard_map/ppermute | solution.py:574
  12.3 10.8 %all-to-all-start = ((s32[16,8,128]{2,1,0:T(8,128)}), s32[16,8,128]{2,1,0:T(8,128)S(1)}, u32[]{:S(2)}, u32[]{:S(2)}) async-start(s32[16,8,128]{2,1,0:T(8,128)} %get-tuple-element.25), calls=%async_computation | async-start | bytes 131072 | tf_op jit(solution)/shard_map/all_to_all | solution.py:608
  18.2 20.4 %collective-permute-start.6 = (bf16[128,2048]{1,0:T(8,128)(2,1)}, bf16[128,2048]{1,0:T(8,128)(2,1)S(1)}, u32[]{:S(2)}, u32[]{:S(2)}) collective-permute-start(bf16[128,2048]{1,0:T(8,128)(2,1)} %get-tuple-element.37), channel_id=1, source_target_pairs={{0,2},{1,3},{2,4},{3,5},{4,6},{5,7},{6,8},{7,9},{8,10},{9,11},{10,... | collective-permute-start | bytes 1572872 | tf_op jit(solution)/shard_map/ppermute | solution.py:574
  18.2 25.8 %collective-permute-start.7 = (bf16[128,2048]{1,0:T(8,128)(2,1)}, bf16[128,2048]{1,0:T(8,128)(2,1)S(1)}, u32[]{:S(2)}, u32[]{:S(2)}) collective-permute-start(bf16[128,2048]{1,0:T(8,128)(2,1)} %get-tuple-element.37), channel_id=1, source_target_pairs={{0,14},{1,15},{2,0},{3,1},{4,2},{5,3},{6,4},{7,5},{8,6},{9,7},{10,... | collective-permute-start | bytes 1572872 | tf_op jit(solution)/shard_map/ppermute | solution.py:574
  21.5 22.6 %collective-permute-start.8 = (bf16[128,2048]{1,0:T(8,128)(2,1)}, bf16[128,2048]{1,0:T(8,128)(2,1)S(1)}, u32[]{:S(2)}, u32[]{:S(2)}) collective-permute-start(bf16[128,2048]{1,0:T(8,128)(2,1)} %get-tuple-element.37), channel_id=1, source_target_pairs={{0,1},{1,0},{2,3},{3,2},{4,5},{5,4},{6,7},{7,6},{8,9},{9,8},{10,11... | collective-permute-start | bytes 1572872 | tf_op jit(solution)/shard_map/ppermute | solution.py:574
  24.3 0.8 copy-start.2
  25.2 19.5 %copy-start = (bf16[256,2048]{1,0:T(8,128)(2,1)S(1)}, bf16[256,2048]{1,0:T(8,128)(2,1)}, u32[]{:S(2)}) copy-start(bf16[256,2048]{1,0:T(8,128)(2,1)} %w_own.1) | copy-start | bytes 3145732
  33.0 11.6 %collective-permute-start.3 = (f32[1,512]{1,0:T(1,128)S(1)}, f32[1,512]{1,0:T(1,128)S(1)}, u32[]{:S(2)}, u32[]{:S(2)}) collective-permute-start(f32[1,512]{1,0:T(1,128)S(1)} %get-tuple-element.35.q0), channel_id=1, source_target_pairs={{0,8},{1,9},{2,10},{3,11},{4,12},{5,13},{6,14},{7,15},{8,0},{9,1},... | collective-permute-start | bytes 6152 | tf_op jit(solution)/shard_map/ppermute | solution.py:574
  37.5 9.0 %collective-permute-start.4 = (f32[1,512]{1,0:T(1,128)S(1)}, f32[1,512]{1,0:T(1,128)S(1)}, u32[]{:S(2)}, u32[]{:S(2)}) collective-permute-start(f32[1,512]{1,0:T(1,128)S(1)} %get-tuple-element.35.q0), channel_id=1, source_target_pairs={{0,5},{1,4},{2,7},{3,6},{4,9},{5,8},{6,11},{7,10},{8,13},{9,12},{1... | collective-permute-start | bytes 6152 | tf_op jit(solution)/shard_map/ppermute | solution.py:574
  38.6 7.9 %collective-permute-start.5 = (f32[1,512]{1,0:T(1,128)S(1)}, f32[1,512]{1,0:T(1,128)S(1)}, u32[]{:S(2)}, u32[]{:S(2)}) collective-permute-start(f32[1,512]{1,0:T(1,128)S(1)} %get-tuple-element.35.q0), channel_id=1, source_target_pairs={{0,13},{1,12},{2,15},{3,14},{4,1},{5,0},{6,3},{7,2},{8,5},{9,4},{1... | collective-permute-start | bytes 6152 | tf_op jit(solution)/shard_map/ppermute | solution.py:574
  44.0 2.4 %collective-permute-start.10 = (bf16[128,2048]{1,0:T(8,128)(2,1)S(1)}, bf16[128,2048]{1,0:T(8,128)(2,1)S(1)}, u32[]{:S(2)}, u32[]{:S(2)}) collective-permute-start(bf16[128,2048]{1,0:T(8,128)(2,1)S(1)} %collective-permute-done.7.a2), channel_id=1, source_target_pairs={{0,16},{16,0},{32,48},{48,32},{64,80},{80,64},{96,112},{112,96},{1... | collective-permute-start | bytes 1572872 | tf_op jit(solution)/shard_map/ppermute | solution.py:579
  44.0 2.7 %collective-permute-start.11 = (bf16[128,2048]{1,0:T(8,128)(2,1)S(1)}, bf16[128,2048]{1,0:T(8,128)(2,1)S(1)}, u32[]{:S(2)}, u32[]{:S(2)}) collective-permute-start(bf16[128,2048]{1,0:T(8,128)(2,1)S(1)} %collective-permute-done.8.a3), channel_id=1, source_target_pairs={{0,16},{16,0},{32,48},{48,32},{64,80},{80,64},{96,112},{112,96},{1... | collective-permute-start | bytes 1572872 | tf_op jit(solution)/shard_map/ppermute | solution.py:579
  44.6 2.9 %collective-permute-start.9 = (bf16[128,2048]{1,0:T(8,128)(2,1)S(1)}, bf16[128,2048]{1,0:T(8,128)(2,1)S(1)}, u32[]{:S(2)}, u32[]{:S(2)}) collective-permute-start(bf16[128,2048]{1,0:T(8,128)(2,1)S(1)} %collective-permute-done.6.a1), channel_id=1, source_target_pairs={{0,16},{16,0},{32,48},{48,32},{64,80},{80,64},{96,112},{112,96},{1... | collective-permute-start | bytes 1572872 | tf_op jit(solution)/shard_map/ppermute | solution.py:579

commit v5 on v4

--- a/solution.py
+++ b/solution.py
@@ -607,7 +607,6 @@
     )
     everyone = lax.all_to_all(spread, "context", 0, 0, tiled=True).reshape(ROWS, LANES)
     tabs = [tab] + exchange(tab, PEERS)
-    everyone, tabs[1] = lax.optimization_barrier((everyone, tabs[1]))
     prepared = prepare(place, complement, everyone)
     mine = exchange(share, PEERS)
 

time: 84.6 us -> 86.4 us (1.021)
  waiting for transfers between devices: 1.17 us -> 2.59 us
    all_to_all x1, waiting for transfers between devices: 0.19 us -> 1.6 us  [local(): lax.all_to_all(spread, 'context', 0, 0, tiled=True).reshape(ROWS, LANES)]
where the time goes in v5:
time: 86.4 us; the launch traced here: 86.1 us
  blocking collectives  34.5 us (40%)
  starting transfers between devices  30.6 us (35%)
  Pallas kernels  16.6 us (19%)
  waiting for transfers between devices  2.59 us (3%)
    all_to_all x1, blocking collectives, local(): arrived = lax.all_to_all(terms, 'tensor', 0, 0, tiled=True)  34.5 us
    ppermute x9, starting transfers between devices, exchange(): return [lax.ppermute(x, 'tensor', pairs) for pairs in group]  24.1 us
    pallas_call x1, Pallas kernels, run_block(): pl.pallas_call(block_kernel, in_specs=[smem] + [vmem] * 10, out_specs=(vm...  7.8 us
    all_to_all x1, starting transfers between devices, local(): lax.all_to_all(spread, 'context', 0, 0, tiled=True).reshape(ROWS, LANES)  5.95 us
    pallas_call x1, Pallas kernels, build_tables(): pl.pallas_call(table_kernel, in_specs=[pl.BlockSpec(memory_space=pltpu.SM...  4.13 us
    pallas_call x1, Pallas kernels, run_first(): pl.pallas_call(first_kernel, in_specs=[smem] + [vmem] * 5, out_specs=(vme...  1.79 us
  transfers between devices with their start and end apart: 13, of which 3 were waited for; matrix products, arithmetic and copies ran while one was open for 0% of the time, Pallas kernels for 13%

profile of v5, /device:TPU:2, one launch (start us, length us, event | category | flops | bytes accessed | tf_op | source)
XLA Modules:
  0.0 86.1 jit_solution(13191556683343967598)
XLA Ops:
  0.0 4.1 %tables.1 = (f32[64,256]{1,0:T(8,128)}, bf16[128,2048]{1,0:T(8,128)(2,1)}, s32[16,8,128]{2,1,0:T(8,128)}) custom-call(s32[1]{0:T(128)} %bitcast.1.parity, s32[8,128]{1,0:T(8,128)} %bitcast.21, bf16[256,2048]{1,0:T(8,128)(2,1)} %w_own.1, bf16[5,2048]{1,0:T(8,128)(2,1)} %refs_0_.1, f32[1,2048]{1,0:T(1,128)} %bitcast.20, bf16[2048,256]{1,0:T(8,128)(2,1)} %refs_2_.1, ...), custom_call_target="tpu_custom_call" | custom-call | tf_op jit(solution)/shard_map/tables/pallas_call | solution.py:468
  4.1 2.0 %collective-permute-start = (f32[64,256]{1,0:T(8,128)}, f32[64,256]{1,0:T(8,128)S(1)}, u32[]{:S(2)}, u32[]{:S(2)}) collective-permute-start(f32[64,256]{1,0:T(8,128)} %get-tuple-element.30.t0), channel_id=1, source_target_pairs={{0,2},{1,3},{2,4},{3,5},{4,6},{5,7},{6,8},{7,9},{8,10},{9,11},{10,... | collective-permute-start | bytes 196616 | tf_op jit(solution)/shard_map/ppermute | solution.py:574
  6.1 4.0 %collective-permute-start.1 = (f32[64,256]{1,0:T(8,128)}, f32[64,256]{1,0:T(8,128)S(1)}, u32[]{:S(2)}, u32[]{:S(2)}) collective-permute-start(f32[64,256]{1,0:T(8,128)} %get-tuple-element.30.t0), channel_id=1, source_target_pairs={{0,14},{1,15},{2,0},{3,1},{4,2},{5,3},{6,4},{7,5},{8,6},{9,7},{10,... | collective-permute-start | bytes 196616 | tf_op jit(solution)/shard_map/ppermute | solution.py:574
  10.2 2.1 %collective-permute-start.2 = (f32[64,256]{1,0:T(8,128)}, f32[64,256]{1,0:T(8,128)S(1)}, u32[]{:S(2)}, u32[]{:S(2)}) collective-permute-start(f32[64,256]{1,0:T(8,128)} %get-tuple-element.30.t0), channel_id=1, source_target_pairs={{0,1},{1,0},{2,3},{3,2},{4,5},{5,4},{6,7},{7,6},{8,9},{9,8},{10,11... | collective-permute-start | bytes 196616 | tf_op jit(solution)/shard_map/ppermute | solution.py:574
  12.3 5.9 %all-to-all-start = ((s32[16,8,128]{2,1,0:T(8,128)}), s32[16,8,128]{2,1,0:T(8,128)S(1)}, u32[]{:S(2)}, u32[]{:S(2)}) async-start(s32[16,8,128]{2,1,0:T(8,128)} %get-tuple-element.23), calls=%async_computation | async-start | bytes 131072 | tf_op jit(solution)/shard_map/all_to_all | solution.py:608
  18.2 0.0 collective-permute-start.6
  18.2 3.2 %collective-permute-start.7 = (bf16[128,2048]{1,0:T(8,128)(2,1)}, bf16[128,2048]{1,0:T(8,128)(2,1)S(1)}, u32[]{:S(2)}, u32[]{:S(2)}) collective-permute-start(bf16[128,2048]{1,0:T(8,128)(2,1)} %get-tuple-element.33), channel_id=1, source_target_pairs={{0,14},{1,15},{2,0},{3,1},{4,2},{5,3},{6,4},{7,5},{8,6},{9,7},{10,... | collective-permute-start | bytes 1572872 | tf_op jit(solution)/shard_map/ppermute | solution.py:574
  21.5 1.6 %all-to-all-done = s32[16,8,128]{2,1,0:T(8,128)S(1)} async-done(((s32[16,8,128]{2,1,0:T(8,128)}), s32[16,8,128]{2,1,0:T(8,128)S(1)}, u32[]{:S(2)}, u32[]{:S(2)}) %all-to-all-start) | async-done | bytes 65568 | tf_op jit(solution)/shard_map/all_to_all | solution.py:608
  23.1 1.2 %prepare.1 = (f32[128,128]{1,0:T(8,128)S(1)}, f32[128,128]{1,0:T(8,128)S(1)}, f32[5,128,128]{2,1,0:T(8,128)S(1)}, bf16[512,128]{1,0:T(8,128)(2,1)S(1)}, f32[32,2...) custom-call(s32[1]{0:T(128)} %bitcast.place, s32[5]{0:T(128)S(1)} %copy-done.1, s32[128,128]{1,0:T(8,128)S(1)} %bitcast.18), custom_call_target="tpu_custom_call" | custom-call | tf_op jit(solution)/shard_map/prepare/pallas_call | solution.py:494
  24.3 0.0 collective-permute-done.t1
  24.3 1.7 %collective-permute-start.8 = (bf16[128,2048]{1,0:T(8,128)(2,1)}, bf16[128,2048]{1,0:T(8,128)(2,1)S(1)}, u32[]{:S(2)}, u32[]{:S(2)}) collective-permute-start(bf16[128,2048]{1,0:T(8,128)(2,1)} %get-tuple-element.33), channel_id=1, source_target_pairs={{0,1},{1,0},{2,3},{3,2},{4,5},{5,4},{6,7},{7,6},{8,9},{9,8},{10,11... | collective-permute-start | bytes 1572872 | tf_op jit(solution)/shard_map/ppermute | solution.py:574
  26.0 0.0 collective-permute-done.1.t2
  26.0 0.0 collective-permute-done.2.t3
  26.0 0.8 copy-done.2
  26.8 7.8 %block.1 = (bf16[512,1024]{1,0:T(8,128)(2,1)S(1)}, f32[1,512]{1,0:T(1,128)S(1)}) custom-call(s32[1]{0:T(128)} %bitcast.place, f32[128,128]{1,0:T(8,128)S(1)} %get-tuple-element.24.grams, f32[128,128]{1,0:T(8,128)S(1)} %get-tuple-element.25.side_tok, f32[5,128,128]{2,1,0:T(8,128)S(1)} %get-tuple-element.26.count, ...), custom_call_target="tpu_custom_call" | custom-call | flops 40000000000 | bytes 104857600 | tf_op jit(solution)/shard_map/block/pallas_call | solution.py:514
  34.6 4.5 %collective-permute-start.3 = (f32[1,512]{1,0:T(1,128)S(1)}, f32[1,512]{1,0:T(1,128)S(1)}, u32[]{:S(2)}, u32[]{:S(2)}) collective-permute-start(f32[1,512]{1,0:T(1,128)S(1)} %get-tuple-element.31.q0), channel_id=1, source_target_pairs={{0,8},{1,9},{2,10},{3,11},{4,12},{5,13},{6,14},{7,15},{8,0},{9,1},... | collective-permute-start | bytes 6152 | tf_op jit(solution)/shard_map/ppermute | solution.py:574
  39.1 1.8 %collective-permute-start.4 = (f32[1,512]{1,0:T(1,128)S(1)}, f32[1,512]{1,0:T(1,128)S(1)}, u32[]{:S(2)}, u32[]{:S(2)}) collective-permute-start(f32[1,512]{1,0:T(1,128)S(1)} %get-tuple-element.31.q0), channel_id=1, source_target_pairs={{0,5},{1,4},{2,7},{3,6},{4,9},{5,8},{6,11},{7,10},{8,13},{9,12},{1... | collective-permute-start | bytes 6152 | tf_op jit(solution)/shard_map/ppermute | solution.py:574
  41.0 0.0 collective-permute-done.6.a1
  41.0 4.7 %collective-permute-start.5 = (f32[1,512]{1,0:T(1,128)S(1)}, f32[1,512]{1,0:T(1,128)S(1)}, u32[]{:S(2)}, u32[]{:S(2)}) collective-permute-start(f32[1,512]{1,0:T(1,128)S(1)} %get-tuple-element.31.q0), channel_id=1, source_target_pairs={{0,13},{1,12},{2,15},{3,14},{4,1},{5,0},{6,3},{7,2},{8,5},{9,4},{1... | collective-permute-start | bytes 6152 | tf_op jit(solution)/shard_map/ppermute | solution.py:574
  45.7 0.0 collective-permute-done.7.a2
  45.7 0.5 collective-permute-start.11
  46.2 0.0 collective-permute-done.3.q1
  46.2 0.1 collective-permute-start.9
  46.3 1.8 %project_first.1 = (f32[256,2048]{1,0:T(8,128)S(1)}, f32[256,2048]{1,0:T(8,128)S(1)}, bf16[512,384]{1,0:T(8,128)(2,1)S(1)}) custom-call(s32[1]{0:T(128)} %bitcast.1.parity, bf16[512,1024]{1,0:T(8,128)(2,1)S(1)} %get-tuple-element.34.vg, bf16[256,2048]{1,0:T(8,128)(2,1)S(1)} %copy-done, bf16[128,2048]{1,0:T(8,128)(2,1)S(1)} %collective-permute-done.6.a1, ...), custom_call_target="tpu_custom_call" | custom-call | flops 60000002048 | bytes 104857600 | tf_op jit(solution)/shard_map/project_first/pallas_call | solution.py:535
  48.1 0.0 collective-permute-done.5.q3
  48.1 0.0 collective-permute-done.10.b2
  48.1 0.2 collective-permute-done.11.b3
  48.4 0.7 collective-permute-done.9.b1
  49.1 1.6 %project_second.1 = bf16[16,256,128]{2,1,0:T(8,128)(2,1)S(1)} custom-call(f32[1,512]{1,0:T(1,128)S(1)} %get-tuple-element.31.q0, f32[1,512]{1,0:T(1,128)S(1)} %collective-permute-done.3.q1, f32[1,512]{1,0:T(1,128)S(1)} %collective-permute-done.4.q2, f32[1,512]{1,0:T(1,128)S(1)} %collective-permute-done.5.q3, f32[256,2048]{1,0:T(8,128)S(1)} %get-tuple-element.38.forward, ...), custom_call_target="tpu_custom_call" | custom-call | tf_op jit(solution)/shard_map/project_second/pallas_call | solution.py:556
  50.7 34.5 %all_to_all.10 = bf16[16,256,128]{2,1,0:T(8,128)(2,1)S(1)} all-to-all(bf16[16,256,128]{2,1,0:T(8,128)(2,1)S(1)} %project_second.1), channel_id=1, replica_groups=mesh['context'=16,'tensor'=16] {'tensor'}, dimensions={0} | all-to-all | bytes 2097152 | tf_op jit(solution)/shard_map/all_to_all | solution.py:619
  85.2 0.1 fusion
  85.4 0.7 pad_maximum_fusion
  (8 shorter events, 0.0 us)
Async XLA Ops:
  0.0 23.1 %copy-start.1 = (s32[5]{0:T(128)S(1)}, s32[5]{0:T(128)}, u32[]{:S(2)}) copy-start(s32[5]{0:T(128)} %comp.1) | copy-start | bytes 64
  4.1 20.2 %collective-permute-start = (f32[64,256]{1,0:T(8,128)}, f32[64,256]{1,0:T(8,128)S(1)}, u32[]{:S(2)}, u32[]{:S(2)}) collective-permute-start(f32[64,256]{1,0:T(8,128)} %get-tuple-element.30.t0), channel_id=1, source_target_pairs={{0,2},{1,3},{2,4},{3,5},{4,6},{5,7},{6,8},{7,9},{8,10},{9,11},{10,... | collective-permute-start | bytes 196616 | tf_op jit(solution)/shard_map/ppermute | solution.py:574
  6.1 19.9 %collective-permute-start.1 = (f32[64,256]{1,0:T(8,128)}, f32[64,256]{1,0:T(8,128)S(1)}, u32[]{:S(2)}, u32[]{:S(2)}) collective-permute-start(f32[64,256]{1,0:T(8,128)} %get-tuple-element.30.t0), channel_id=1, source_target_pairs={{0,14},{1,15},{2,0},{3,1},{4,2},{5,3},{6,4},{7,5},{8,6},{9,7},{10,... | collective-permute-start | bytes 196616 | tf_op jit(solution)/shard_map/ppermute | solution.py:574
  10.2 15.8 %collective-permute-start.2 = (f32[64,256]{1,0:T(8,128)}, f32[64,256]{1,0:T(8,128)S(1)}, u32[]{:S(2)}, u32[]{:S(2)}) collective-permute-start(f32[64,256]{1,0:T(8,128)} %get-tuple-element.30.t0), channel_id=1, source_target_pairs={{0,1},{1,0},{2,3},{3,2},{4,5},{5,4},{6,7},{7,6},{8,9},{9,8},{10,11... | collective-permute-start | bytes 196616 | tf_op jit(solution)/shard_map/ppermute | solution.py:574
  12.3 10.8 %all-to-all-start = ((s32[16,8,128]{2,1,0:T(8,128)}), s32[16,8,128]{2,1,0:T(8,128)S(1)}, u32[]{:S(2)}, u32[]{:S(2)}) async-start(s32[16,8,128]{2,1,0:T(8,128)} %get-tuple-element.23), calls=%async_computation | async-start | bytes 131072 | tf_op jit(solution)/shard_map/all_to_all | solution.py:608
  18.2 22.8 %collective-permute-start.6 = (bf16[128,2048]{1,0:T(8,128)(2,1)}, bf16[128,2048]{1,0:T(8,128)(2,1)S(1)}, u32[]{:S(2)}, u32[]{:S(2)}) collective-permute-start(bf16[128,2048]{1,0:T(8,128)(2,1)} %get-tuple-element.33), channel_id=1, source_target_pairs={{0,2},{1,3},{2,4},{3,5},{4,6},{5,7},{6,8},{7,9},{8,10},{9,11},{10,... | collective-permute-start | bytes 1572872 | tf_op jit(solution)/shard_map/ppermute | solution.py:574
  18.2 27.5 %collective-permute-start.7 = (bf16[128,2048]{1,0:T(8,128)(2,1)}, bf16[128,2048]{1,0:T(8,128)(2,1)S(1)}, u32[]{:S(2)}, u32[]{:S(2)}) collective-permute-start(bf16[128,2048]{1,0:T(8,128)(2,1)} %get-tuple-element.33), channel_id=1, source_target_pairs={{0,14},{1,15},{2,0},{3,1},{4,2},{5,3},{6,4},{7,5},{8,6},{9,7},{10,... | collective-permute-start | bytes 1572872 | tf_op jit(solution)/shard_map/ppermute | solution.py:574
  24.3 21.4 %collective-permute-start.8 = (bf16[128,2048]{1,0:T(8,128)(2,1)}, bf16[128,2048]{1,0:T(8,128)(2,1)S(1)}, u32[]{:S(2)}, u32[]{:S(2)}) collective-permute-start(bf16[128,2048]{1,0:T(8,128)(2,1)} %get-tuple-element.33), channel_id=1, source_target_pairs={{0,1},{1,0},{2,3},{3,2},{4,5},{5,4},{6,7},{7,6},{8,9},{9,8},{10,11... | collective-permute-start | bytes 1572872 | tf_op jit(solution)/shard_map/ppermute | solution.py:574
  26.0 0.8 copy-start.2
  26.8 19.5 %copy-start = (bf16[256,2048]{1,0:T(8,128)(2,1)S(1)}, bf16[256,2048]{1,0:T(8,128)(2,1)}, u32[]{:S(2)}) copy-start(bf16[256,2048]{1,0:T(8,128)(2,1)} %w_own.1) | copy-start | bytes 3145732
  34.6 11.6 %collective-permute-start.3 = (f32[1,512]{1,0:T(1,128)S(1)}, f32[1,512]{1,0:T(1,128)S(1)}, u32[]{:S(2)}, u32[]{:S(2)}) collective-permute-start(f32[1,512]{1,0:T(1,128)S(1)} %get-tuple-element.31.q0), channel_id=1, source_target_pairs={{0,8},{1,9},{2,10},{3,11},{4,12},{5,13},{6,14},{7,15},{8,0},{9,1},... | collective-permute-start | bytes 6152 | tf_op jit(solution)/shard_map/ppermute | solution.py:574
  39.1 9.0 %collective-permute-start.4 = (f32[1,512]{1,0:T(1,128)S(1)}, f32[1,512]{1,0:T(1,128)S(1)}, u32[]{:S(2)}, u32[]{:S(2)}) collective-permute-start(f32[1,512]{1,0:T(1,128)S(1)} %get-tuple-element.31.q0), channel_id=1, source_target_pairs={{0,5},{1,4},{2,7},{3,6},{4,9},{5,8},{6,11},{7,10},{8,13},{9,12},{1... | collective-permute-start | bytes 6152 | tf_op jit(solution)/shard_map/ppermute | solution.py:574
  41.0 7.1 %collective-permute-start.5 = (f32[1,512]{1,0:T(1,128)S(1)}, f32[1,512]{1,0:T(1,128)S(1)}, u32[]{:S(2)}, u32[]{:S(2)}) collective-permute-start(f32[1,512]{1,0:T(1,128)S(1)} %get-tuple-element.31.q0), channel_id=1, source_target_pairs={{0,13},{1,12},{2,15},{3,14},{4,1},{5,0},{6,3},{7,2},{8,5},{9,4},{1... | collective-permute-start | bytes 6152 | tf_op jit(solution)/shard_map/ppermute | solution.py:574
  45.7 2.4 %collective-permute-start.10 = (bf16[128,2048]{1,0:T(8,128)(2,1)S(1)}, bf16[128,2048]{1,0:T(8,128)(2,1)S(1)}, u32[]{:S(2)}, u32[]{:S(2)}) collective-permute-start(bf16[128,2048]{1,0:T(8,128)(2,1)S(1)} %collective-permute-done.7.a2), channel_id=1, source_target_pairs={{0,16},{16,0},{32,48},{48,32},{64,80},{80,64},{96,112},{112,96},{1... | collective-permute-start | bytes 1572872 | tf_op jit(solution)/shard_map/ppermute | solution.py:579
  45.7 2.7 %collective-permute-start.11 = (bf16[128,2048]{1,0:T(8,128)(2,1)S(1)}, bf16[128,2048]{1,0:T(8,128)(2,1)S(1)}, u32[]{:S(2)}, u32[]{:S(2)}) collective-permute-start(bf16[128,2048]{1,0:T(8,128)(2,1)S(1)} %collective-permute-done.8.a3), channel_id=1, source_target_pairs={{0,16},{16,0},{32,48},{48,32},{64,80},{80,64},{96,112},{112,96},{1... | collective-permute-start | bytes 1572872 | tf_op jit(solution)/shard_map/ppermute | solution.py:579
  46.2 2.9 %collective-permute-start.9 = (bf16[128,2048]{1,0:T(8,128)(2,1)S(1)}, bf16[128,2048]{1,0:T(8,128)(2,1)S(1)}, u32[]{:S(2)}, u32[]{:S(2)}) collective-permute-start(bf16[128,2048]{1,0:T(8,128)(2,1)S(1)} %collective-permute-done.6.a1), channel_id=1, source_target_pairs={{0,16},{16,0},{32,48},{48,32},{64,80},{80,64},{96,112},{112,96},{1... | collective-permute-start | bytes 1572872 | tf_op jit(solution)/shard_map/ppermute | solution.py:579
